TPU v7x, 32 devices: a whole 2x2x4 slice. The times are simulated.
32 devices in a mesh: parts: 2 (over x), row: 16 (over z, y, core).
Axes of the slice: x: 2, y: 2, z: 4, core: 2. Of those that a mesh axis runs over, the one named last changes fastest.
Arguments:
- pair: bfloat16 [512, 256, 128], P(('parts', 'row')), parts along dimension 0, may hold values from -6 to 6
- pair_mask: int32 [512, 256], P(('parts', 'row')), parts along dimension 0, may hold values 0 or 1
- in_gain: float32 [128], replicated, may hold values from 0.1 to 1.9
- in_proj: bfloat16 [128, 512], replicated, may hold values from -0.5 to 0.5
- gate_proj: bfloat16 [128, 128], replicated, may hold values from -0.5 to 0.5
- out_proj: bfloat16 [128, 128], replicated, may hold values from -0.5 to 0.5
Outputs:
- update: bfloat16 [512, 256, 128], P(('parts', 'row')), parts along dimension 0
There are 2 independent parts, one for each index of `parts`. A program takes and returns all parts, laid end to end along the dimension named above; an argument that names none is the same for every part. Nothing has to cross between parts.
All inputs are finite; a program needn't handle non-finite values. No bound on the sum of `pair_mask` on one device may be relied on, other than what follows from the above.
Results may differ from a plain program's by a relative error of at most 0.0085.
Values may be sent and summed in bfloat16 or wider, within the bound.
No kernel may reach another device: no remote copies, remote signals or barrier semaphores. Data moves between devices by JAX's collectives and lax.ppermute only.
A program may use at most 128 MiB of HBM per device.

v0:
```python
import jax
import jax.numpy as jnp
from jax import lax
from jax.sharding import PartitionSpec as P


def norm_axis(values, axis, eps):
    mean = jnp.mean(values, axis=axis, keepdims=True)
    centered = values - mean
    variance = jnp.mean(centered * centered, axis=axis, keepdims=True)
    return centered * jax.lax.rsqrt(variance + eps)


def on_device(pair, pair_mask, in_gain, in_proj, gate_proj, out_proj):
    hidden = out_proj.shape[0]
    normed = (norm_axis(pair.astype(jnp.float32), -1, 1e-05) * in_gain).astype(jnp.bfloat16)
    gate = jax.nn.sigmoid(
        jnp.einsum("rkd,de->rke", normed, gate_proj, preferred_element_type=jnp.float32)
    )
    proj = jnp.einsum("rkd,dc->crk", normed, in_proj, preferred_element_type=jnp.float32)
    keep = pair_mask.astype(jnp.float32)[None, :, :]
    left = (keep * jax.nn.sigmoid(proj[hidden : 2 * hidden]) * proj[:hidden]).astype(jnp.bfloat16)
    right = (keep * jax.nn.sigmoid(proj[3 * hidden :]) * proj[2 * hidden : 3 * hidden]).astype(
        jnp.bfloat16
    )
    left_group, right_group = (
        lax.all_to_all(left, "row", split_axis=0, concat_axis=1, tiled=True),
        lax.all_to_all(right, "row", split_axis=0, concat_axis=1, tiled=True),
    )
    crossed_group = jnp.einsum(
        "cik,cjk->cij", left_group, right_group, preferred_element_type=jnp.float32
    ).astype(jnp.bfloat16)
    crossed = lax.all_to_all(crossed_group, "row", split_axis=1, concat_axis=0, tiled=True)
    crossed_norm = norm_axis(crossed.astype(jnp.float32), 0, 1e-05).astype(jnp.bfloat16)
    mixed = jnp.einsum("crj,ce->rje", crossed_norm, out_proj, preferred_element_type=jnp.float32)
    return (gate * mixed).astype(jnp.bfloat16)


def solution(mesh):
    in_specs = (P(("parts", "row"), None, None), P(("parts", "row"), None), P(), P(), P(), P())
    out_specs = P(("parts", "row"), None, None)
    return jax.shard_map(
        on_device, mesh=mesh, in_specs=in_specs, out_specs=out_specs, check_vma=False
    )
```

profile of v0, /device:TPU:0, one launch (start us, length us, event | category | flops | bytes accessed | tf_op | source)
XLA Modules:
  0.0 106.3 jit_solution(13282336574966164291)
XLA Ops:
  0.0 0.0 copy-start
  0.0 0.0 copy-start.1
  0.0 0.0 copy-start.4
  0.0 0.0 copy-start.5
  0.0 1.7 %convert_reduce_fusion = f32[16,256]{1,0:T(8,128)S(1)} fusion(bf16[16,256,128]{2,1,0:T(8,128)(2,1)} %param.6), kind=kLoop, calls=%fused_computation.2 | loop fusion | flops 1044480 | bytes 1064960 | tf_op jit(solution)/shard_map/reduce_sum | solution.py:8
  1.7 2.3 %fusion.2 = f32[16,256]{1,0:T(8,128)S(1)} fusion(bf16[16,256,128]{2,1,0:T(8,128)(2,1)} %param.6, f32[16,256]{1,0:T(8,128)S(1)} %broadcast_multiply_fusion.1), kind=kLoop, calls=%fused_computation.5 | loop fusion | flops 2093056 | bytes 1081344 | tf_op jit(solution)/shard_map/reduce_sum | solution.py:10
  4.1 0.0 copy-done.4
  4.1 0.0 copy-done
  4.1 0.0 copy-done.1
  4.1 0.0 copy-done.5
  4.1 1.3 %convolution_bitcast_fusion = f32[512,16,256]{0,2,1:T(8,128)S(1)} fusion(bf16[16,256,128]{2,1,0:T(8,128)(2,1)S(1)} %copy-done.1, f32[128]{0:T(128)S(1)} %copy-done.5, f32[16,256]{1,0:T(8,128)S(1)} %add_rsqrt_fusion.1, f32[16,256]{1,0:T(8,128)S(1)} %broadcast_multiply_fusion.1, bf16[128,512]{1,0:T(8,128)(2,1)S(1)} %copy-done), kind=kOutput, calls=%fused_computation | convolution fusion | flops 539492352 | bytes 9601536 | tf_op jit(solution)/shard_map/rkd,dc->crk/dot_general | solution.py:20
  5.4 1.2 %fusion.5 = (bf16[128,16,256]{0,2,1:T(8,128)(2,1)S(1)}, bf16[128,16,256]{0,2,1:T(8,128)(2,1)S(1)}) fusion(f32[512,16,256]{0,2,1:T(8,128)S(1)} %convolution_bitcast_fusion, f32[16,256]{1,0:T(8,128)S(1)} %convert_element_type.44), kind=kLoop, calls=%fused_computation.9 | loop fusion | flops 6291456 | bytes 10502144 | tf_op jit(solution)/shard_map/convert_element_type | solution.py:23
  6.7 1.7 %copy.22 = bf16[128,16,256]{2,1,0:T(8,128)(2,1)} copy(bf16[128,16,256]{0,2,1:T(8,128)(2,1)S(1)} %get-tuple-element.6) | data formatting | bytes 2097152 | tf_op jit(solution)/shard_map/convert_element_type | solution.py:22
  8.3 7.4 %all-to-all-start = ((bf16[128,16,256]{2,1,0:T(8,128)(2,1)}), bf16[128,16,256]{2,1,0:T(8,128)(2,1)S(1)}, u32[]{:S(2)}, u32[]{:S(2)}) async-start(bf16[128,16,256]{2,1,0:T(8,128)(2,1)} %copy.22), calls=%async_computation | async-start | bytes 2097152 | tf_op jit(solution)/shard_map/all_to_all | solution.py:27
  15.7 1.7 %copy.24 = bf16[128,16,256]{2,1,0:T(8,128)(2,1)} copy(bf16[128,16,256]{0,2,1:T(8,128)(2,1)S(1)} %get-tuple-element.5) | data formatting | bytes 2097152 | tf_op jit(solution)/shard_map/convert_element_type | solution.py:23
  17.4 21.2 %all-to-all-done = bf16[128,16,256]{2,1,0:T(8,128)(2,1)S(1)} async-done(((bf16[128,16,256]{2,1,0:T(8,128)(2,1)}), bf16[128,16,256]{2,1,0:T(8,128)(2,1)S(1)}, u32[]{:S(2)}, u32[]{:S(2)}) %all-to-all-start) | async-done | bytes 1048608 | tf_op jit(solution)/shard_map/all_to_all | solution.py:27
  38.7 6.9 %all-to-all-start.1 = ((bf16[128,16,256]{2,1,0:T(8,128)(2,1)}), bf16[128,16,256]{2,1,0:T(8,128)(2,1)}, u32[]{:S(2)}, u32[]{:S(2)}) async-start(bf16[128,16,256]{2,1,0:T(8,128)(2,1)} %copy.24), calls=%async_computation.1 | async-start | bytes 2097152 | tf_op jit(solution)/shard_map/all_to_all | solution.py:28
  45.6 0.1 copy.23
  45.7 22.9 %all-to-all-done.1 = bf16[128,16,256]{2,1,0:T(8,128)(2,1)} async-done(((bf16[128,16,256]{2,1,0:T(8,128)(2,1)}), bf16[128,16,256]{2,1,0:T(8,128)(2,1)}, u32[]{:S(2)}, u32[]{:S(2)}) %all-to-all-start.1) | async-done | bytes 1048608 | tf_op jit(solution)/shard_map/all_to_all | solution.py:28
  68.6 1.3 %copy.25 = bf16[8,16,16,256]{3,2,1,0:T(8,128)(2,1)S(1)} copy(bf16[8,16,16,256]{3,2,0,1:T(8,128)(2,1)} %bitcast.7) | data formatting | bytes 2097152 | tf_op jit(solution)/shard_map/all_to_all | solution.py:28
  69.9 0.5 convolution_convert_fusion
  70.4 0.0 copy-start.3
  70.4 1.6 %copy.26 = bf16[8,256,256]{2,0,1:T(8,128)(2,1)} copy(bf16[8,256,256]{2,1,0:T(8,128)(2,1)S(1)} %convolution_convert_fusion) | data formatting | bytes 2097152 | tf_op jit(solution)/shard_map/convert_element_type | solution.py:32
  72.0 6.9 %all-to-all-start.2 = ((bf16[8,256,256]{2,0,1:T(8,128)(2,1)}), bf16[8,256,256]{2,0,1:T(8,128)(2,1)S(1)}, u32[]{:S(2)}, u32[]{:S(2)}) async-start(bf16[8,256,256]{2,0,1:T(8,128)(2,1)} %copy.26), calls=%async_computation.2 | async-start | bytes 2097152 | tf_op jit(solution)/shard_map/all_to_all | solution.py:33
  78.8 0.0 copy-done.3
  78.8 2.5 %fusion.20 = f32[16,256,128]{2,1,0:T(8,128)} fusion(bf16[16,256,128]{2,1,0:T(8,128)(2,1)S(1)} %copy-done.1, f32[128]{0:T(128)S(1)} %copy-done.5, f32[16,256]{1,0:T(8,128)S(1)} %add_rsqrt_fusion.1, f32[16,256]{1,0:T(8,128)S(1)} %broadcast_multiply_fusion.1, bf16[128,128]{1,0:T(8,128)(2,1)S(1)} %copy-done.3), kind=kOutput, calls=%fused_computation.31 | convolution fusion | flops 136839168 | bytes 3211776 | tf_op jit(solution)/shard_map/rkd,de->rke/dot_general | solution.py:18
  81.3 20.5 %all-to-all-done.2 = bf16[8,256,256]{2,0,1:T(8,128)(2,1)S(1)} async-done(((bf16[8,256,256]{2,0,1:T(8,128)(2,1)}), bf16[8,256,256]{2,0,1:T(8,128)(2,1)S(1)}, u32[]{:S(2)}, u32[]{:S(2)}) %all-to-all-start.2) | async-done | bytes 1048608 | tf_op jit(solution)/shard_map/all_to_all | solution.py:33
  101.8 0.3 fusion.25
  102.1 0.2 fusion.17
  102.3 0.3 multiply_reduce_fusion
  102.6 0.2 copy.28
  102.9 0.0 copy-start.2
  102.9 0.0 copy-start.6
  102.9 0.3 fusion.16
  103.2 1.3 %copy-done.2 = f32[16,256,128]{2,1,0:T(8,128)S(1)} copy-done((f32[16,256,128]{2,1,0:T(8,128)S(1)}, f32[16,256,128]{2,1,0:T(8,128)}, u32[]{:S(2)}) %copy-start.2) | copy-done | bytes 2097176
  104.5 0.0 copy-done.6
  104.5 1.9 %multiply_convert_fusion = bf16[16,256,128]{2,1,0:T(8,128)(2,1)} fusion(f32[16,256,128]{2,1,0:T(8,128)S(1)} %copy-done.2, bf16[128,16,256]{2,1,0:T(8,128)(2,1)S(1)} %fusion.16, bf16[128,128]{1,0:T(8,128)(2,1)S(1)} %copy-done.6), kind=kOutput, calls=%fused_computation.26 | convolution fusion | flops 136839168 | bytes 4227072 | tf_op jit(solution)/shard_map/crj,ce->rje/dot_general | solution.py:35
  (5 shorter events, 0.0 us)
Async XLA Ops:
  0.0 4.1 %copy-start = (bf16[128,512]{1,0:T(8,128)(2,1)S(1)}, bf16[128,512]{1,0:T(8,128)(2,1)}, u32[]{:S(2)}) copy-start(bf16[128,512]{1,0:T(8,128)(2,1)} %param.9) | copy-start | bytes 393220
  0.0 4.1 %copy-start.1 = (bf16[16,256,128]{2,1,0:T(8,128)(2,1)S(1)}, bf16[16,256,128]{2,1,0:T(8,128)(2,1)}, u32[]{:S(2)}) copy-start(bf16[16,256,128]{2,1,0:T(8,128)(2,1)} %param.6) | copy-start | bytes 3145732
  0.0 4.1 %copy-start.4 = (s32[16,256]{1,0:T(8,128)S(1)}, s32[16,256]{1,0:T(8,128)}, u32[]{:S(2)}) copy-start(s32[16,256]{1,0:T(8,128)} %param.7) | copy-start | bytes 49156
  0.0 4.1 %copy-start.5 = (f32[128]{0:T(128)S(1)}, f32[128]{0:T(128)}, u32[]{:S(2)}) copy-start(f32[128]{0:T(128)} %param.8) | copy-start | bytes 1540
  8.3 30.3 %all-to-all-start = ((bf16[128,16,256]{2,1,0:T(8,128)(2,1)}), bf16[128,16,256]{2,1,0:T(8,128)(2,1)S(1)}, u32[]{:S(2)}, u32[]{:S(2)}) async-start(bf16[128,16,256]{2,1,0:T(8,128)(2,1)} %copy.22), calls=%async_computation | async-start | bytes 2097152 | tf_op jit(solution)/shard_map/all_to_all | solution.py:27
  38.7 29.9 %all-to-all-start.1 = ((bf16[128,16,256]{2,1,0:T(8,128)(2,1)}), bf16[128,16,256]{2,1,0:T(8,128)(2,1)}, u32[]{:S(2)}, u32[]{:S(2)}) async-start(bf16[128,16,256]{2,1,0:T(8,128)(2,1)} %copy.24), calls=%async_computation.1 | async-start | bytes 2097152 | tf_op jit(solution)/shard_map/all_to_all | solution.py:28
  70.4 8.4 %copy-start.3 = (bf16[128,128]{1,0:T(8,128)(2,1)S(1)}, bf16[128,128]{1,0:T(8,128)(2,1)}, u32[]{:S(2)}) copy-start(bf16[128,128]{1,0:T(8,128)(2,1)} %param.10) | copy-start | bytes 98308
  72.0 29.8 %all-to-all-start.2 = ((bf16[8,256,256]{2,0,1:T(8,128)(2,1)}), bf16[8,256,256]{2,0,1:T(8,128)(2,1)S(1)}, u32[]{:S(2)}, u32[]{:S(2)}) async-start(bf16[8,256,256]{2,0,1:T(8,128)(2,1)} %copy.26), calls=%async_computation.2 | async-start | bytes 2097152 | tf_op jit(solution)/shard_map/all_to_all | solution.py:33
  102.9 1.6 %copy-start.2 = (f32[16,256,128]{2,1,0:T(8,128)S(1)}, f32[16,256,128]{2,1,0:T(8,128)}, u32[]{:S(2)}) copy-start(f32[16,256,128]{2,1,0:T(8,128)} %fusion.20) | copy-start | bytes 6291460
  102.9 1.6 %copy-start.6 = (bf16[128,128]{1,0:T(8,128)(2,1)S(1)}, bf16[128,128]{1,0:T(8,128)(2,1)}, u32[]{:S(2)}) copy-start(bf16[128,128]{1,0:T(8,128)(2,1)} %param.11) | copy-start | bytes 98308
where the time goes:
time: 108 us; the launch traced here: 106 us
  waiting for transfers between devices  64.6 us (60%)
  starting transfers between devices  21.2 us (20%)
  local copies, waits for them, and re-layouts  7.87 us (7%)
  other arithmetic  6.41 us (6%)
  matrix products  6.13 us (6%)
    all_to_all x1, waiting for transfers between devices, on_device(): lax.all_to_all(right, 'row', split_axis=0, concat_axis=1, tiled=True)  22.9 us
    all_to_all x1, waiting for transfers between devices, on_device(): lax.all_to_all(left, 'row', split_axis=0, concat_axis=1, tiled=True)  21.2 us
    all_to_all x1, waiting for transfers between devices, on_device(): lax.all_to_all(crossed_group, 'row', split_axis=1, concat_axis=0, tiled=T...  20.5 us
    all_to_all x1, starting transfers between devices, on_device(): lax.all_to_all(left, 'row', split_axis=0, concat_axis=1, tiled=True)  7.39 us
    all_to_all x1, starting transfers between devices, on_device(): lax.all_to_all(right, 'row', split_axis=0, concat_axis=1, tiled=True)  6.92 us
    all_to_all x1, starting transfers between devices, on_device(): lax.all_to_all(crossed_group, 'row', split_axis=1, concat_axis=0, tiled=T...  6.86 us
    reduce_sum x2, other arithmetic, norm_axis(): variance = jnp.mean(centered * centered, axis=axis, keepdims=True)  2.66 us
    dot_general x1, matrix products, on_device(): jnp.einsum('rkd,de->rke', normed, gate_proj, preferred_element_type=jnp.f...  2.47 us
  transfers between devices with their start and end apart: 3, of which 3 were waited for; matrix products, arithmetic and copies ran while one was open for 4% of the time, Pallas kernels for 0%

commit v1 on v0

v1 whole, which is shorter than its diff:
```python
import functools

import jax
import jax.numpy as jnp
from jax import lax
from jax.experimental import pallas as pl
from jax.experimental.pallas import tpu as pltpu
from jax.sharding import PartitionSpec as P

EPS = 1e-05
VMEM = pl.BlockSpec(memory_space=pltpu.VMEM)
SMEM = pl.BlockSpec(memory_space=pltpu.SMEM)
PARAMS = pltpu.CompilerParams(vmem_limit_bytes=48 * 2**20)
OVER_LAST = (((1,), (1,)), ((), ()))


def sigmoid(x):
    return 0.5 * jnp.tanh(0.5 * x) + 0.5


def normed_row(pair_ref, gain, r):
    x = pair_ref[r].astype(jnp.float32)
    centered = x - jnp.mean(x, axis=-1, keepdims=True)
    variance = jnp.mean(centered * centered, axis=-1, keepdims=True)
    return (centered * lax.rsqrt(variance + EPS) * gain).astype(jnp.bfloat16)


def operand(pair_ref, mask_ref, gain_ref, proj_ref, total, first):
    rows, tokens, _ = pair_ref.shape
    hidden = proj_ref.shape[1] // 4
    weights = proj_ref[:, first * hidden : (first + 2) * hidden].T
    gain = gain_ref[...]

    def step(r, carry):
        normed = normed_row(pair_ref, gain, r)
        proj = lax.dot_general(weights, normed, OVER_LAST, preferred_element_type=jnp.float32)
        keep = mask_ref[pl.ds(r, 1), :].astype(jnp.float32)
        value = keep * sigmoid(proj[hidden:]) * proj[:hidden]
        for t in range(tokens // 128):
            total[t, pl.ds(r, hidden, stride=rows), :] = value[:, t * 128 : (t + 1) * 128]
        return carry

    lax.fori_loop(0, rows, step, 0, unroll=4)


def right_kernel(pair_ref, mask_ref, gain_ref, proj_ref, out_ref, total):
    copies, blocks, group, rows, tokens = out_ref.shape
    operand(pair_ref, mask_ref, gain_ref, proj_ref, total, 2)
    for b in range(blocks):
        for t in range(tokens // 128):
            block = total[t, b * group * rows : (b + 1) * group * rows, :].astype(jnp.bfloat16)
            for c in range(copies):
                out_ref[c, b, :, :, t * 128 : (t + 1) * 128] = block.reshape(group, rows, 128)


def left_kernel(me_ref, pair_ref, mask_ref, gain_ref, proj_ref, *rest):
    *out_refs, total = rest
    blocks = len(out_refs)
    group, rows, tokens = out_refs[0].shape
    operand(pair_ref, mask_ref, gain_ref, proj_ref, total, 0)
    for s, out_ref in enumerate(out_refs):
        b = lax.rem(me_ref[0] + s, blocks)
        for t in range(tokens // 128):
            block = total[t, pl.ds(pl.multiple_of(b * group * rows, group * rows), group * rows), :]
            out_ref[:, :, t * 128 : (t + 1) * 128] = block.astype(jnp.bfloat16).reshape(group, rows, 128)


def cross_kernel(me_ref, right_ref, *rest):
    *left_refs, out_ref = rest
    blocks = len(left_refs)
    sources, group, rows, tokens = right_ref.shape
    for c in range(group):
        right = right_ref[:, c].reshape(sources * rows, tokens)
        left = jnp.concatenate([ref[c] for ref in left_refs], axis=0)
        crossed = lax.dot_general(left, right, OVER_LAST, preferred_element_type=jnp.float32)
        crossed = crossed.astype(jnp.bfloat16).reshape(blocks, rows, sources * rows)
        for s in range(blocks):
            owner = lax.rem(me_ref[0] + blocks - s, blocks)
            out_ref[owner, c] = crossed[s]


def gate_kernel(pair_ref, gain_ref, proj_ref, out_ref):
    rows = pair_ref.shape[0]
    gain = gain_ref[...]
    weights = proj_ref[...]

    def step(r, carry):
        normed = normed_row(pair_ref, gain, r)
        out_ref[r] = sigmoid(jnp.dot(normed, weights, preferred_element_type=jnp.float32))
        return carry

    lax.fori_loop(0, rows, step, 0, unroll=4)


def final_kernel(crossed_ref, gate_ref, proj_ref, out_ref, total):
    hidden, rows, tokens = crossed_ref.shape
    for t in range(tokens // 128):
        lanes = slice(t * 128, (t + 1) * 128)
        x = crossed_ref[:, :, lanes].astype(jnp.float32)
        centered = x - jnp.mean(x, axis=0, keepdims=True)
        variance = jnp.mean(centered * centered, axis=0, keepdims=True)
        total[t] = (centered * lax.rsqrt(variance + EPS)).reshape(hidden * rows, 128)
    weights = proj_ref[...]

    def step(r, carry):
        for t in range(tokens // 128):
            lanes = slice(t * 128, (t + 1) * 128)
            x = total[t, pl.ds(r, hidden, stride=rows), :].T.astype(jnp.bfloat16)
            mixed = jnp.dot(x, weights, preferred_element_type=jnp.float32)
            out_ref[r, lanes, :] = (gate_ref[r, lanes, :] * mixed).astype(jnp.bfloat16)
        return carry

    lax.fori_loop(0, rows, step, 0, unroll=4)


def call(kernel, out_shape, operands, scratch=(), cost=1.0):
    specs = [SMEM if x.dtype == jnp.int32 and x.ndim == 1 else VMEM for x in operands]
    return pl.pallas_call(
        kernel,
        out_shape=out_shape,
        in_specs=specs,
        out_specs=jax.tree.map(lambda _: VMEM, out_shape),
        scratch_shapes=list(scratch),
        compiler_params=PARAMS,
        cost_estimate=pl.CostEstimate(
            flops=int(cost * 1e9), bytes_accessed=int(cost * 4e6), transcendentals=0
        ),
    )(*operands)


def on_device(devices, pair, pair_mask, in_gain, in_proj, gate_proj, out_proj):
    rows, tokens, width = pair.shape
    hidden = out_proj.shape[0]
    blocks = devices // 2
    group = hidden // blocks
    sds = jax.ShapeDtypeStruct
    bf16 = jnp.bfloat16
    me = lax.rem(lax.axis_index("row"), blocks).astype(jnp.int32).reshape(1)
    gain = in_gain.reshape(1, width)
    total = pltpu.VMEM((tokens // 128, hidden * rows, 128), jnp.float32)

    right = call(
        right_kernel,
        sds((2, blocks, group, rows, tokens), bf16),
        (pair, pair_mask, gain, in_proj),
        (total,),
    ).reshape(devices, group, rows, tokens)
    right = lax.all_to_all(right, "row", split_axis=0, concat_axis=0, tiled=True)
    lefts = call(
        left_kernel,
        tuple(sds((group, rows, tokens), bf16) for _ in range(blocks)),
        (me, pair, pair_mask, gain, in_proj),
        (total,),
    )
    halves = (range(blocks), range(blocks, devices))
    lefts = [lefts[0]] + [
        lax.ppermute(
            lefts[s],
            "row",
            [(h[i], h[(i + s) % blocks]) for h in halves for i in range(blocks)],
        )
        for s in range(1, blocks)
    ]
    gate = call(gate_kernel, sds((rows, tokens, width), jnp.float32), (pair, gain, gate_proj))
    crossed = call(
        cross_kernel, sds((blocks, group, rows, devices * rows), bf16), (me, right, *lefts)
    )
    crossed = lax.all_to_all(
        crossed, "row", split_axis=0, concat_axis=0, tiled=True,
        axis_index_groups=[list(h) for h in halves],
    ).reshape(hidden, rows, tokens)
    return call(final_kernel, sds((rows, tokens, width), bf16), (crossed, gate, out_proj), (total,))


def solution(mesh):
    in_specs = (P(("parts", "row"), None, None), P(("parts", "row"), None), P(), P(), P(), P())
    out_specs = P(("parts", "row"), None, None)
    return jax.shard_map(
        functools.partial(on_device, mesh.shape["row"]),
        mesh=mesh, in_specs=in_specs, out_specs=out_specs, check_vma=False,
    )
```

time: 108 us -> 88.9 us (0.82); the launches traced: 106 us -> 88.4 us
  waiting for transfers between devices: 64.6 us -> 49.1 us
  Pallas kernels: 0 us -> 13.3 us
  other arithmetic: 6.41 us -> 0 us
  matrix products: 6.13 us -> 0 us
  local copies, waits for them, and re-layouts: 7.87 us -> 6.06 us
  starting transfers between devices: 21.2 us -> 19.9 us
    all_to_all x3 -> x2, waiting for transfers between devices: 64.6 us -> 11.3 us  [the longest x1 11.3 us: on_device(): lax.all_to_all(crossed, 'row', split_axis=0, concat_axis=0, tiled=True, a...]
    ppermute x0 -> x7, waiting for transfers between devices: none -> 37.8 us  [on_device(): lax.ppermute(lefts[s], 'row', [(h[i], h[(i + s) % blocks]) for h in halve...]
    pallas_call x0 -> x5, Pallas kernels: none -> 13.3 us  [call(): pl.pallas_call(kernel, out_shape=out_shape, in_specs=specs, out_specs=jax...]
    all_to_all x3 -> x2, starting transfers between devices: 21.2 us -> 13.7 us  [the longest x1 7.53 us: on_device(): lax.all_to_all(right, 'row', split_axis=0, concat_axis=0, tiled=True)]
    ppermute x0 -> x7, starting transfers between devices: none -> 6.18 us  [on_device(): lax.ppermute(lefts[s], 'row', [(h[i], h[(i + s) % blocks]) for h in halve...]
    dot_general x4 -> x0, matrix products: 6.13 us -> none  [the longest x1 2.47 us: on_device(): jnp.einsum('rkd,de->rke', normed, gate_proj, preferred_element_type=jnp.f...]
    convert_element_type x4 -> x0, local copies, waits for them, and re-layouts: 5.17 us -> none  [the longest x1 1.7 us: on_device(): (keep * jax.nn.sigmoid(proj[3 * hidden:]) * proj[2 * hidden:3 * hidden])....]
    unnamed x14 -> x24, local copies, waits for them, and re-layouts: 1.29 us -> 6.06 us
  transfers between devices with their start and end apart: 3 -> 9, of which waited for: 3 -> 7; matrix products, arithmetic and copies ran while one was open for 4% -> 0% of each run, Pallas kernels for 0% -> 6%
where the time goes in v1:
time: 88.9 us; the launch traced here: 88.4 us
  waiting for transfers between devices  49.1 us (55%)
  starting transfers between devices  19.9 us (22%)
  Pallas kernels  13.3 us (15%)
  local copies, waits for them, and re-layouts  6.06 us (7%)
    ppermute x7, waiting for transfers between devices, on_device(): lax.ppermute(lefts[s], 'row', [(h[i], h[(i + s) % blocks]) for h in halve...  37.8 us
    pallas_call x5, Pallas kernels, call(): pl.pallas_call(kernel, out_shape=out_shape, in_specs=specs, out_specs=jax...  13.3 us
    all_to_all x1, waiting for transfers between devices, on_device(): lax.all_to_all(crossed, 'row', split_axis=0, concat_axis=0, tiled=True, a...  11.3 us
    all_to_all x1, starting transfers between devices, on_device(): lax.all_to_all(right, 'row', split_axis=0, concat_axis=0, tiled=True)  7.53 us
    ppermute x7, starting transfers between devices, on_device(): lax.ppermute(lefts[s], 'row', [(h[i], h[(i + s) % blocks]) for h in halve...  6.18 us
    all_to_all x1, starting transfers between devices, on_device(): lax.all_to_all(crossed, 'row', split_axis=0, concat_axis=0, tiled=True, a...  6.15 us
    unnamed x24, local copies, waits for them, and re-layouts  6.06 us
  transfers between devices with their start and end apart: 9, of which 7 were waited for; matrix products, arithmetic and copies ran while one was open for 0% of the time, Pallas kernels for 6%

profile of v1, /device:TPU:0, one launch (start us, length us, event | category | flops | bytes accessed | tf_op | source)
XLA Modules:
  0.0 88.4 jit_solution(4966062727286931202)
XLA Ops:
  0.0 0.0 copy-start.2
  0.0 1.2 %copy-done.2 = bf16[16,256,128]{2,1,0:T(8,128)(2,1)S(1)} copy-done((bf16[16,256,128]{2,1,0:T(8,128)(2,1)S(1)}, bf16[16,256,128]{2,1,0:T(8,128)(2,1)}, u32[]{:S(2)}) %copy-start.2) | copy-done | bytes 1048600
  1.2 0.0 copy-start.5
  1.2 0.9 %copy-done.5 = bf16[128,512]{1,0:T(8,128)(2,1)S(1)} copy-done((bf16[128,512]{1,0:T(8,128)(2,1)S(1)}, bf16[128,512]{1,0:T(8,128)(2,1)}, u32[]{:S(2)}) %copy-start.5) | copy-done | bytes 131096
  2.1 0.0 copy-start.8
  2.1 0.7 copy-done.8
  2.8 0.0 copy-start.10
  2.9 0.7 copy-done.10
  3.5 3.3 %shard_map.64 = bf16[2,8,16,16,256]{4,3,2,1,0:T(8,128)(2,1)S(1)} custom-call(bf16[16,256,128]{2,1,0:T(8,128)(2,1)S(1)} %copy-done.2, s32[16,256]{1,0:T(8,128)S(1)} %copy-done.8, f32[1,128]{1,0:T(1,128)S(1)} %bitcast.6, bf16[128,512]{1,0:T(8,128)(2,1)S(1)} %copy-done.5), custom_call_target="tpu_custom_call" | custom-call | flops 1000000000 | bytes 4000000 | tf_op jit(solution)/shard_map/pallas_call | solution.py:118
  6.8 0.0 copy-start
  6.8 1.3 %copy-done = bf16[2,8,16,16,256]{4,3,2,1,0:T(8,128)(2,1)} copy-done((bf16[2,8,16,16,256]{4,3,2,1,0:T(8,128)(2,1)}, bf16[2,8,16,16,256]{4,3,2,1,0:T(8,128)(2,1)S(1)}, u32[]{:S(2)}) %copy-start) | copy-done | bytes 2097176
  8.1 0.0 copy-start.3
  8.1 0.0 copy-start.6
  8.1 0.0 copy-start.9
  8.1 0.0 copy-start.11
  8.1 7.5 %all-to-all-start = ((bf16[16,16,16,256]{3,2,1,0:T(8,128)(2,1)}), bf16[16,16,16,256]{3,2,1,0:T(8,128)(2,1)S(1)}, u32[]{:S(2)}, u32[]{:S(2)}) async-start(bf16[16,16,16,256]{3,2,1,0:T(8,128)(2,1)} %bitcast.5), calls=%async_computation | async-start | bytes 4194304 | tf_op jit(solution)/shard_map/all_to_all | solution.py:148
  15.7 0.0 copy-done.3
  15.7 0.0 copy-done.6
  15.7 0.0 copy-done.9
  15.7 0.0 copy-done.11
  15.7 3.1 %shard_map.65 = (bf16[16,16,256]{2,1,0:T(8,128)(2,1)S(1)}, bf16[16,16,256]{2,1,0:T(8,128)(2,1)S(1)}, bf16[16,16,256]{2,1,0:T(8,128)(2,1)S(1)}, bf16[16,16,256]{2...) custom-call(s32[1]{0:T(128)} %bitcast.me_ref, ...), custom_call_target="tpu_custom_call" | custom-call | flops 1000000000 | bytes 4000000 | tf_op jit(solution)/shard_map/pallas_call | solution.py:118
  18.9 0.5 collective-permute-start
  19.3 1.7 %collective-permute-start.1 = (bf16[16,16,256]{2,1,0:T(8,128)(2,1)S(1)}, bf16[16,16,256]{2,1,0:T(8,128)(2,1)S(1)}, u32[]{:S(2)}, u32[]{:S(2)}) collective-permute-start(bf16[16,16,256]{2,1,0:T(8,128)(2,1)S(1)} %get-tuple-element.15), channel_id=1, source_target_pairs={{0,2},{1,3},{2,4},{3,5},{4,6},{5,7},{6,0},{7,1},{8,10},{9,11},{10,... | collective-permute-start | bytes 393224 | tf_op jit(solution)/shard_map/ppermute | solution.py:157
  21.0 2.2 %collective-permute-start.2 = (bf16[16,16,256]{2,1,0:T(8,128)(2,1)S(1)}, bf16[16,16,256]{2,1,0:T(8,128)(2,1)S(1)}, u32[]{:S(2)}, u32[]{:S(2)}) collective-permute-start(bf16[16,16,256]{2,1,0:T(8,128)(2,1)S(1)} %get-tuple-element.16), channel_id=1, source_target_pairs={{0,3},{1,4},{2,5},{3,6},{4,7},{5,0},{6,1},{7,2},{8,11},{9,12},{10,... | collective-permute-start | bytes 393224 | tf_op jit(solution)/shard_map/ppermute | solution.py:157
  23.2 0.6 collective-permute-start.3
  23.8 0.1 collective-permute-start.4
  23.9 23.5 %collective-permute-done.rest_1_ = bf16[16,16,256]{2,1,0:T(8,128)(2,1)S(1)} collective-permute-done((bf16[16,16,256]{2,1,0:T(8,128)(2,1)S(1)}, bf16[16,16,256]{2,1,0:T(8,128)(2,1)S(1)}, u32[]{:S(2)}, u32[]{:S(2)}) %collective-permute-start) | collective-permute-done | bytes 131104 | tf_op jit(solution)/shard_map/ppermute | solution.py:157
  47.4 0.0 collective-permute-start.5
  47.4 0.9 %collective-permute-done.1.rest_2_ = bf16[16,16,256]{2,1,0:T(8,128)(2,1)S(1)} collective-permute-done((bf16[16,16,256]{2,1,0:T(8,128)(2,1)S(1)}, bf16[16,16,256]{2,1,0:T(8,128)(2,1)S(1)}, u32[]{:S(2)}, u32[]{:S(2)}) %collective-permute-start.1) | collective-permute-done | bytes 131104 | tf_op jit(solution)/shard_map/ppermute | solution.py:157
  48.3 1.1 %collective-permute-start.6 = (bf16[16,16,256]{2,1,0:T(8,128)(2,1)S(1)}, bf16[16,16,256]{2,1,0:T(8,128)(2,1)S(1)}, u32[]{:S(2)}, u32[]{:S(2)}) collective-permute-start(bf16[16,16,256]{2,1,0:T(8,128)(2,1)S(1)} %get-tuple-element.20), channel_id=1, source_target_pairs={{0,7},{1,0},{2,1},{3,2},{4,3},{5,4},{6,5},{7,6},{8,15},{9,8},{10,9... | collective-permute-start | bytes 393224 | tf_op jit(solution)/shard_map/ppermute | solution.py:157
  49.5 0.0 collective-permute-done.2.rest_3_
  49.5 4.2 %collective-permute-done.3.rest_4_ = bf16[16,16,256]{2,1,0:T(8,128)(2,1)S(1)} collective-permute-done((bf16[16,16,256]{2,1,0:T(8,128)(2,1)S(1)}, bf16[16,16,256]{2,1,0:T(8,128)(2,1)S(1)}, u32[]{:S(2)}, u32[]{:S(2)}) %collective-permute-start.3) | collective-permute-done | bytes 131104 | tf_op jit(solution)/shard_map/ppermute | solution.py:157
  53.6 2.8 %collective-permute-done.4.rest_5_ = bf16[16,16,256]{2,1,0:T(8,128)(2,1)S(1)} collective-permute-done((bf16[16,16,256]{2,1,0:T(8,128)(2,1)S(1)}, bf16[16,16,256]{2,1,0:T(8,128)(2,1)S(1)}, u32[]{:S(2)}, u32[]{:S(2)}) %collective-permute-start.4) | collective-permute-done | bytes 131104 | tf_op jit(solution)/shard_map/ppermute | solution.py:157
  56.5 2.8 %collective-permute-done.5.rest_6_ = bf16[16,16,256]{2,1,0:T(8,128)(2,1)S(1)} collective-permute-done((bf16[16,16,256]{2,1,0:T(8,128)(2,1)S(1)}, bf16[16,16,256]{2,1,0:T(8,128)(2,1)S(1)}, u32[]{:S(2)}, u32[]{:S(2)}) %collective-permute-start.5) | collective-permute-done | bytes 131104 | tf_op jit(solution)/shard_map/ppermute | solution.py:157
  59.3 3.6 %collective-permute-done.6.rest_7_ = bf16[16,16,256]{2,1,0:T(8,128)(2,1)S(1)} collective-permute-done((bf16[16,16,256]{2,1,0:T(8,128)(2,1)S(1)}, bf16[16,16,256]{2,1,0:T(8,128)(2,1)S(1)}, u32[]{:S(2)}, u32[]{:S(2)}) %collective-permute-start.6) | collective-permute-done | bytes 131104 | tf_op jit(solution)/shard_map/ppermute | solution.py:157
  62.8 0.0 all-to-all-done.right_ref
  62.8 1.8 %shard_map.66 = bf16[8,16,16,256]{3,2,1,0:T(8,128)(2,1)} custom-call(s32[1]{0:T(128)} %bitcast.me_ref, bf16[16,16,16,256]{3,2,1,0:T(8,128)(2,1)S(1)} %all-to-all-done.right_ref, bf16[16,16,256]{2,1,0:T(8,128)(2,1)S(1)} %get-tuple-element.13.rest_0_, bf16[16,16,256]{2,1,0:T(8,128)(2,1)S(1)} %collective-permute-done.rest_1_, ...), custom_call_target="tpu_custom_call" | custom-call | flops 1000000000 | bytes 4000000 | tf_op jit(solution)/shard_map/pallas_call | solution.py:118
  64.6 0.0 copy-start.7
  64.6 6.1 %all-to-all-start.1 = ((bf16[8,16,16,256]{3,2,1,0:T(8,128)(2,1)}), bf16[8,16,16,256]{3,2,1,0:T(8,128)(2,1)S(1)}, u32[]{:S(2)}, u32[]{:S(2)}) async-start(bf16[8,16,16,256]{3,2,1,0:T(8,128)(2,1)} %shard_map.66), calls=%async_computation.1 | async-start | bytes 2097152 | tf_op jit(solution)/shard_map/all_to_all | solution.py:168
  70.8 0.0 copy-done.7
  70.8 0.0 copy-start.4
  70.8 1.2 %copy-done.4 = bf16[16,256,128]{2,1,0:T(8,128)(2,1)S(1)} copy-done((bf16[16,256,128]{2,1,0:T(8,128)(2,1)S(1)}, bf16[16,256,128]{2,1,0:T(8,128)(2,1)}, u32[]{:S(2)}) %copy-start.4) | copy-done | bytes 1048600
  72.0 0.0 copy-start.1
  72.0 1.9 %shard_map.67.gate_ref = f32[16,256,128]{2,1,0:T(8,128)S(1)} custom-call(bf16[16,256,128]{2,1,0:T(8,128)(2,1)S(1)} %copy-done.4, f32[1,128]{1,0:T(1,128)S(1)} %bitcast.8, bf16[128,128]{1,0:T(8,128)(2,1)S(1)} %copy-done.7), custom_call_target="tpu_custom_call" | custom-call | flops 1000000000 | bytes 4000000 | tf_op jit(solution)/shard_map/pallas_call | solution.py:118
  74.0 11.3 %all-to-all-done.1 = bf16[8,16,16,256]{3,2,1,0:T(8,128)(2,1)S(1)} async-done(((bf16[8,16,16,256]{3,2,1,0:T(8,128)(2,1)}), bf16[8,16,16,256]{3,2,1,0:T(8,128)(2,1)S(1)}, u32[]{:S(2)}, u32[]{:S(2)}) %all-to-all-start.1) | async-done | bytes 1048608 | tf_op jit(solution)/shard_map/all_to_all | solution.py:168
  85.3 0.0 copy-done.1
  85.3 3.2 %shard_map.68 = bf16[16,256,128]{2,1,0:T(8,128)(2,1)} custom-call(bf16[128,16,256]{2,1,0:T(8,128)(2,1)S(1)} %bitcast.4, f32[16,256,128]{2,1,0:T(8,128)S(1)} %shard_map.67.gate_ref, bf16[128,128]{1,0:T(8,128)(2,1)S(1)} %copy-done.1), custom_call_target="tpu_custom_call" | custom-call | flops 1000000000 | bytes 4000000 | tf_op jit(solution)/shard_map/pallas_call | solution.py:118
Async XLA Ops:
  0.0 1.2 %copy-start.2 = (bf16[16,256,128]{2,1,0:T(8,128)(2,1)S(1)}, bf16[16,256,128]{2,1,0:T(8,128)(2,1)}, u32[]{:S(2)}) copy-start(bf16[16,256,128]{2,1,0:T(8,128)(2,1)} %pair_ref.5) | copy-start | bytes 3145732
  1.2 0.9 %copy-start.5 = (bf16[128,512]{1,0:T(8,128)(2,1)S(1)}, bf16[128,512]{1,0:T(8,128)(2,1)}, u32[]{:S(2)}) copy-start(bf16[128,512]{1,0:T(8,128)(2,1)} %proj_ref.5) | copy-start | bytes 393220
  2.1 0.7 copy-start.8
  2.8 0.7 copy-start.10
  6.8 1.3 %copy-start = (bf16[2,8,16,16,256]{4,3,2,1,0:T(8,128)(2,1)}, bf16[2,8,16,16,256]{4,3,2,1,0:T(8,128)(2,1)S(1)}, u32[]{:S(2)}) copy-start(bf16[2,8,16,16,256]{4,3,2,1,0:T(8,128)(2,1)S(1)} %shard_map.64) | copy-start | bytes 6291460
  8.1 7.6 %copy-start.3 = (bf16[16,256,128]{2,1,0:T(8,128)(2,1)S(1)}, bf16[16,256,128]{2,1,0:T(8,128)(2,1)}, u32[]{:S(2)}) copy-start(bf16[16,256,128]{2,1,0:T(8,128)(2,1)} %pair_ref.5) | copy-start | bytes 3145732
  8.1 7.6 %copy-start.6 = (bf16[128,512]{1,0:T(8,128)(2,1)S(1)}, bf16[128,512]{1,0:T(8,128)(2,1)}, u32[]{:S(2)}) copy-start(bf16[128,512]{1,0:T(8,128)(2,1)} %proj_ref.5) | copy-start | bytes 393220
  8.1 7.6 %copy-start.9 = (s32[16,256]{1,0:T(8,128)S(1)}, s32[16,256]{1,0:T(8,128)}, u32[]{:S(2)}) copy-start(s32[16,256]{1,0:T(8,128)} %mask_ref.3) | copy-start | bytes 49156
  8.1 7.6 %copy-start.11 = (f32[128]{0:T(128)S(1)}, f32[128]{0:T(128)}, u32[]{:S(2)}) copy-start(f32[128]{0:T(128)} %param.8) | copy-start | bytes 1540
  8.1 54.7 %all-to-all-start = ((bf16[16,16,16,256]{3,2,1,0:T(8,128)(2,1)}), bf16[16,16,16,256]{3,2,1,0:T(8,128)(2,1)S(1)}, u32[]{:S(2)}, u32[]{:S(2)}) async-start(bf16[16,16,16,256]{3,2,1,0:T(8,128)(2,1)} %bitcast.5), calls=%async_computation | async-start | bytes 4194304 | tf_op jit(solution)/shard_map/all_to_all | solution.py:148
  18.9 28.5 %collective-permute-start = (bf16[16,16,256]{2,1,0:T(8,128)(2,1)S(1)}, bf16[16,16,256]{2,1,0:T(8,128)(2,1)S(1)}, u32[]{:S(2)}, u32[]{:S(2)}) collective-permute-start(bf16[16,16,256]{2,1,0:T(8,128)(2,1)S(1)} %get-tuple-element.14), channel_id=1, source_target_pairs={{0,1},{1,2},{2,3},{3,4},{4,5},{5,6},{6,7},{7,0},{8,9},{9,10},{10,1... | collective-permute-start | bytes 393224 | tf_op jit(solution)/shard_map/ppermute | solution.py:157
  19.3 29.0 %collective-permute-start.1 = (bf16[16,16,256]{2,1,0:T(8,128)(2,1)S(1)}, bf16[16,16,256]{2,1,0:T(8,128)(2,1)S(1)}, u32[]{:S(2)}, u32[]{:S(2)}) collective-permute-start(bf16[16,16,256]{2,1,0:T(8,128)(2,1)S(1)} %get-tuple-element.15), channel_id=1, source_target_pairs={{0,2},{1,3},{2,4},{3,5},{4,6},{5,7},{6,0},{7,1},{8,10},{9,11},{10,... | collective-permute-start | bytes 393224 | tf_op jit(solution)/shard_map/ppermute | solution.py:157
  21.0 28.5 %collective-permute-start.2 = (bf16[16,16,256]{2,1,0:T(8,128)(2,1)S(1)}, bf16[16,16,256]{2,1,0:T(8,128)(2,1)S(1)}, u32[]{:S(2)}, u32[]{:S(2)}) collective-permute-start(bf16[16,16,256]{2,1,0:T(8,128)(2,1)S(1)} %get-tuple-element.16), channel_id=1, source_target_pairs={{0,3},{1,4},{2,5},{3,6},{4,7},{5,0},{6,1},{7,2},{8,11},{9,12},{10,... | collective-permute-start | bytes 393224 | tf_op jit(solution)/shard_map/ppermute | solution.py:157
  23.2 30.4 %collective-permute-start.3 = (bf16[16,16,256]{2,1,0:T(8,128)(2,1)S(1)}, bf16[16,16,256]{2,1,0:T(8,128)(2,1)S(1)}, u32[]{:S(2)}, u32[]{:S(2)}) collective-permute-start(bf16[16,16,256]{2,1,0:T(8,128)(2,1)S(1)} %get-tuple-element.17), channel_id=1, source_target_pairs={{0,4},{1,5},{2,6},{3,7},{4,0},{5,1},{6,2},{7,3},{8,12},{9,13},{10,... | collective-permute-start | bytes 393224 | tf_op jit(solution)/shard_map/ppermute | solution.py:157
  23.8 32.7 %collective-permute-start.4 = (bf16[16,16,256]{2,1,0:T(8,128)(2,1)S(1)}, bf16[16,16,256]{2,1,0:T(8,128)(2,1)S(1)}, u32[]{:S(2)}, u32[]{:S(2)}) collective-permute-start(bf16[16,16,256]{2,1,0:T(8,128)(2,1)S(1)} %get-tuple-element.18), channel_id=1, source_target_pairs={{0,5},{1,6},{2,7},{3,0},{4,1},{5,2},{6,3},{7,4},{8,13},{9,14},{10,... | collective-permute-start | bytes 393224 | tf_op jit(solution)/shard_map/ppermute | solution.py:157
  47.4 11.9 %collective-permute-start.5 = (bf16[16,16,256]{2,1,0:T(8,128)(2,1)S(1)}, bf16[16,16,256]{2,1,0:T(8,128)(2,1)S(1)}, u32[]{:S(2)}, u32[]{:S(2)}) collective-permute-start(bf16[16,16,256]{2,1,0:T(8,128)(2,1)S(1)} %get-tuple-element.19), channel_id=1, source_target_pairs={{0,6},{1,7},{2,0},{3,1},{4,2},{5,3},{6,4},{7,5},{8,14},{9,15},{10,... | collective-permute-start | bytes 393224 | tf_op jit(solution)/shard_map/ppermute | solution.py:157
  48.3 14.5 %collective-permute-start.6 = (bf16[16,16,256]{2,1,0:T(8,128)(2,1)S(1)}, bf16[16,16,256]{2,1,0:T(8,128)(2,1)S(1)}, u32[]{:S(2)}, u32[]{:S(2)}) collective-permute-start(bf16[16,16,256]{2,1,0:T(8,128)(2,1)S(1)} %get-tuple-element.20), channel_id=1, source_target_pairs={{0,7},{1,0},{2,1},{3,2},{4,3},{5,4},{6,5},{7,6},{8,15},{9,8},{10,9... | collective-permute-start | bytes 393224 | tf_op jit(solution)/shard_map/ppermute | solution.py:157
  64.6 6.2 %copy-start.7 = (bf16[128,128]{1,0:T(8,128)(2,1)S(1)}, bf16[128,128]{1,0:T(8,128)(2,1)}, u32[]{:S(2)}) copy-start(bf16[128,128]{1,0:T(8,128)(2,1)} %proj_ref.6) | copy-start | bytes 98308
  64.6 20.6 %all-to-all-start.1 = ((bf16[8,16,16,256]{3,2,1,0:T(8,128)(2,1)}), bf16[8,16,16,256]{3,2,1,0:T(8,128)(2,1)S(1)}, u32[]{:S(2)}, u32[]{:S(2)}) async-start(bf16[8,16,16,256]{3,2,1,0:T(8,128)(2,1)} %shard_map.66), calls=%async_computation.1 | async-start | bytes 2097152 | tf_op jit(solution)/shard_map/all_to_all | solution.py:168
  70.8 1.2 %copy-start.4 = (bf16[16,256,128]{2,1,0:T(8,128)(2,1)S(1)}, bf16[16,256,128]{2,1,0:T(8,128)(2,1)}, u32[]{:S(2)}) copy-start(bf16[16,256,128]{2,1,0:T(8,128)(2,1)} %pair_ref.5) | copy-start | bytes 3145732
  72.0 13.2 %copy-start.1 = (bf16[128,128]{1,0:T(8,128)(2,1)S(1)}, bf16[128,128]{1,0:T(8,128)(2,1)}, u32[]{:S(2)}) copy-start(bf16[128,128]{1,0:T(8,128)(2,1)} %proj_ref.7) | copy-start | bytes 98308

commit v2 on v1

--- a/solution.py
+++ b/solution.py
@@ -10,7 +10,7 @@
 EPS = 1e-05
 VMEM = pl.BlockSpec(memory_space=pltpu.VMEM)
 SMEM = pl.BlockSpec(memory_space=pltpu.SMEM)
-PARAMS = pltpu.CompilerParams(vmem_limit_bytes=48 * 2**20)
+ANY = pl.BlockSpec(memory_space=pl.ANY)
 OVER_LAST = (((1,), (1,)), ((), ()))
 
 
@@ -18,8 +18,8 @@
     return 0.5 * jnp.tanh(0.5 * x) + 0.5
 
 
-def normed_row(pair_ref, gain, r):
-    x = pair_ref[r].astype(jnp.float32)
+def normed_rows(pair, gain):
+    x = pair.astype(jnp.float32)
     centered = x - jnp.mean(x, axis=-1, keepdims=True)
     variance = jnp.mean(centered * centered, axis=-1, keepdims=True)
     return (centered * lax.rsqrt(variance + EPS) * gain).astype(jnp.bfloat16)
@@ -32,7 +32,7 @@
     gain = gain_ref[...]
 
     def step(r, carry):
-        normed = normed_row(pair_ref, gain, r)
+        normed = normed_rows(pair_ref[r], gain)
         proj = lax.dot_general(weights, normed, OVER_LAST, preferred_element_type=jnp.float32)
         keep = mask_ref[pl.ds(r, 1), :].astype(jnp.float32)
         value = keep * sigmoid(proj[hidden:]) * proj[:hidden]
@@ -43,14 +43,50 @@
     lax.fori_loop(0, rows, step, 0, unroll=4)
 
 
-def right_kernel(pair_ref, mask_ref, gain_ref, proj_ref, out_ref, total):
-    copies, blocks, group, rows, tokens = out_ref.shape
-    operand(pair_ref, mask_ref, gain_ref, proj_ref, total, 2)
+def right_kernel(
+    pair_hbm, mask_hbm, gain_hbm, proj_hbm, out_hbm,
+    pair_ref, mask_ref, gain_ref, weights_ref, total, staged, in_sems, out_sems,
+):
+    copies, blocks, group, rows, tokens = out_hbm.shape
+    hidden = blocks * group
+    loads = [
+        pltpu.make_async_copy(source, target, in_sems.at[i])
+        for i, (source, target) in enumerate((
+            (pair_hbm, pair_ref),
+            (proj_hbm.at[:, 2 * hidden : 4 * hidden], weights_ref),
+            (mask_hbm, mask_ref),
+            (gain_hbm, gain_ref),
+        ))
+    ]
+    for load in loads:
+        load.start()
+    for load in loads:
+        load.wait()
+    weights = weights_ref[...].T
+    gain = gain_ref[...]
+    step = 4 if rows % 4 == 0 else 1
+    for first in range(0, rows, step):
+        x = pair_ref[first : first + step].reshape(step * tokens, -1)
+        proj = lax.dot_general(
+            weights, normed_rows(x, gain), OVER_LAST, preferred_element_type=jnp.float32
+        )
+        for r in range(first, first + step):
+            of_row = proj[:, (r - first) * tokens : (r - first + 1) * tokens]
+            keep = mask_ref[r : r + 1, :].astype(jnp.float32)
+            value = keep * sigmoid(of_row[hidden:]) * of_row[:hidden]
+            for t in range(tokens // 128):
+                total[t, pl.ds(r, hidden, stride=rows), :] = value[:, t * 128 : (t + 1) * 128]
+    stores = []
     for b in range(blocks):
         for t in range(tokens // 128):
             block = total[t, b * group * rows : (b + 1) * group * rows, :].astype(jnp.bfloat16)
-            for c in range(copies):
-                out_ref[c, b, :, :, t * 128 : (t + 1) * 128] = block.reshape(group, rows, 128)
+            staged[b, :, :, t * 128 : (t + 1) * 128] = block.reshape(group, rows, 128)
+        for c in range(copies):
+            store = pltpu.make_async_copy(staged.at[b], out_hbm.at[c, b], out_sems.at[c, b])
+            store.start()
+            stores.append(store)
+    for store in stores:
+        store.wait()
 
 
 def left_kernel(me_ref, pair_ref, mask_ref, gain_ref, proj_ref, *rest):
@@ -85,43 +121,44 @@
     weights = proj_ref[...]
 
     def step(r, carry):
-        normed = normed_row(pair_ref, gain, r)
+        normed = normed_rows(pair_ref[r], gain)
         out_ref[r] = sigmoid(jnp.dot(normed, weights, preferred_element_type=jnp.float32))
         return carry
 
     lax.fori_loop(0, rows, step, 0, unroll=4)
 
 
-def final_kernel(crossed_ref, gate_ref, proj_ref, out_ref, total):
+def final_kernel(crossed_ref, gate_ref, proj_ref, out_hbm, total, staged, sems):
     hidden, rows, tokens = crossed_ref.shape
+    weights = proj_ref[...]
+    stores = []
     for t in range(tokens // 128):
         lanes = slice(t * 128, (t + 1) * 128)
         x = crossed_ref[:, :, lanes].astype(jnp.float32)
         centered = x - jnp.mean(x, axis=0, keepdims=True)
         variance = jnp.mean(centered * centered, axis=0, keepdims=True)
         total[t] = (centered * lax.rsqrt(variance + EPS)).reshape(hidden * rows, 128)
-    weights = proj_ref[...]
-
-    def step(r, carry):
-        for t in range(tokens // 128):
-            lanes = slice(t * 128, (t + 1) * 128)
+        for r in range(rows):
             x = total[t, pl.ds(r, hidden, stride=rows), :].T.astype(jnp.bfloat16)
             mixed = jnp.dot(x, weights, preferred_element_type=jnp.float32)
-            out_ref[r, lanes, :] = (gate_ref[r, lanes, :] * mixed).astype(jnp.bfloat16)
-        return carry
-
-    lax.fori_loop(0, rows, step, 0, unroll=4)
-
-
-def call(kernel, out_shape, operands, scratch=(), cost=1.0):
-    specs = [SMEM if x.dtype == jnp.int32 and x.ndim == 1 else VMEM for x in operands]
+            staged[r, lanes, :] = (gate_ref[r, lanes, :] * mixed).astype(jnp.bfloat16)
+        part = pl.ds(t * 128, 128)
+        store = pltpu.make_async_copy(staged.at[:, part], out_hbm.at[:, part], sems.at[t])
+        store.start()
+        stores.append(store)
+    for store in stores:
+        store.wait()
+
+
+def call(kernel, out_shape, operands, scratch=(), cost=1.0, in_hbm=False, out_hbm=False):
+    specs = [ANY for _ in operands] if in_hbm else [SMEM if x.dtype == jnp.int32 and x.ndim == 1 else VMEM for x in operands]
     return pl.pallas_call(
         kernel,
         out_shape=out_shape,
         in_specs=specs,
-        out_specs=jax.tree.map(lambda _: VMEM, out_shape),
+        out_specs=jax.tree.map(lambda _: ANY if out_hbm else VMEM, out_shape),
         scratch_shapes=list(scratch),
-        compiler_params=PARAMS,
+        compiler_params=pltpu.CompilerParams(vmem_limit_bytes=(62 if in_hbm else 48) * 2**20),
         cost_estimate=pl.CostEstimate(
             flops=int(cost * 1e9), bytes_accessed=int(cost * 4e6), transcendentals=0
         ),
@@ -143,7 +180,18 @@
         right_kernel,
         sds((2, blocks, group, rows, tokens), bf16),
         (pair, pair_mask, gain, in_proj),
-        (total,),
+        (
+            pltpu.VMEM(pair.shape, bf16),
+            pltpu.VMEM(pair_mask.shape, jnp.int32),
+            pltpu.VMEM(gain.shape, jnp.float32),
+            pltpu.VMEM((width, 2 * hidden), bf16),
+            total,
+            pltpu.VMEM((blocks, group, rows, tokens), bf16),
+            pltpu.SemaphoreType.DMA((4,)),
+            pltpu.SemaphoreType.DMA((2, blocks)),
+        ),
+        in_hbm=True,
+        out_hbm=True,
     ).reshape(devices, group, rows, tokens)
     right = lax.all_to_all(right, "row", split_axis=0, concat_axis=0, tiled=True)
     lefts = call(
@@ -169,7 +217,17 @@
         crossed, "row", split_axis=0, concat_axis=0, tiled=True,
         axis_index_groups=[list(h) for h in halves],
     ).reshape(hidden, rows, tokens)
-    return call(final_kernel, sds((rows, tokens, width), bf16), (crossed, gate, out_proj), (total,))
+    return call(
+        final_kernel,
+        sds((rows, tokens, width), bf16),
+        (crossed, gate, out_proj),
+        (
+            total,
+            pltpu.VMEM((rows, tokens, width), bf16),
+            pltpu.SemaphoreType.DMA((tokens // 128,)),
+        ),
+        out_hbm=True,
+    )
 
 
 def solution(mesh):

time: 88.9 us -> 85.1 us (0.957)
  local copies, waits for them, and re-layouts: 6.06 us -> 1.25 us
  Pallas kernels: 13.3 us -> 14.4 us
    unnamed x24 -> x14, local copies, waits for them, and re-layouts: 6.06 us -> 1.25 us
    pallas_call x5, Pallas kernels: 13.3 us -> 14.4 us  [call(): pl.pallas_call(kernel, out_shape=out_shape, in_specs=specs, out_specs=jax...]
where the time goes in v2:
time: 85.1 us; the launch traced here: 84.7 us
  waiting for transfers between devices  49.1 us (58%)
  starting transfers between devices  19.9 us (23%)
  Pallas kernels  14.4 us (17%)
  local copies, waits for them, and re-layouts  1.25 us (1%)
    ppermute x7, waiting for transfers between devices, on_device(): lax.ppermute(lefts[s], 'row', [(h[i], h[(i + s) % blocks]) for h in halve...  37.8 us
    pallas_call x5, Pallas kernels, call(): pl.pallas_call(kernel, out_shape=out_shape, in_specs=specs, out_specs=jax...  14.4 us
    all_to_all x1, waiting for transfers between devices, on_device(): lax.all_to_all(crossed, 'row', split_axis=0, concat_axis=0, tiled=True, a...  11.3 us
    all_to_all x1, starting transfers between devices, on_device(): lax.all_to_all(right, 'row', split_axis=0, concat_axis=0, tiled=True)  7.53 us
    ppermute x7, starting transfers between devices, on_device(): lax.ppermute(lefts[s], 'row', [(h[i], h[(i + s) % blocks]) for h in halve...  6.18 us
    all_to_all x1, starting transfers between devices, on_device(): lax.all_to_all(crossed, 'row', split_axis=0, concat_axis=0, tiled=True, a...  6.15 us
  transfers between devices with their start and end apart: 9, of which 7 were waited for; matrix products, arithmetic and copies ran while one was open for 0% of the time, Pallas kernels for 6%

profile of v2, /device:TPU:0, one launch (start us, length us, event | category | flops | bytes accessed | tf_op | source)
XLA Modules:
  0.0 84.7 jit_solution(678742418291172062)
XLA Ops:
  0.0 5.0 %shard_map.64 = bf16[2,8,16,16,256]{4,3,2,1,0:T(8,128)(2,1)} custom-call(bf16[16,256,128]{2,1,0:T(8,128)(2,1)} %pair_ref.3, s32[16,256]{1,0:T(8,128)} %mask_ref.1, f32[1,128]{1,0:T(1,128)} %bitcast.5, bf16[128,512]{1,0:T(8,128)(2,1)} %proj_ref.3), custom_call_target="tpu_custom_call" | custom-call | flops 1000000000 | bytes 4000000 | tf_op jit(solution)/shard_map/pallas_call | solution.py:155
  5.0 0.0 copy-start.1
  5.0 0.0 copy-start.3
  5.1 0.0 copy-start.5
  5.1 0.0 copy-start.6
  5.1 7.5 %all-to-all-start = ((bf16[16,16,16,256]{3,2,1,0:T(8,128)(2,1)}), bf16[16,16,16,256]{3,2,1,0:T(8,128)(2,1)S(1)}, u32[]{:S(2)}, u32[]{:S(2)}) async-start(bf16[16,16,16,256]{3,2,1,0:T(8,128)(2,1)} %bitcast.8), calls=%async_computation | async-start | bytes 4194304 | tf_op jit(solution)/shard_map/all_to_all | solution.py:196
  12.6 0.0 copy-done.1
  12.6 0.0 copy-done.3
  12.6 0.0 copy-done.5
  12.7 0.0 copy-done.6
  12.7 3.1 %shard_map.65 = (bf16[16,16,256]{2,1,0:T(8,128)(2,1)S(1)}, bf16[16,16,256]{2,1,0:T(8,128)(2,1)S(1)}, bf16[16,16,256]{2,1,0:T(8,128)(2,1)S(1)}, bf16[16,16,256]{2...) custom-call(s32[1]{0:T(128)} %bitcast.me_ref, ...), custom_call_target="tpu_custom_call" | custom-call | flops 1000000000 | bytes 4000000 | tf_op jit(solution)/shard_map/pallas_call | solution.py:155
  15.8 0.5 collective-permute-start
  16.3 1.7 %collective-permute-start.1 = (bf16[16,16,256]{2,1,0:T(8,128)(2,1)S(1)}, bf16[16,16,256]{2,1,0:T(8,128)(2,1)S(1)}, u32[]{:S(2)}, u32[]{:S(2)}) collective-permute-start(bf16[16,16,256]{2,1,0:T(8,128)(2,1)S(1)} %get-tuple-element.15), channel_id=1, source_target_pairs={{0,2},{1,3},{2,4},{3,5},{4,6},{5,7},{6,0},{7,1},{8,10},{9,11},{10,... | collective-permute-start | bytes 393224 | tf_op jit(solution)/shard_map/ppermute | solution.py:205
  17.9 2.2 %collective-permute-start.2 = (bf16[16,16,256]{2,1,0:T(8,128)(2,1)S(1)}, bf16[16,16,256]{2,1,0:T(8,128)(2,1)S(1)}, u32[]{:S(2)}, u32[]{:S(2)}) collective-permute-start(bf16[16,16,256]{2,1,0:T(8,128)(2,1)S(1)} %get-tuple-element.16), channel_id=1, source_target_pairs={{0,3},{1,4},{2,5},{3,6},{4,7},{5,0},{6,1},{7,2},{8,11},{9,12},{10,... | collective-permute-start | bytes 393224 | tf_op jit(solution)/shard_map/ppermute | solution.py:205
  20.2 0.6 collective-permute-start.3
  20.7 0.2 collective-permute-start.4
  20.9 23.5 %collective-permute-done.rest_1_ = bf16[16,16,256]{2,1,0:T(8,128)(2,1)S(1)} collective-permute-done((bf16[16,16,256]{2,1,0:T(8,128)(2,1)S(1)}, bf16[16,16,256]{2,1,0:T(8,128)(2,1)S(1)}, u32[]{:S(2)}, u32[]{:S(2)}) %collective-permute-start) | collective-permute-done | bytes 131104 | tf_op jit(solution)/shard_map/ppermute | solution.py:205
  44.4 0.0 collective-permute-start.5
  44.4 0.9 %collective-permute-done.1.rest_2_ = bf16[16,16,256]{2,1,0:T(8,128)(2,1)S(1)} collective-permute-done((bf16[16,16,256]{2,1,0:T(8,128)(2,1)S(1)}, bf16[16,16,256]{2,1,0:T(8,128)(2,1)S(1)}, u32[]{:S(2)}, u32[]{:S(2)}) %collective-permute-start.1) | collective-permute-done | bytes 131104 | tf_op jit(solution)/shard_map/ppermute | solution.py:205
  45.3 1.1 %collective-permute-start.6 = (bf16[16,16,256]{2,1,0:T(8,128)(2,1)S(1)}, bf16[16,16,256]{2,1,0:T(8,128)(2,1)S(1)}, u32[]{:S(2)}, u32[]{:S(2)}) collective-permute-start(bf16[16,16,256]{2,1,0:T(8,128)(2,1)S(1)} %get-tuple-element.20), channel_id=1, source_target_pairs={{0,7},{1,0},{2,1},{3,2},{4,3},{5,4},{6,5},{7,6},{8,15},{9,8},{10,9... | collective-permute-start | bytes 393224 | tf_op jit(solution)/shard_map/ppermute | solution.py:205
  46.4 0.0 collective-permute-done.2.rest_3_
  46.4 4.2 %collective-permute-done.3.rest_4_ = bf16[16,16,256]{2,1,0:T(8,128)(2,1)S(1)} collective-permute-done((bf16[16,16,256]{2,1,0:T(8,128)(2,1)S(1)}, bf16[16,16,256]{2,1,0:T(8,128)(2,1)S(1)}, u32[]{:S(2)}, u32[]{:S(2)}) %collective-permute-start.3) | collective-permute-done | bytes 131104 | tf_op jit(solution)/shard_map/ppermute | solution.py:205
  50.6 2.8 %collective-permute-done.4.rest_5_ = bf16[16,16,256]{2,1,0:T(8,128)(2,1)S(1)} collective-permute-done((bf16[16,16,256]{2,1,0:T(8,128)(2,1)S(1)}, bf16[16,16,256]{2,1,0:T(8,128)(2,1)S(1)}, u32[]{:S(2)}, u32[]{:S(2)}) %collective-permute-start.4) | collective-permute-done | bytes 131104 | tf_op jit(solution)/shard_map/ppermute | solution.py:205
  53.4 2.8 %collective-permute-done.5.rest_6_ = bf16[16,16,256]{2,1,0:T(8,128)(2,1)S(1)} collective-permute-done((bf16[16,16,256]{2,1,0:T(8,128)(2,1)S(1)}, bf16[16,16,256]{2,1,0:T(8,128)(2,1)S(1)}, u32[]{:S(2)}, u32[]{:S(2)}) %collective-permute-start.5) | collective-permute-done | bytes 131104 | tf_op jit(solution)/shard_map/ppermute | solution.py:205
  56.2 3.6 %collective-permute-done.6.rest_7_ = bf16[16,16,256]{2,1,0:T(8,128)(2,1)S(1)} collective-permute-done((bf16[16,16,256]{2,1,0:T(8,128)(2,1)S(1)}, bf16[16,16,256]{2,1,0:T(8,128)(2,1)S(1)}, u32[]{:S(2)}, u32[]{:S(2)}) %collective-permute-start.6) | collective-permute-done | bytes 131104 | tf_op jit(solution)/shard_map/ppermute | solution.py:205
  59.8 0.0 all-to-all-done.right_ref
  59.8 1.8 %shard_map.66 = bf16[8,16,16,256]{3,2,1,0:T(8,128)(2,1)} custom-call(s32[1]{0:T(128)} %bitcast.me_ref, bf16[16,16,16,256]{3,2,1,0:T(8,128)(2,1)S(1)} %all-to-all-done.right_ref, bf16[16,16,256]{2,1,0:T(8,128)(2,1)S(1)} %get-tuple-element.13.rest_0_, bf16[16,16,256]{2,1,0:T(8,128)(2,1)S(1)} %collective-permute-done.rest_1_, ...), custom_call_target="tpu_custom_call" | custom-call | flops 1000000000 | bytes 4000000 | tf_op jit(solution)/shard_map/pallas_call | solution.py:155
  61.6 0.0 copy-start.4
  61.6 6.2 %all-to-all-start.1 = ((bf16[8,16,16,256]{3,2,1,0:T(8,128)(2,1)}), bf16[8,16,16,256]{3,2,1,0:T(8,128)(2,1)S(1)}, u32[]{:S(2)}, u32[]{:S(2)}) async-start(bf16[8,16,16,256]{3,2,1,0:T(8,128)(2,1)} %shard_map.66), calls=%async_computation.1 | async-start | bytes 2097152 | tf_op jit(solution)/shard_map/all_to_all | solution.py:216
  67.8 0.0 copy-done.4
  67.8 0.0 copy-start.2
  67.8 1.2 %copy-done.2 = bf16[16,256,128]{2,1,0:T(8,128)(2,1)S(1)} copy-done((bf16[16,256,128]{2,1,0:T(8,128)(2,1)S(1)}, bf16[16,256,128]{2,1,0:T(8,128)(2,1)}, u32[]{:S(2)}) %copy-start.2) | copy-done | bytes 1048600
  69.0 0.0 copy-start
  69.0 1.9 %shard_map.67.gate_ref = f32[16,256,128]{2,1,0:T(8,128)S(1)} custom-call(bf16[16,256,128]{2,1,0:T(8,128)(2,1)S(1)} %copy-done.2, f32[1,128]{1,0:T(1,128)S(1)} %bitcast.7, bf16[128,128]{1,0:T(8,128)(2,1)S(1)} %copy-done.4), custom_call_target="tpu_custom_call" | custom-call | flops 1000000000 | bytes 4000000 | tf_op jit(solution)/shard_map/pallas_call | solution.py:155
  70.9 11.3 %all-to-all-done.1 = bf16[8,16,16,256]{3,2,1,0:T(8,128)(2,1)S(1)} async-done(((bf16[8,16,16,256]{3,2,1,0:T(8,128)(2,1)}), bf16[8,16,16,256]{3,2,1,0:T(8,128)(2,1)S(1)}, u32[]{:S(2)}, u32[]{:S(2)}) %all-to-all-start.1) | async-done | bytes 1048608 | tf_op jit(solution)/shard_map/all_to_all | solution.py:216
  82.2 0.0 copy-done
  82.2 2.5 %shard_map.68 = bf16[16,256,128]{2,1,0:T(8,128)(2,1)} custom-call(bf16[128,16,256]{2,1,0:T(8,128)(2,1)S(1)} %bitcast.4, f32[16,256,128]{2,1,0:T(8,128)S(1)} %shard_map.67.gate_ref, bf16[128,128]{1,0:T(8,128)(2,1)S(1)} %copy-done), custom_call_target="tpu_custom_call" | custom-call | flops 1000000000 | bytes 4000000 | tf_op jit(solution)/shard_map/pallas_call | solution.py:155
Async XLA Ops:
  5.0 7.6 %copy-start.1 = (bf16[16,256,128]{2,1,0:T(8,128)(2,1)S(1)}, bf16[16,256,128]{2,1,0:T(8,128)(2,1)}, u32[]{:S(2)}) copy-start(bf16[16,256,128]{2,1,0:T(8,128)(2,1)} %pair_ref.3) | copy-start | bytes 3145732
  5.0 7.6 %copy-start.3 = (bf16[128,512]{1,0:T(8,128)(2,1)S(1)}, bf16[128,512]{1,0:T(8,128)(2,1)}, u32[]{:S(2)}) copy-start(bf16[128,512]{1,0:T(8,128)(2,1)} %proj_ref.3) | copy-start | bytes 393220
  5.1 7.6 %copy-start.5 = (s32[16,256]{1,0:T(8,128)S(1)}, s32[16,256]{1,0:T(8,128)}, u32[]{:S(2)}) copy-start(s32[16,256]{1,0:T(8,128)} %mask_ref.1) | copy-start | bytes 49156
  5.1 7.6 %copy-start.6 = (f32[128]{0:T(128)S(1)}, f32[128]{0:T(128)}, u32[]{:S(2)}) copy-start(f32[128]{0:T(128)} %param.8) | copy-start | bytes 1540
  5.1 54.7 %all-to-all-start = ((bf16[16,16,16,256]{3,2,1,0:T(8,128)(2,1)}), bf16[16,16,16,256]{3,2,1,0:T(8,128)(2,1)S(1)}, u32[]{:S(2)}, u32[]{:S(2)}) async-start(bf16[16,16,16,256]{3,2,1,0:T(8,128)(2,1)} %bitcast.8), calls=%async_computation | async-start | bytes 4194304 | tf_op jit(solution)/shard_map/all_to_all | solution.py:196
  15.8 28.5 %collective-permute-start = (bf16[16,16,256]{2,1,0:T(8,128)(2,1)S(1)}, bf16[16,16,256]{2,1,0:T(8,128)(2,1)S(1)}, u32[]{:S(2)}, u32[]{:S(2)}) collective-permute-start(bf16[16,16,256]{2,1,0:T(8,128)(2,1)S(1)} %get-tuple-element.14), channel_id=1, source_target_pairs={{0,1},{1,2},{2,3},{3,4},{4,5},{5,6},{6,7},{7,0},{8,9},{9,10},{10,1... | collective-permute-start | bytes 393224 | tf_op jit(solution)/shard_map/ppermute | solution.py:205
  16.3 29.0 %collective-permute-start.1 = (bf16[16,16,256]{2,1,0:T(8,128)(2,1)S(1)}, bf16[16,16,256]{2,1,0:T(8,128)(2,1)S(1)}, u32[]{:S(2)}, u32[]{:S(2)}) collective-permute-start(bf16[16,16,256]{2,1,0:T(8,128)(2,1)S(1)} %get-tuple-element.15), channel_id=1, source_target_pairs={{0,2},{1,3},{2,4},{3,5},{4,6},{5,7},{6,0},{7,1},{8,10},{9,11},{10,... | collective-permute-start | bytes 393224 | tf_op jit(solution)/shard_map/ppermute | solution.py:205
  17.9 28.5 %collective-permute-start.2 = (bf16[16,16,256]{2,1,0:T(8,128)(2,1)S(1)}, bf16[16,16,256]{2,1,0:T(8,128)(2,1)S(1)}, u32[]{:S(2)}, u32[]{:S(2)}) collective-permute-start(bf16[16,16,256]{2,1,0:T(8,128)(2,1)S(1)} %get-tuple-element.16), channel_id=1, source_target_pairs={{0,3},{1,4},{2,5},{3,6},{4,7},{5,0},{6,1},{7,2},{8,11},{9,12},{10,... | collective-permute-start | bytes 393224 | tf_op jit(solution)/shard_map/ppermute | solution.py:205
  20.2 30.4 %collective-permute-start.3 = (bf16[16,16,256]{2,1,0:T(8,128)(2,1)S(1)}, bf16[16,16,256]{2,1,0:T(8,128)(2,1)S(1)}, u32[]{:S(2)}, u32[]{:S(2)}) collective-permute-start(bf16[16,16,256]{2,1,0:T(8,128)(2,1)S(1)} %get-tuple-element.17), channel_id=1, source_target_pairs={{0,4},{1,5},{2,6},{3,7},{4,0},{5,1},{6,2},{7,3},{8,12},{9,13},{10,... | collective-permute-start | bytes 393224 | tf_op jit(solution)/shard_map/ppermute | solution.py:205
  20.7 32.7 %collective-permute-start.4 = (bf16[16,16,256]{2,1,0:T(8,128)(2,1)S(1)}, bf16[16,16,256]{2,1,0:T(8,128)(2,1)S(1)}, u32[]{:S(2)}, u32[]{:S(2)}) collective-permute-start(bf16[16,16,256]{2,1,0:T(8,128)(2,1)S(1)} %get-tuple-element.18), channel_id=1, source_target_pairs={{0,5},{1,6},{2,7},{3,0},{4,1},{5,2},{6,3},{7,4},{8,13},{9,14},{10,... | collective-permute-start | bytes 393224 | tf_op jit(solution)/shard_map/ppermute | solution.py:205
  44.4 11.9 %collective-permute-start.5 = (bf16[16,16,256]{2,1,0:T(8,128)(2,1)S(1)}, bf16[16,16,256]{2,1,0:T(8,128)(2,1)S(1)}, u32[]{:S(2)}, u32[]{:S(2)}) collective-permute-start(bf16[16,16,256]{2,1,0:T(8,128)(2,1)S(1)} %get-tuple-element.19), channel_id=1, source_target_pairs={{0,6},{1,7},{2,0},{3,1},{4,2},{5,3},{6,4},{7,5},{8,14},{9,15},{10,... | collective-permute-start | bytes 393224 | tf_op jit(solution)/shard_map/ppermute | solution.py:205
  45.3 14.5 %collective-permute-start.6 = (bf16[16,16,256]{2,1,0:T(8,128)(2,1)S(1)}, bf16[16,16,256]{2,1,0:T(8,128)(2,1)S(1)}, u32[]{:S(2)}, u32[]{:S(2)}) collective-permute-start(bf16[16,16,256]{2,1,0:T(8,128)(2,1)S(1)} %get-tuple-element.20), channel_id=1, source_target_pairs={{0,7},{1,0},{2,1},{3,2},{4,3},{5,4},{6,5},{7,6},{8,15},{9,8},{10,9... | collective-permute-start | bytes 393224 | tf_op jit(solution)/shard_map/ppermute | solution.py:205
  61.6 6.2 %copy-start.4 = (bf16[128,128]{1,0:T(8,128)(2,1)S(1)}, bf16[128,128]{1,0:T(8,128)(2,1)}, u32[]{:S(2)}) copy-start(bf16[128,128]{1,0:T(8,128)(2,1)} %proj_ref.4) | copy-start | bytes 98308
  61.6 20.6 %all-to-all-start.1 = ((bf16[8,16,16,256]{3,2,1,0:T(8,128)(2,1)}), bf16[8,16,16,256]{3,2,1,0:T(8,128)(2,1)S(1)}, u32[]{:S(2)}, u32[]{:S(2)}) async-start(bf16[8,16,16,256]{3,2,1,0:T(8,128)(2,1)} %shard_map.66), calls=%async_computation.1 | async-start | bytes 2097152 | tf_op jit(solution)/shard_map/all_to_all | solution.py:216
  67.8 1.2 %copy-start.2 = (bf16[16,256,128]{2,1,0:T(8,128)(2,1)S(1)}, bf16[16,256,128]{2,1,0:T(8,128)(2,1)}, u32[]{:S(2)}) copy-start(bf16[16,256,128]{2,1,0:T(8,128)(2,1)} %pair_ref.3) | copy-start | bytes 3145732
  69.0 13.2 %copy-start = (bf16[128,128]{1,0:T(8,128)(2,1)S(1)}, bf16[128,128]{1,0:T(8,128)(2,1)}, u32[]{:S(2)}) copy-start(bf16[128,128]{1,0:T(8,128)(2,1)} %proj_ref.5) | copy-start | bytes 98308

commit v3 on v2

--- a/solution.py
+++ b/solution.py
@@ -12,6 +12,10 @@
 SMEM = pl.BlockSpec(memory_space=pltpu.SMEM)
 ANY = pl.BlockSpec(memory_space=pl.ANY)
 OVER_LAST = (((1,), (1,)), ((), ()))
+
+
+def steps_of(blocks):
+    return (0, 1, 6, 2, 4, 7, 3, 5) if blocks == 8 else tuple(range(blocks))
 
 
 def sigmoid(x):
@@ -94,25 +98,36 @@
     blocks = len(out_refs)
     group, rows, tokens = out_refs[0].shape
     operand(pair_ref, mask_ref, gain_ref, proj_ref, total, 0)
-    for s, out_ref in enumerate(out_refs):
-        b = lax.rem(me_ref[0] + s, blocks)
+    for step, out_ref in zip(steps_of(blocks), out_refs):
+        b = me_ref[0] ^ step
         for t in range(tokens // 128):
             block = total[t, pl.ds(pl.multiple_of(b * group * rows, group * rows), group * rows), :]
             out_ref[:, :, t * 128 : (t + 1) * 128] = block.astype(jnp.bfloat16).reshape(group, rows, 128)
 
 
-def cross_kernel(me_ref, right_ref, *rest):
-    *left_refs, out_ref = rest
-    blocks = len(left_refs)
+def cross_kernel(right_hbm, *rest):
+    *refs, right_ref, sems = rest
+    blocks = len(refs) // 2
+    left_refs, out_refs = refs[:blocks], refs[blocks:]
     sources, group, rows, tokens = right_ref.shape
+    parts = sems.shape[0]
+    loads = []
+    for part in range(parts):
+        channels = pl.ds(part * (group // parts), group // parts)
+        load = pltpu.make_async_copy(
+            right_hbm.at[:, channels], right_ref.at[:, channels], sems.at[part]
+        )
+        load.start()
+        loads.append(load)
     for c in range(group):
+        if c % (group // parts) == 0:
+            loads[c // (group // parts)].wait()
         right = right_ref[:, c].reshape(sources * rows, tokens)
         left = jnp.concatenate([ref[c] for ref in left_refs], axis=0)
         crossed = lax.dot_general(left, right, OVER_LAST, preferred_element_type=jnp.float32)
         crossed = crossed.astype(jnp.bfloat16).reshape(blocks, rows, sources * rows)
-        for s in range(blocks):
-            owner = lax.rem(me_ref[0] + blocks - s, blocks)
-            out_ref[owner, c] = crossed[s]
+        for s, out_ref in enumerate(out_refs):
+            out_ref[c] = crossed[s]
 
 
 def gate_kernel(pair_ref, gain_ref, proj_ref, out_ref):
@@ -128,16 +143,23 @@
     lax.fori_loop(0, rows, step, 0, unroll=4)
 
 
-def final_kernel(crossed_ref, gate_ref, proj_ref, out_hbm, total, staged, sems):
-    hidden, rows, tokens = crossed_ref.shape
+def final_kernel(me_ref, gate_ref, proj_ref, *rest):
+    *crossed_refs, out_hbm, total, staged, sems = rest
+    group, rows, tokens = crossed_refs[0].shape
+    hidden = group * len(crossed_refs)
     weights = proj_ref[...]
     stores = []
     for t in range(tokens // 128):
         lanes = slice(t * 128, (t + 1) * 128)
-        x = crossed_ref[:, :, lanes].astype(jnp.float32)
+        x = jnp.concatenate([ref[:, :, lanes] for ref in crossed_refs], axis=0)
+        x = x.astype(jnp.float32)
         centered = x - jnp.mean(x, axis=0, keepdims=True)
         variance = jnp.mean(centered * centered, axis=0, keepdims=True)
-        total[t] = (centered * lax.rsqrt(variance + EPS)).reshape(hidden * rows, 128)
+        x = (centered * lax.rsqrt(variance + EPS)).reshape(len(crossed_refs), group * rows, 128)
+        for s, step in enumerate(steps_of(len(crossed_refs))):
+            owner = me_ref[0] ^ step
+            first = pl.multiple_of(owner * (group * rows), group * rows)
+            total[t, pl.ds(first, group * rows), :] = x[s]
         for r in range(rows):
             x = total[t, pl.ds(r, hidden, stride=rows), :].T.astype(jnp.bfloat16)
             mixed = jnp.dot(x, weights, preferred_element_type=jnp.float32)
@@ -150,19 +172,29 @@
         store.wait()
 
 
-def call(kernel, out_shape, operands, scratch=(), cost=1.0, in_hbm=False, out_hbm=False):
-    specs = [ANY for _ in operands] if in_hbm else [SMEM if x.dtype == jnp.int32 and x.ndim == 1 else VMEM for x in operands]
+def call(kernel, out_shape, operands, scratch=(), in_hbm=(), out_hbm=False, limit=48, cost=1.0):
+    specs = [
+        ANY if i in in_hbm else SMEM if x.ndim == 1 else VMEM
+        for i, x in enumerate(operands)
+    ]
     return pl.pallas_call(
         kernel,
         out_shape=out_shape,
         in_specs=specs,
         out_specs=jax.tree.map(lambda _: ANY if out_hbm else VMEM, out_shape),
         scratch_shapes=list(scratch),
-        compiler_params=pltpu.CompilerParams(vmem_limit_bytes=(62 if in_hbm else 48) * 2**20),
+        compiler_params=pltpu.CompilerParams(vmem_limit_bytes=limit * 2**20),
         cost_estimate=pl.CostEstimate(
             flops=int(cost * 1e9), bytes_accessed=int(cost * 4e6), transcendentals=0
         ),
     )(*operands)
+
+
+def exchange(parts, devices):
+    return [
+        lax.ppermute(part, "row", [(i, i ^ step) for i in range(devices)]) if step else part
+        for part, step in zip(parts, steps_of(len(parts)))
+    ]
 
 
 def on_device(devices, pair, pair_mask, in_gain, in_proj, gate_proj, out_proj):
@@ -190,37 +222,35 @@
             pltpu.SemaphoreType.DMA((4,)),
             pltpu.SemaphoreType.DMA((2, blocks)),
         ),
-        in_hbm=True,
+        in_hbm=range(4),
         out_hbm=True,
+        limit=62,
     ).reshape(devices, group, rows, tokens)
     right = lax.all_to_all(right, "row", split_axis=0, concat_axis=0, tiled=True)
+    right = pltpu.with_memory_space_constraint(right, pltpu.HBM)
     lefts = call(
         left_kernel,
         tuple(sds((group, rows, tokens), bf16) for _ in range(blocks)),
         (me, pair, pair_mask, gain, in_proj),
         (total,),
     )
-    halves = (range(blocks), range(blocks, devices))
-    lefts = [lefts[0]] + [
-        lax.ppermute(
-            lefts[s],
-            "row",
-            [(h[i], h[(i + s) % blocks]) for h in halves for i in range(blocks)],
-        )
-        for s in range(1, blocks)
-    ]
+    lefts = exchange(lefts, devices)
     gate = call(gate_kernel, sds((rows, tokens, width), jnp.float32), (pair, gain, gate_proj))
     crossed = call(
-        cross_kernel, sds((blocks, group, rows, devices * rows), bf16), (me, right, *lefts)
-    )
-    crossed = lax.all_to_all(
-        crossed, "row", split_axis=0, concat_axis=0, tiled=True,
-        axis_index_groups=[list(h) for h in halves],
-    ).reshape(hidden, rows, tokens)
+        cross_kernel,
+        tuple(sds((group, rows, devices * rows), bf16) for _ in range(blocks)),
+        (right, *lefts),
+        (
+            pltpu.VMEM(right.shape, bf16),
+            pltpu.SemaphoreType.DMA((4 if group % 4 == 0 else 1,)),
+        ),
+        in_hbm=(0,),
+    )
+    crossed = exchange(crossed, devices)
     return call(
         final_kernel,
         sds((rows, tokens, width), bf16),
-        (crossed, gate, out_proj),
+        (me, gate, out_proj, *crossed),
         (
             total,
             pltpu.VMEM((rows, tokens, width), bf16),

time: 85.1 us -> 81.5 us (0.958)
  waiting for transfers between devices: 49.1 us -> 42.6 us
  starting transfers between devices: 19.9 us -> 23.8 us
  local copies, waits for them, and re-layouts: 1.25 us -> 0.04 us
    all_to_all x1 -> x0, waiting for transfers between devices: 11.3 us -> none  [on_device(): lax.all_to_all(crossed, 'row', split_axis=0, concat_axis=0, tiled=True, a...]
    ppermute x7 -> x14, starting transfers between devices: 6.18 us -> 16.2 us  [exchange(): lax.ppermute(part, 'row', [(i, i ^ step) for i in range(devices)])]
    all_to_all x1 -> x0, starting transfers between devices: 6.15 us -> none  [on_device(): lax.all_to_all(crossed, 'row', split_axis=0, concat_axis=0, tiled=True, a...]
    ppermute x7 -> x14, waiting for transfers between devices: 37.8 us -> 42.6 us  [exchange(): lax.ppermute(part, 'row', [(i, i ^ step) for i in range(devices)])]
    unnamed x14 -> x12, local copies, waits for them, and re-layouts: 1.25 us -> 0.04 us
  transfers between devices with their start and end apart: 9 -> 15, of which waited for: 7 -> 8; matrix products, arithmetic and copies ran while one was open for 0% -> 0% of each run, Pallas kernels for 6% -> 6%
where the time goes in v3:
time: 81.5 us; the launch traced here: 81.3 us
  waiting for transfers between devices  42.6 us (52%)
  starting transfers between devices  23.8 us (29%)
  Pallas kernels  14.8 us (18%)
    ppermute x14, waiting for transfers between devices, exchange(): lax.ppermute(part, 'row', [(i, i ^ step) for i in range(devices)])  42.6 us
    ppermute x14, starting transfers between devices, exchange(): lax.ppermute(part, 'row', [(i, i ^ step) for i in range(devices)])  16.2 us
    pallas_call x5, Pallas kernels, call(): pl.pallas_call(kernel, out_shape=out_shape, in_specs=specs, out_specs=jax...  14.8 us
    all_to_all x1, starting transfers between devices, on_device(): lax.all_to_all(right, 'row', split_axis=0, concat_axis=0, tiled=True)  7.58 us
  transfers between devices with their start and end apart: 15, of which 8 were waited for; matrix products, arithmetic and copies ran while one was open for 0% of the time, Pallas kernels for 6%

profile of v3, /device:TPU:0, one launch (start us, length us, event | category | flops | bytes accessed | tf_op | source)
XLA Modules:
  0.0 81.3 jit_solution(96559064998203998)
XLA Ops:
  0.0 5.0 %shard_map.65 = bf16[2,8,16,16,256]{4,3,2,1,0:T(8,128)(2,1)} custom-call(bf16[16,256,128]{2,1,0:T(8,128)(2,1)} %pair_ref.3, s32[16,256]{1,0:T(8,128)} %mask_ref.1, f32[1,128]{1,0:T(1,128)} %bitcast.3, bf16[128,512]{1,0:T(8,128)(2,1)} %proj_ref.4), custom_call_target="tpu_custom_call" | custom-call | flops 1000000000 | bytes 4000000 | tf_op jit(solution)/shard_map/pallas_call | solution.py:180
  5.0 0.0 copy-start.1
  5.0 0.0 copy-start.2
  5.0 0.0 copy-start.4
  5.0 0.0 copy-start.5
  5.0 7.6 %all-to-all-start = ((bf16[16,16,16,256]{3,2,1,0:T(8,128)(2,1)}), bf16[16,16,16,256]{3,2,1,0:T(8,128)(2,1)}, u32[]{:S(2)}, u32[]{:S(2)}) async-start(bf16[16,16,16,256]{3,2,1,0:T(8,128)(2,1)} %bitcast.6), calls=%async_computation | async-start | bytes 4194304 | tf_op jit(solution)/shard_map/all_to_all | solution.py:229
  12.6 0.0 copy-done.1
  12.6 0.0 copy-done.2
  12.7 0.0 copy-done.4
  12.7 0.0 copy-done.5
  12.7 3.2 %shard_map.66 = (bf16[16,16,256]{2,1,0:T(8,128)(2,1)S(1)}, bf16[16,16,256]{2,1,0:T(8,128)(2,1)S(1)}, bf16[16,16,256]{2,1,0:T(8,128)(2,1)S(1)}, bf16[16,16,256]{2...) custom-call(s32[1]{0:T(128)} %bitcast.me_ref, ...), custom_call_target="tpu_custom_call" | custom-call | flops 1000000000 | bytes 4000000 | tf_op jit(solution)/shard_map/pallas_call | solution.py:180
  15.8 0.0 copy-start.3
  15.8 0.4 collective-permute-start
  16.3 2.6 %collective-permute-start.1 = (bf16[16,16,256]{2,1,0:T(8,128)(2,1)S(1)}, bf16[16,16,256]{2,1,0:T(8,128)(2,1)S(1)}, u32[]{:S(2)}, u32[]{:S(2)}) collective-permute-start(bf16[16,16,256]{2,1,0:T(8,128)(2,1)S(1)} %get-tuple-element.23), channel_id=1, source_target_pairs={{0,6},{1,7},{2,4},{3,5},{4,2},{5,3},{6,0},{7,1},{8,14},{9,15},{10,... | collective-permute-start | bytes 393224 | tf_op jit(solution)/shard_map/ppermute | solution.py:195
  18.8 0.6 collective-permute-start.2
  19.4 0.3 collective-permute-start.3
  19.8 1.7 %collective-permute-start.4 = (bf16[16,16,256]{2,1,0:T(8,128)(2,1)S(1)}, bf16[16,16,256]{2,1,0:T(8,128)(2,1)S(1)}, u32[]{:S(2)}, u32[]{:S(2)}) collective-permute-start(bf16[16,16,256]{2,1,0:T(8,128)(2,1)S(1)} %get-tuple-element.26), channel_id=1, source_target_pairs={{0,7},{1,6},{2,5},{3,4},{4,3},{5,2},{6,1},{7,0},{8,15},{9,14},{10,... | collective-permute-start | bytes 393224 | tf_op jit(solution)/shard_map/ppermute | solution.py:195
  21.4 0.0 collective-permute-done.rest_1_
  21.4 1.2 %collective-permute-start.5 = (bf16[16,16,256]{2,1,0:T(8,128)(2,1)S(1)}, bf16[16,16,256]{2,1,0:T(8,128)(2,1)S(1)}, u32[]{:S(2)}, u32[]{:S(2)}) collective-permute-start(bf16[16,16,256]{2,1,0:T(8,128)(2,1)S(1)} %get-tuple-element.27), channel_id=1, source_target_pairs={{0,3},{1,2},{2,1},{3,0},{4,7},{5,6},{6,5},{7,4},{8,11},{9,10},{10,... | collective-permute-start | bytes 393224 | tf_op jit(solution)/shard_map/ppermute | solution.py:195
  22.6 28.8 %collective-permute-done.1.rest_2_ = bf16[16,16,256]{2,1,0:T(8,128)(2,1)S(1)} collective-permute-done((bf16[16,16,256]{2,1,0:T(8,128)(2,1)S(1)}, bf16[16,16,256]{2,1,0:T(8,128)(2,1)S(1)}, u32[]{:S(2)}, u32[]{:S(2)}) %collective-permute-start.1) | collective-permute-done | bytes 131104 | tf_op jit(solution)/shard_map/ppermute | solution.py:195
  51.4 2.1 %collective-permute-start.6 = (bf16[16,16,256]{2,1,0:T(8,128)(2,1)S(1)}, bf16[16,16,256]{2,1,0:T(8,128)(2,1)S(1)}, u32[]{:S(2)}, u32[]{:S(2)}) collective-permute-start(bf16[16,16,256]{2,1,0:T(8,128)(2,1)S(1)} %get-tuple-element.28), channel_id=1, source_target_pairs={{0,5},{1,4},{2,7},{3,6},{4,1},{5,0},{6,3},{7,2},{8,13},{9,12},{10,... | collective-permute-start | bytes 393224 | tf_op jit(solution)/shard_map/ppermute | solution.py:195
  53.5 0.0 collective-permute-done.2.rest_3_
  53.5 0.8 collective-permute-done.3.rest_4_
  54.2 4.2 %collective-permute-done.4.rest_5_ = bf16[16,16,256]{2,1,0:T(8,128)(2,1)S(1)} collective-permute-done((bf16[16,16,256]{2,1,0:T(8,128)(2,1)S(1)}, bf16[16,16,256]{2,1,0:T(8,128)(2,1)S(1)}, u32[]{:S(2)}, u32[]{:S(2)}) %collective-permute-start.4) | collective-permute-done | bytes 131104 | tf_op jit(solution)/shard_map/ppermute | solution.py:195
  58.4 0.0 collective-permute-done.5.rest_6_
  58.4 1.8 %collective-permute-done.6.rest_7_ = bf16[16,16,256]{2,1,0:T(8,128)(2,1)S(1)} collective-permute-done((bf16[16,16,256]{2,1,0:T(8,128)(2,1)S(1)}, bf16[16,16,256]{2,1,0:T(8,128)(2,1)S(1)}, u32[]{:S(2)}, u32[]{:S(2)}) %collective-permute-start.6) | collective-permute-done | bytes 131104 | tf_op jit(solution)/shard_map/ppermute | solution.py:195
  60.2 0.0 all-to-all-done.right_hbm
  60.2 2.3 %shard_map.67 = (bf16[16,16,256]{2,1,0:T(8,128)(2,1)S(1)}, bf16[16,16,256]{2,1,0:T(8,128)(2,1)S(1)}, bf16[16,16,256]{2,1,0:T(8,128)(2,1)S(1)}, bf16[16,16,256]{2...) custom-call(bf16[16,16,16,256]{3,2,1,0:T(8,128)(2,1)} %all-to-all-do, ...), custom_call_target="tpu_custom_call" | custom-call | flops 1000000000 | bytes 4000000 | tf_op jit(solution)/shard_map/pallas_call | solution.py:180
  62.5 0.0 copy-start
  62.5 0.4 collective-permute-start.7
  62.9 3.8 %collective-permute-start.8 = (bf16[16,16,256]{2,1,0:T(8,128)(2,1)S(1)}, bf16[16,16,256]{2,1,0:T(8,128)(2,1)S(1)}, u32[]{:S(2)}, u32[]{:S(2)}) collective-permute-start(bf16[16,16,256]{2,1,0:T(8,128)(2,1)S(1)} %get-tuple-element.31), channel_id=1, source_target_pairs={{0,6},{1,7},{2,4},{3,5},{4,2},{5,3},{6,0},{7,1},{8,14},{9,15},{10,... | collective-permute-start | bytes 393224 | tf_op jit(solution)/shard_map/ppermute | solution.py:195
  66.7 0.0 collective-permute-start.9
  66.7 0.6 collective-permute-start.10
  67.3 1.9 %collective-permute-start.11 = (bf16[16,16,256]{2,1,0:T(8,128)(2,1)S(1)}, bf16[16,16,256]{2,1,0:T(8,128)(2,1)S(1)}, u32[]{:S(2)}, u32[]{:S(2)}) collective-permute-start(bf16[16,16,256]{2,1,0:T(8,128)(2,1)S(1)} %get-tuple-element.34), channel_id=1, source_target_pairs={{0,7},{1,6},{2,5},{3,4},{4,3},{5,2},{6,1},{7,0},{8,15},{9,14},{10,... | collective-permute-start | bytes 393224 | tf_op jit(solution)/shard_map/ppermute | solution.py:195
  69.2 0.0 collective-permute-done.7.rest_1_
  69.2 0.7 collective-permute-start.12
  69.9 0.8 collective-permute-done.8.rest_2_
  70.7 0.0 collective-permute-start.13
  70.7 0.0 copy-done.3
  70.7 1.9 %shard_map.64.gate_ref = f32[16,256,128]{2,1,0:T(8,128)S(1)} custom-call(bf16[16,256,128]{2,1,0:T(8,128)(2,1)S(1)} %copy-done.1, f32[1,128]{1,0:T(1,128)S(1)} %bitcast.5, bf16[128,128]{1,0:T(8,128)(2,1)S(1)} %copy-done.3), custom_call_target="tpu_custom_call" | custom-call | flops 1000000000 | bytes 4000000 | tf_op jit(solution)/shard_map/pallas_call | solution.py:180
  72.6 2.0 %collective-permute-done.9.rest_3_ = bf16[16,16,256]{2,1,0:T(8,128)(2,1)S(1)} collective-permute-done((bf16[16,16,256]{2,1,0:T(8,128)(2,1)S(1)}, bf16[16,16,256]{2,1,0:T(8,128)(2,1)S(1)}, u32[]{:S(2)}, u32[]{:S(2)}) %collective-permute-start.9) | collective-permute-done | bytes 131104 | tf_op jit(solution)/shard_map/ppermute | solution.py:195
  74.7 0.0 collective-permute-done.10.rest_4_
  74.7 1.6 %collective-permute-done.11.rest_5_ = bf16[16,16,256]{2,1,0:T(8,128)(2,1)S(1)} collective-permute-done((bf16[16,16,256]{2,1,0:T(8,128)(2,1)S(1)}, bf16[16,16,256]{2,1,0:T(8,128)(2,1)S(1)}, u32[]{:S(2)}, u32[]{:S(2)}) %collective-permute-start.11) | collective-permute-done | bytes 131104 | tf_op jit(solution)/shard_map/ppermute | solution.py:195
  76.2 2.6 %collective-permute-done.12.rest_6_ = bf16[16,16,256]{2,1,0:T(8,128)(2,1)S(1)} collective-permute-done((bf16[16,16,256]{2,1,0:T(8,128)(2,1)S(1)}, bf16[16,16,256]{2,1,0:T(8,128)(2,1)S(1)}, u32[]{:S(2)}, u32[]{:S(2)}) %collective-permute-start.12) | collective-permute-done | bytes 131104 | tf_op jit(solution)/shard_map/ppermute | solution.py:195
  78.9 0.0 collective-permute-done.13.rest_7_
  78.9 0.0 copy-done
  78.9 2.4 %shard_map.68 = bf16[16,256,128]{2,1,0:T(8,128)(2,1)} custom-call(s32[1]{0:T(128)} %bitcast.me_ref, f32[16,256,128]{2,1,0:T(8,128)S(1)} %shard_map.64.gate_ref, bf16[128,128]{1,0:T(8,128)(2,1)S(1)} %copy-done, bf16[16,16,256]{2,1,0:T(8,128)(2,1)S(1)} %get-tuple-element.29.rest_0_, bf16[16,16,256]{2,1,0:T(8,128)(2,1)S(1)} %collective-permute-done.7.rest_1_, ...), custom_call_target="tpu_custom_call" | custom-call | flops 1000000000 | bytes 4000000 | tf_op jit(solution)/shard_map/pallas_call | solution.py:180
Async XLA Ops:
  5.0 7.6 %copy-start.1 = (bf16[16,256,128]{2,1,0:T(8,128)(2,1)S(1)}, bf16[16,256,128]{2,1,0:T(8,128)(2,1)}, u32[]{:S(2)}) copy-start(bf16[16,256,128]{2,1,0:T(8,128)(2,1)} %pair_ref.3) | copy-start | bytes 3145732
  5.0 7.6 %copy-start.2 = (bf16[128,512]{1,0:T(8,128)(2,1)S(1)}, bf16[128,512]{1,0:T(8,128)(2,1)}, u32[]{:S(2)}) copy-start(bf16[128,512]{1,0:T(8,128)(2,1)} %proj_ref.4) | copy-start | bytes 393220
  5.0 7.6 %copy-start.4 = (s32[16,256]{1,0:T(8,128)S(1)}, s32[16,256]{1,0:T(8,128)}, u32[]{:S(2)}) copy-start(s32[16,256]{1,0:T(8,128)} %mask_ref.1) | copy-start | bytes 49156
  5.0 7.6 %copy-start.5 = (f32[128]{0:T(128)S(1)}, f32[128]{0:T(128)}, u32[]{:S(2)}) copy-start(f32[128]{0:T(128)} %param.8) | copy-start | bytes 1540
  5.0 55.2 %all-to-all-start = ((bf16[16,16,16,256]{3,2,1,0:T(8,128)(2,1)}), bf16[16,16,16,256]{3,2,1,0:T(8,128)(2,1)}, u32[]{:S(2)}, u32[]{:S(2)}) async-start(bf16[16,16,16,256]{3,2,1,0:T(8,128)(2,1)} %bitcast.6), calls=%async_computation | async-start | bytes 4194304 | tf_op jit(solution)/shard_map/all_to_all | solution.py:229
  15.8 54.8 %copy-start.3 = (bf16[128,128]{1,0:T(8,128)(2,1)S(1)}, bf16[128,128]{1,0:T(8,128)(2,1)}, u32[]{:S(2)}) copy-start(bf16[128,128]{1,0:T(8,128)(2,1)} %proj_ref.3) | copy-start | bytes 98308
  15.8 5.6 %collective-permute-start = (bf16[16,16,256]{2,1,0:T(8,128)(2,1)S(1)}, bf16[16,16,256]{2,1,0:T(8,128)(2,1)S(1)}, u32[]{:S(2)}, u32[]{:S(2)}) collective-permute-start(bf16[16,16,256]{2,1,0:T(8,128)(2,1)S(1)} %get-tuple-element.22), channel_id=1, source_target_pairs={{0,1},{1,0},{2,3},{3,2},{4,5},{5,4},{6,7},{7,6},{8,9},{9,8},{10,11... | collective-permute-start | bytes 393224 | tf_op jit(solution)/shard_map/ppermute | solution.py:195
  16.3 35.2 %collective-permute-start.1 = (bf16[16,16,256]{2,1,0:T(8,128)(2,1)S(1)}, bf16[16,16,256]{2,1,0:T(8,128)(2,1)S(1)}, u32[]{:S(2)}, u32[]{:S(2)}) collective-permute-start(bf16[16,16,256]{2,1,0:T(8,128)(2,1)S(1)} %get-tuple-element.23), channel_id=1, source_target_pairs={{0,6},{1,7},{2,4},{3,5},{4,2},{5,3},{6,0},{7,1},{8,14},{9,15},{10,... | collective-permute-start | bytes 393224 | tf_op jit(solution)/shard_map/ppermute | solution.py:195
  18.8 34.6 %collective-permute-start.2 = (bf16[16,16,256]{2,1,0:T(8,128)(2,1)S(1)}, bf16[16,16,256]{2,1,0:T(8,128)(2,1)S(1)}, u32[]{:S(2)}, u32[]{:S(2)}) collective-permute-start(bf16[16,16,256]{2,1,0:T(8,128)(2,1)S(1)} %get-tuple-element.24), channel_id=1, source_target_pairs={{0,2},{1,3},{2,0},{3,1},{4,6},{5,7},{6,4},{7,5},{8,10},{9,11},{10,... | collective-permute-start | bytes 393224 | tf_op jit(solution)/shard_map/ppermute | solution.py:195
  19.4 34.8 %collective-permute-start.3 = (bf16[16,16,256]{2,1,0:T(8,128)(2,1)S(1)}, bf16[16,16,256]{2,1,0:T(8,128)(2,1)S(1)}, u32[]{:S(2)}, u32[]{:S(2)}) collective-permute-start(bf16[16,16,256]{2,1,0:T(8,128)(2,1)S(1)} %get-tuple-element.25), channel_id=1, source_target_pairs={{0,4},{1,5},{2,6},{3,7},{4,0},{5,1},{6,2},{7,3},{8,12},{9,13},{10,... | collective-permute-start | bytes 393224 | tf_op jit(solution)/shard_map/ppermute | solution.py:195
  19.8 38.6 %collective-permute-start.4 = (bf16[16,16,256]{2,1,0:T(8,128)(2,1)S(1)}, bf16[16,16,256]{2,1,0:T(8,128)(2,1)S(1)}, u32[]{:S(2)}, u32[]{:S(2)}) collective-permute-start(bf16[16,16,256]{2,1,0:T(8,128)(2,1)S(1)} %get-tuple-element.26), channel_id=1, source_target_pairs={{0,7},{1,6},{2,5},{3,4},{4,3},{5,2},{6,1},{7,0},{8,15},{9,14},{10,... | collective-permute-start | bytes 393224 | tf_op jit(solution)/shard_map/ppermute | solution.py:195
  21.4 37.0 %collective-permute-start.5 = (bf16[16,16,256]{2,1,0:T(8,128)(2,1)S(1)}, bf16[16,16,256]{2,1,0:T(8,128)(2,1)S(1)}, u32[]{:S(2)}, u32[]{:S(2)}) collective-permute-start(bf16[16,16,256]{2,1,0:T(8,128)(2,1)S(1)} %get-tuple-element.27), channel_id=1, source_target_pairs={{0,3},{1,2},{2,1},{3,0},{4,7},{5,6},{6,5},{7,4},{8,11},{9,10},{10,... | collective-permute-start | bytes 393224 | tf_op jit(solution)/shard_map/ppermute | solution.py:195
  51.4 8.8 %collective-permute-start.6 = (bf16[16,16,256]{2,1,0:T(8,128)(2,1)S(1)}, bf16[16,16,256]{2,1,0:T(8,128)(2,1)S(1)}, u32[]{:S(2)}, u32[]{:S(2)}) collective-permute-start(bf16[16,16,256]{2,1,0:T(8,128)(2,1)S(1)} %get-tuple-element.28), channel_id=1, source_target_pairs={{0,5},{1,4},{2,7},{3,6},{4,1},{5,0},{6,3},{7,2},{8,13},{9,12},{10,... | collective-permute-start | bytes 393224 | tf_op jit(solution)/shard_map/ppermute | solution.py:195
  62.5 16.4 %copy-start = (bf16[128,128]{1,0:T(8,128)(2,1)S(1)}, bf16[128,128]{1,0:T(8,128)(2,1)}, u32[]{:S(2)}) copy-start(bf16[128,128]{1,0:T(8,128)(2,1)} %proj_ref.5) | copy-start | bytes 98308
  62.5 6.6 %collective-permute-start.7 = (bf16[16,16,256]{2,1,0:T(8,128)(2,1)S(1)}, bf16[16,16,256]{2,1,0:T(8,128)(2,1)S(1)}, u32[]{:S(2)}, u32[]{:S(2)}) collective-permute-start(bf16[16,16,256]{2,1,0:T(8,128)(2,1)S(1)} %get-tuple-element.30), channel_id=1, source_target_pairs={{0,1},{1,0},{2,3},{3,2},{4,5},{5,4},{6,7},{7,6},{8,9},{9,8},{10,11... | collective-permute-start | bytes 393224 | tf_op jit(solution)/shard_map/ppermute | solution.py:195
  62.9 7.8 %collective-permute-start.8 = (bf16[16,16,256]{2,1,0:T(8,128)(2,1)S(1)}, bf16[16,16,256]{2,1,0:T(8,128)(2,1)S(1)}, u32[]{:S(2)}, u32[]{:S(2)}) collective-permute-start(bf16[16,16,256]{2,1,0:T(8,128)(2,1)S(1)} %get-tuple-element.31), channel_id=1, source_target_pairs={{0,6},{1,7},{2,4},{3,5},{4,2},{5,3},{6,0},{7,1},{8,14},{9,15},{10,... | collective-permute-start | bytes 393224 | tf_op jit(solution)/shard_map/ppermute | solution.py:195
  66.7 8.0 %collective-permute-start.9 = (bf16[16,16,256]{2,1,0:T(8,128)(2,1)S(1)}, bf16[16,16,256]{2,1,0:T(8,128)(2,1)S(1)}, u32[]{:S(2)}, u32[]{:S(2)}) collective-permute-start(bf16[16,16,256]{2,1,0:T(8,128)(2,1)S(1)} %get-tuple-element.32), channel_id=1, source_target_pairs={{0,2},{1,3},{2,0},{3,1},{4,6},{5,7},{6,4},{7,5},{8,10},{9,11},{10,... | collective-permute-start | bytes 393224 | tf_op jit(solution)/shard_map/ppermute | solution.py:195
  66.7 8.0 %collective-permute-start.10 = (bf16[16,16,256]{2,1,0:T(8,128)(2,1)S(1)}, bf16[16,16,256]{2,1,0:T(8,128)(2,1)S(1)}, u32[]{:S(2)}, u32[]{:S(2)}) collective-permute-start(bf16[16,16,256]{2,1,0:T(8,128)(2,1)S(1)} %get-tuple-element.33), channel_id=1, source_target_pairs={{0,4},{1,5},{2,6},{3,7},{4,0},{5,1},{6,2},{7,3},{8,12},{9,13},{10,... | collective-permute-start | bytes 393224 | tf_op jit(solution)/shard_map/ppermute | solution.py:195
  67.3 9.0 %collective-permute-start.11 = (bf16[16,16,256]{2,1,0:T(8,128)(2,1)S(1)}, bf16[16,16,256]{2,1,0:T(8,128)(2,1)S(1)}, u32[]{:S(2)}, u32[]{:S(2)}) collective-permute-start(bf16[16,16,256]{2,1,0:T(8,128)(2,1)S(1)} %get-tuple-element.34), channel_id=1, source_target_pairs={{0,7},{1,6},{2,5},{3,4},{4,3},{5,2},{6,1},{7,0},{8,15},{9,14},{10,... | collective-permute-start | bytes 393224 | tf_op jit(solution)/shard_map/ppermute | solution.py:195
  69.2 9.7 %collective-permute-start.12 = (bf16[16,16,256]{2,1,0:T(8,128)(2,1)S(1)}, bf16[16,16,256]{2,1,0:T(8,128)(2,1)S(1)}, u32[]{:S(2)}, u32[]{:S(2)}) collective-permute-start(bf16[16,16,256]{2,1,0:T(8,128)(2,1)S(1)} %get-tuple-element.35), channel_id=1, source_target_pairs={{0,3},{1,2},{2,1},{3,0},{4,7},{5,6},{6,5},{7,4},{8,11},{9,10},{10,... | collective-permute-start | bytes 393224 | tf_op jit(solution)/shard_map/ppermute | solution.py:195
  70.7 8.2 %collective-permute-start.13 = (bf16[16,16,256]{2,1,0:T(8,128)(2,1)S(1)}, bf16[16,16,256]{2,1,0:T(8,128)(2,1)S(1)}, u32[]{:S(2)}, u32[]{:S(2)}) collective-permute-start(bf16[16,16,256]{2,1,0:T(8,128)(2,1)S(1)} %get-tuple-element.36), channel_id=1, source_target_pairs={{0,5},{1,4},{2,7},{3,6},{4,1},{5,0},{6,3},{7,2},{8,13},{9,12},{10,... | collective-permute-start | bytes 393224 | tf_op jit(solution)/shard_map/ppermute | solution.py:195

commit v4 on v3

--- a/solution.py
+++ b/solution.py
@@ -105,23 +105,11 @@
             out_ref[:, :, t * 128 : (t + 1) * 128] = block.astype(jnp.bfloat16).reshape(group, rows, 128)
 
 
-def cross_kernel(right_hbm, *rest):
-    *refs, right_ref, sems = rest
-    blocks = len(refs) // 2
-    left_refs, out_refs = refs[:blocks], refs[blocks:]
+def cross_kernel(right_ref, *rest):
+    blocks = len(rest) // 2
+    left_refs, out_refs = rest[:blocks], rest[blocks:]
     sources, group, rows, tokens = right_ref.shape
-    parts = sems.shape[0]
-    loads = []
-    for part in range(parts):
-        channels = pl.ds(part * (group // parts), group // parts)
-        load = pltpu.make_async_copy(
-            right_hbm.at[:, channels], right_ref.at[:, channels], sems.at[part]
-        )
-        load.start()
-        loads.append(load)
     for c in range(group):
-        if c % (group // parts) == 0:
-            loads[c // (group // parts)].wait()
         right = right_ref[:, c].reshape(sources * rows, tokens)
         left = jnp.concatenate([ref[c] for ref in left_refs], axis=0)
         crossed = lax.dot_general(left, right, OVER_LAST, preferred_element_type=jnp.float32)
@@ -130,10 +118,13 @@
             out_ref[c] = crossed[s]
 
 
-def gate_kernel(pair_ref, gain_ref, proj_ref, out_ref):
+def gate_kernel(pair_hbm, gain_ref, proj_ref, out_ref, pair_ref, sem):
+    load = pltpu.make_async_copy(pair_hbm, pair_ref, sem)
+    load.start()
     rows = pair_ref.shape[0]
     gain = gain_ref[...]
     weights = proj_ref[...]
+    load.wait()
 
     def step(r, carry):
         normed = normed_rows(pair_ref[r], gain)
@@ -227,7 +218,6 @@
         limit=62,
     ).reshape(devices, group, rows, tokens)
     right = lax.all_to_all(right, "row", split_axis=0, concat_axis=0, tiled=True)
-    right = pltpu.with_memory_space_constraint(right, pltpu.HBM)
     lefts = call(
         left_kernel,
         tuple(sds((group, rows, tokens), bf16) for _ in range(blocks)),
@@ -235,16 +225,17 @@
         (total,),
     )
     lefts = exchange(lefts, devices)
-    gate = call(gate_kernel, sds((rows, tokens, width), jnp.float32), (pair, gain, gate_proj))
+    gate = call(
+        gate_kernel,
+        sds((rows, tokens, width), jnp.float32),
+        (pltpu.with_memory_space_constraint(pair, pltpu.HBM), gain, gate_proj),
+        (pltpu.VMEM(pair.shape, bf16), pltpu.SemaphoreType.DMA),
+        in_hbm=(0,),
+    )
     crossed = call(
         cross_kernel,
         tuple(sds((group, rows, devices * rows), bf16) for _ in range(blocks)),
         (right, *lefts),
-        (
-            pltpu.VMEM(right.shape, bf16),
-            pltpu.SemaphoreType.DMA((4 if group % 4 == 0 else 1,)),
-        ),
-        in_hbm=(0,),
     )
     crossed = exchange(crossed, devices)
     return call(

time: 81.5 us -> 79.9 us (0.980)
  waiting for transfers between devices: 42.6 us -> 41.3 us
    ppermute x14, waiting for transfers between devices: 42.6 us -> 41.3 us  [exchange(): lax.ppermute(part, 'row', [(i, i ^ step) for i in range(devices)])]
  transfers between devices with their start and end apart: 15 -> 15, of which waited for: 8 -> 8; matrix products, arithmetic and copies ran while one was open for 0% -> 0% of each run, Pallas kernels for 6% -> 8%
where the time goes in v4:
time: 79.9 us; the launch traced here: 79.7 us
  waiting for transfers between devices  41.3 us (52%)
  starting transfers between devices  23.7 us (30%)
  Pallas kernels  14.5 us (18%)
    ppermute x14, waiting for transfers between devices, exchange(): lax.ppermute(part, 'row', [(i, i ^ step) for i in range(devices)])  41.3 us
    ppermute x14, starting transfers between devices, exchange(): lax.ppermute(part, 'row', [(i, i ^ step) for i in range(devices)])  16.1 us
    pallas_call x5, Pallas kernels, call(): pl.pallas_call(kernel, out_shape=out_shape, in_specs=specs, out_specs=jax...  14.5 us
    all_to_all x1, starting transfers between devices, on_device(): lax.all_to_all(right, 'row', split_axis=0, concat_axis=0, tiled=True)  7.53 us
  transfers between devices with their start and end apart: 15, of which 8 were waited for; matrix products, arithmetic and copies ran while one was open for 0% of the time, Pallas kernels for 8%

profile of v4, /device:TPU:0, one launch (start us, length us, event | category | flops | bytes accessed | tf_op | source)
XLA Modules:
  0.0 79.7 jit_solution(6688078421329998830)
XLA Ops:
  0.0 5.0 %shard_map.65 = bf16[2,8,16,16,256]{4,3,2,1,0:T(8,128)(2,1)} custom-call(bf16[16,256,128]{2,1,0:T(8,128)(2,1)} %pair_ref.1, s32[16,256]{1,0:T(8,128)} %mask_ref.1, f32[1,128]{1,0:T(1,128)} %bitcast.3, bf16[128,512]{1,0:T(8,128)(2,1)} %proj_ref.4), custom_call_target="tpu_custom_call" | custom-call | flops 1000000000 | bytes 4000000 | tf_op jit(solution)/shard_map/pallas_call | solution.py:171
  5.0 0.0 copy-start.1
  5.0 0.0 copy-start.2
  5.1 0.0 copy-start.4
  5.1 0.0 copy-start.5
  5.1 7.5 %all-to-all-start = ((bf16[16,16,16,256]{3,2,1,0:T(8,128)(2,1)}), bf16[16,16,16,256]{3,2,1,0:T(8,128)(2,1)S(1)}, u32[]{:S(2)}, u32[]{:S(2)}) async-start(bf16[16,16,16,256]{3,2,1,0:T(8,128)(2,1)} %bitcast.6), calls=%async_computation | async-start | bytes 4194304 | tf_op jit(solution)/shard_map/all_to_all | solution.py:220
  12.6 0.0 copy-done.1
  12.6 0.0 copy-done.2
  12.6 0.0 copy-done.4
  12.7 0.0 copy-done.5
  12.7 3.2 %shard_map.66 = (bf16[16,16,256]{2,1,0:T(8,128)(2,1)S(1)}, bf16[16,16,256]{2,1,0:T(8,128)(2,1)S(1)}, bf16[16,16,256]{2,1,0:T(8,128)(2,1)S(1)}, bf16[16,16,256]{2...) custom-call(s32[1]{0:T(128)} %bitcast.me_ref, ...), custom_call_target="tpu_custom_call" | custom-call | flops 1000000000 | bytes 4000000 | tf_op jit(solution)/shard_map/pallas_call | solution.py:171
  15.8 0.0 copy-start.3
  15.8 0.5 collective-permute-start
  16.3 2.6 %collective-permute-start.1 = (bf16[16,16,256]{2,1,0:T(8,128)(2,1)S(1)}, bf16[16,16,256]{2,1,0:T(8,128)(2,1)S(1)}, u32[]{:S(2)}, u32[]{:S(2)}) collective-permute-start(bf16[16,16,256]{2,1,0:T(8,128)(2,1)S(1)} %get-tuple-element.23), channel_id=1, source_target_pairs={{0,6},{1,7},{2,4},{3,5},{4,2},{5,3},{6,0},{7,1},{8,14},{9,15},{10,... | collective-permute-start | bytes 393224 | tf_op jit(solution)/shard_map/ppermute | solution.py:186
  18.9 0.6 collective-permute-start.2
  19.4 0.3 collective-permute-start.3
  19.8 1.7 %collective-permute-start.4 = (bf16[16,16,256]{2,1,0:T(8,128)(2,1)S(1)}, bf16[16,16,256]{2,1,0:T(8,128)(2,1)S(1)}, u32[]{:S(2)}, u32[]{:S(2)}) collective-permute-start(bf16[16,16,256]{2,1,0:T(8,128)(2,1)S(1)} %get-tuple-element.26), channel_id=1, source_target_pairs={{0,7},{1,6},{2,5},{3,4},{4,3},{5,2},{6,1},{7,0},{8,15},{9,14},{10,... | collective-permute-start | bytes 393224 | tf_op jit(solution)/shard_map/ppermute | solution.py:186
  21.5 0.0 collective-permute-done.rest_1_
  21.5 1.2 %collective-permute-start.5 = (bf16[16,16,256]{2,1,0:T(8,128)(2,1)S(1)}, bf16[16,16,256]{2,1,0:T(8,128)(2,1)S(1)}, u32[]{:S(2)}, u32[]{:S(2)}) collective-permute-start(bf16[16,16,256]{2,1,0:T(8,128)(2,1)S(1)} %get-tuple-element.27), channel_id=1, source_target_pairs={{0,3},{1,2},{2,1},{3,0},{4,7},{5,6},{6,5},{7,4},{8,11},{9,10},{10,... | collective-permute-start | bytes 393224 | tf_op jit(solution)/shard_map/ppermute | solution.py:186
  22.7 28.8 %collective-permute-done.1.rest_2_ = bf16[16,16,256]{2,1,0:T(8,128)(2,1)S(1)} collective-permute-done((bf16[16,16,256]{2,1,0:T(8,128)(2,1)S(1)}, bf16[16,16,256]{2,1,0:T(8,128)(2,1)S(1)}, u32[]{:S(2)}, u32[]{:S(2)}) %collective-permute-start.1) | collective-permute-done | bytes 131104 | tf_op jit(solution)/shard_map/ppermute | solution.py:186
  51.5 2.1 %collective-permute-start.6 = (bf16[16,16,256]{2,1,0:T(8,128)(2,1)S(1)}, bf16[16,16,256]{2,1,0:T(8,128)(2,1)S(1)}, u32[]{:S(2)}, u32[]{:S(2)}) collective-permute-start(bf16[16,16,256]{2,1,0:T(8,128)(2,1)S(1)} %get-tuple-element.28), channel_id=1, source_target_pairs={{0,5},{1,4},{2,7},{3,6},{4,1},{5,0},{6,3},{7,2},{8,13},{9,12},{10,... | collective-permute-start | bytes 393224 | tf_op jit(solution)/shard_map/ppermute | solution.py:186
  53.5 0.0 collective-permute-done.2.rest_3_
  53.5 0.8 collective-permute-done.3.rest_4_
  54.3 4.2 %collective-permute-done.4.rest_5_ = bf16[16,16,256]{2,1,0:T(8,128)(2,1)S(1)} collective-permute-done((bf16[16,16,256]{2,1,0:T(8,128)(2,1)S(1)}, bf16[16,16,256]{2,1,0:T(8,128)(2,1)S(1)}, u32[]{:S(2)}, u32[]{:S(2)}) %collective-permute-start.4) | collective-permute-done | bytes 131104 | tf_op jit(solution)/shard_map/ppermute | solution.py:186
  58.4 0.0 collective-permute-done.5.rest_6_
  58.4 1.8 %collective-permute-done.6.rest_7_ = bf16[16,16,256]{2,1,0:T(8,128)(2,1)S(1)} collective-permute-done((bf16[16,16,256]{2,1,0:T(8,128)(2,1)S(1)}, bf16[16,16,256]{2,1,0:T(8,128)(2,1)S(1)}, u32[]{:S(2)}, u32[]{:S(2)}) %collective-permute-start.6) | collective-permute-done | bytes 131104 | tf_op jit(solution)/shard_map/ppermute | solution.py:186
  60.3 0.0 all-to-all-done.right_ref
  60.3 0.8 shard_map.67
  61.1 0.0 copy-start
  61.1 0.4 collective-permute-start.7
  61.4 3.7 %collective-permute-start.8 = (bf16[16,16,256]{2,1,0:T(8,128)(2,1)S(1)}, bf16[16,16,256]{2,1,0:T(8,128)(2,1)S(1)}, u32[]{:S(2)}, u32[]{:S(2)}) collective-permute-start(bf16[16,16,256]{2,1,0:T(8,128)(2,1)S(1)} %get-tuple-element.31), channel_id=1, source_target_pairs={{0,6},{1,7},{2,4},{3,5},{4,2},{5,3},{6,0},{7,1},{8,14},{9,15},{10,... | collective-permute-start | bytes 393224 | tf_op jit(solution)/shard_map/ppermute | solution.py:186
  65.1 0.0 collective-permute-start.9
  65.1 0.6 collective-permute-start.10
  65.7 1.9 %collective-permute-start.11 = (bf16[16,16,256]{2,1,0:T(8,128)(2,1)S(1)}, bf16[16,16,256]{2,1,0:T(8,128)(2,1)S(1)}, u32[]{:S(2)}, u32[]{:S(2)}) collective-permute-start(bf16[16,16,256]{2,1,0:T(8,128)(2,1)S(1)} %get-tuple-element.34), channel_id=1, source_target_pairs={{0,7},{1,6},{2,5},{3,4},{4,3},{5,2},{6,1},{7,0},{8,15},{9,14},{10,... | collective-permute-start | bytes 393224 | tf_op jit(solution)/shard_map/ppermute | solution.py:186
  67.6 0.0 collective-permute-done.7.rest_1_
  67.6 0.7 collective-permute-start.12
  68.3 0.8 collective-permute-done.8.rest_2_
  69.1 0.0 collective-permute-start.13
  69.1 0.0 copy-done.3
  69.1 3.2 %shard_map.64.gate_ref = f32[16,256,128]{2,1,0:T(8,128)S(1)} custom-call(bf16[16,256,128]{2,1,0:T(8,128)(2,1)} %pair_ref.1, f32[1,128]{1,0:T(1,128)S(1)} %bitcast.5, bf16[128,128]{1,0:T(8,128)(2,1)S(1)} %copy-done.3), custom_call_target="tpu_custom_call" | custom-call | flops 1000000000 | bytes 4000000 | tf_op jit(solution)/shard_map/pallas_call | solution.py:171
  72.3 0.8 %collective-permute-done.9.rest_3_ = bf16[16,16,256]{2,1,0:T(8,128)(2,1)S(1)} collective-permute-done((bf16[16,16,256]{2,1,0:T(8,128)(2,1)S(1)}, bf16[16,16,256]{2,1,0:T(8,128)(2,1)S(1)}, u32[]{:S(2)}, u32[]{:S(2)}) %collective-permute-start.9) | collective-permute-done | bytes 131104 | tf_op jit(solution)/shard_map/ppermute | solution.py:186
  73.1 0.0 collective-permute-done.10.rest_4_
  73.1 1.6 %collective-permute-done.11.rest_5_ = bf16[16,16,256]{2,1,0:T(8,128)(2,1)S(1)} collective-permute-done((bf16[16,16,256]{2,1,0:T(8,128)(2,1)S(1)}, bf16[16,16,256]{2,1,0:T(8,128)(2,1)S(1)}, u32[]{:S(2)}, u32[]{:S(2)}) %collective-permute-start.11) | collective-permute-done | bytes 131104 | tf_op jit(solution)/shard_map/ppermute | solution.py:186
  74.7 2.6 %collective-permute-done.12.rest_6_ = bf16[16,16,256]{2,1,0:T(8,128)(2,1)S(1)} collective-permute-done((bf16[16,16,256]{2,1,0:T(8,128)(2,1)S(1)}, bf16[16,16,256]{2,1,0:T(8,128)(2,1)S(1)}, u32[]{:S(2)}, u32[]{:S(2)}) %collective-permute-start.12) | collective-permute-done | bytes 131104 | tf_op jit(solution)/shard_map/ppermute | solution.py:186
  77.3 0.0 collective-permute-done.13.rest_7_
  77.3 0.0 copy-done
  77.3 2.4 %shard_map.68 = bf16[16,256,128]{2,1,0:T(8,128)(2,1)} custom-call(s32[1]{0:T(128)} %bitcast.me_ref, f32[16,256,128]{2,1,0:T(8,128)S(1)} %shard_map.64.gate_ref, bf16[128,128]{1,0:T(8,128)(2,1)S(1)} %copy-done, bf16[16,16,256]{2,1,0:T(8,128)(2,1)S(1)} %get-tuple-element.29.rest_0_, bf16[16,16,256]{2,1,0:T(8,128)(2,1)S(1)} %collective-permute-done.7.rest_1_, ...), custom_call_target="tpu_custom_call" | custom-call | flops 1000000000 | bytes 4000000 | tf_op jit(solution)/shard_map/pallas_call | solution.py:171
Async XLA Ops:
  5.0 7.6 %copy-start.1 = (bf16[16,256,128]{2,1,0:T(8,128)(2,1)S(1)}, bf16[16,256,128]{2,1,0:T(8,128)(2,1)}, u32[]{:S(2)}) copy-start(bf16[16,256,128]{2,1,0:T(8,128)(2,1)} %pair_ref.1) | copy-start | bytes 3145732
  5.0 7.6 %copy-start.2 = (bf16[128,512]{1,0:T(8,128)(2,1)S(1)}, bf16[128,512]{1,0:T(8,128)(2,1)}, u32[]{:S(2)}) copy-start(bf16[128,512]{1,0:T(8,128)(2,1)} %proj_ref.4) | copy-start | bytes 393220
  5.1 7.6 %copy-start.4 = (s32[16,256]{1,0:T(8,128)S(1)}, s32[16,256]{1,0:T(8,128)}, u32[]{:S(2)}) copy-start(s32[16,256]{1,0:T(8,128)} %mask_ref.1) | copy-start | bytes 49156
  5.1 7.6 %copy-start.5 = (f32[128]{0:T(128)S(1)}, f32[128]{0:T(128)}, u32[]{:S(2)}) copy-start(f32[128]{0:T(128)} %param.8) | copy-start | bytes 1540
  5.1 55.2 %all-to-all-start = ((bf16[16,16,16,256]{3,2,1,0:T(8,128)(2,1)}), bf16[16,16,16,256]{3,2,1,0:T(8,128)(2,1)S(1)}, u32[]{:S(2)}, u32[]{:S(2)}) async-start(bf16[16,16,16,256]{3,2,1,0:T(8,128)(2,1)} %bitcast.6), calls=%async_computation | async-start | bytes 4194304 | tf_op jit(solution)/shard_map/all_to_all | solution.py:220
  15.8 53.3 %copy-start.3 = (bf16[128,128]{1,0:T(8,128)(2,1)S(1)}, bf16[128,128]{1,0:T(8,128)(2,1)}, u32[]{:S(2)}) copy-start(bf16[128,128]{1,0:T(8,128)(2,1)} %proj_ref.3) | copy-start | bytes 98308
  15.8 5.7 %collective-permute-start = (bf16[16,16,256]{2,1,0:T(8,128)(2,1)S(1)}, bf16[16,16,256]{2,1,0:T(8,128)(2,1)S(1)}, u32[]{:S(2)}, u32[]{:S(2)}) collective-permute-start(bf16[16,16,256]{2,1,0:T(8,128)(2,1)S(1)} %get-tuple-element.22), channel_id=1, source_target_pairs={{0,1},{1,0},{2,3},{3,2},{4,5},{5,4},{6,7},{7,6},{8,9},{9,8},{10,11... | collective-permute-start | bytes 393224 | tf_op jit(solution)/shard_map/ppermute | solution.py:186
  16.3 35.2 %collective-permute-start.1 = (bf16[16,16,256]{2,1,0:T(8,128)(2,1)S(1)}, bf16[16,16,256]{2,1,0:T(8,128)(2,1)S(1)}, u32[]{:S(2)}, u32[]{:S(2)}) collective-permute-start(bf16[16,16,256]{2,1,0:T(8,128)(2,1)S(1)} %get-tuple-element.23), channel_id=1, source_target_pairs={{0,6},{1,7},{2,4},{3,5},{4,2},{5,3},{6,0},{7,1},{8,14},{9,15},{10,... | collective-permute-start | bytes 393224 | tf_op jit(solution)/shard_map/ppermute | solution.py:186
  18.9 34.6 %collective-permute-start.2 = (bf16[16,16,256]{2,1,0:T(8,128)(2,1)S(1)}, bf16[16,16,256]{2,1,0:T(8,128)(2,1)S(1)}, u32[]{:S(2)}, u32[]{:S(2)}) collective-permute-start(bf16[16,16,256]{2,1,0:T(8,128)(2,1)S(1)} %get-tuple-element.24), channel_id=1, source_target_pairs={{0,2},{1,3},{2,0},{3,1},{4,6},{5,7},{6,4},{7,5},{8,10},{9,11},{10,... | collective-permute-start | bytes 393224 | tf_op jit(solution)/shard_map/ppermute | solution.py:186
  19.4 34.8 %collective-permute-start.3 = (bf16[16,16,256]{2,1,0:T(8,128)(2,1)S(1)}, bf16[16,16,256]{2,1,0:T(8,128)(2,1)S(1)}, u32[]{:S(2)}, u32[]{:S(2)}) collective-permute-start(bf16[16,16,256]{2,1,0:T(8,128)(2,1)S(1)} %get-tuple-element.25), channel_id=1, source_target_pairs={{0,4},{1,5},{2,6},{3,7},{4,0},{5,1},{6,2},{7,3},{8,12},{9,13},{10,... | collective-permute-start | bytes 393224 | tf_op jit(solution)/shard_map/ppermute | solution.py:186
  19.8 38.6 %collective-permute-start.4 = (bf16[16,16,256]{2,1,0:T(8,128)(2,1)S(1)}, bf16[16,16,256]{2,1,0:T(8,128)(2,1)S(1)}, u32[]{:S(2)}, u32[]{:S(2)}) collective-permute-start(bf16[16,16,256]{2,1,0:T(8,128)(2,1)S(1)} %get-tuple-element.26), channel_id=1, source_target_pairs={{0,7},{1,6},{2,5},{3,4},{4,3},{5,2},{6,1},{7,0},{8,15},{9,14},{10,... | collective-permute-start | bytes 393224 | tf_op jit(solution)/shard_map/ppermute | solution.py:186
  21.5 37.0 %collective-permute-start.5 = (bf16[16,16,256]{2,1,0:T(8,128)(2,1)S(1)}, bf16[16,16,256]{2,1,0:T(8,128)(2,1)S(1)}, u32[]{:S(2)}, u32[]{:S(2)}) collective-permute-start(bf16[16,16,256]{2,1,0:T(8,128)(2,1)S(1)} %get-tuple-element.27), channel_id=1, source_target_pairs={{0,3},{1,2},{2,1},{3,0},{4,7},{5,6},{6,5},{7,4},{8,11},{9,10},{10,... | collective-permute-start | bytes 393224 | tf_op jit(solution)/shard_map/ppermute | solution.py:186
  51.5 8.8 %collective-permute-start.6 = (bf16[16,16,256]{2,1,0:T(8,128)(2,1)S(1)}, bf16[16,16,256]{2,1,0:T(8,128)(2,1)S(1)}, u32[]{:S(2)}, u32[]{:S(2)}) collective-permute-start(bf16[16,16,256]{2,1,0:T(8,128)(2,1)S(1)} %get-tuple-element.28), channel_id=1, source_target_pairs={{0,5},{1,4},{2,7},{3,6},{4,1},{5,0},{6,3},{7,2},{8,13},{9,12},{10,... | collective-permute-start | bytes 393224 | tf_op jit(solution)/shard_map/ppermute | solution.py:186
  61.1 16.3 %copy-start = (bf16[128,128]{1,0:T(8,128)(2,1)S(1)}, bf16[128,128]{1,0:T(8,128)(2,1)}, u32[]{:S(2)}) copy-start(bf16[128,128]{1,0:T(8,128)(2,1)} %proj_ref.5) | copy-start | bytes 98308
  61.1 6.5 %collective-permute-start.7 = (bf16[16,16,256]{2,1,0:T(8,128)(2,1)S(1)}, bf16[16,16,256]{2,1,0:T(8,128)(2,1)S(1)}, u32[]{:S(2)}, u32[]{:S(2)}) collective-permute-start(bf16[16,16,256]{2,1,0:T(8,128)(2,1)S(1)} %get-tuple-element.30), channel_id=1, source_target_pairs={{0,1},{1,0},{2,3},{3,2},{4,5},{5,4},{6,7},{7,6},{8,9},{9,8},{10,11... | collective-permute-start | bytes 393224 | tf_op jit(solution)/shard_map/ppermute | solution.py:186
  61.4 7.7 %collective-permute-start.8 = (bf16[16,16,256]{2,1,0:T(8,128)(2,1)S(1)}, bf16[16,16,256]{2,1,0:T(8,128)(2,1)S(1)}, u32[]{:S(2)}, u32[]{:S(2)}) collective-permute-start(bf16[16,16,256]{2,1,0:T(8,128)(2,1)S(1)} %get-tuple-element.31), channel_id=1, source_target_pairs={{0,6},{1,7},{2,4},{3,5},{4,2},{5,3},{6,0},{7,1},{8,14},{9,15},{10,... | collective-permute-start | bytes 393224 | tf_op jit(solution)/shard_map/ppermute | solution.py:186
  65.1 8.0 %collective-permute-start.9 = (bf16[16,16,256]{2,1,0:T(8,128)(2,1)S(1)}, bf16[16,16,256]{2,1,0:T(8,128)(2,1)S(1)}, u32[]{:S(2)}, u32[]{:S(2)}) collective-permute-start(bf16[16,16,256]{2,1,0:T(8,128)(2,1)S(1)} %get-tuple-element.32), channel_id=1, source_target_pairs={{0,2},{1,3},{2,0},{3,1},{4,6},{5,7},{6,4},{7,5},{8,10},{9,11},{10,... | collective-permute-start | bytes 393224 | tf_op jit(solution)/shard_map/ppermute | solution.py:186
  65.1 8.0 %collective-permute-start.10 = (bf16[16,16,256]{2,1,0:T(8,128)(2,1)S(1)}, bf16[16,16,256]{2,1,0:T(8,128)(2,1)S(1)}, u32[]{:S(2)}, u32[]{:S(2)}) collective-permute-start(bf16[16,16,256]{2,1,0:T(8,128)(2,1)S(1)} %get-tuple-element.33), channel_id=1, source_target_pairs={{0,4},{1,5},{2,6},{3,7},{4,0},{5,1},{6,2},{7,3},{8,12},{9,13},{10,... | collective-permute-start | bytes 393224 | tf_op jit(solution)/shard_map/ppermute | solution.py:186
  65.7 9.0 %collective-permute-start.11 = (bf16[16,16,256]{2,1,0:T(8,128)(2,1)S(1)}, bf16[16,16,256]{2,1,0:T(8,128)(2,1)S(1)}, u32[]{:S(2)}, u32[]{:S(2)}) collective-permute-start(bf16[16,16,256]{2,1,0:T(8,128)(2,1)S(1)} %get-tuple-element.34), channel_id=1, source_target_pairs={{0,7},{1,6},{2,5},{3,4},{4,3},{5,2},{6,1},{7,0},{8,15},{9,14},{10,... | collective-permute-start | bytes 393224 | tf_op jit(solution)/shard_map/ppermute | solution.py:186
  67.6 9.7 %collective-permute-start.12 = (bf16[16,16,256]{2,1,0:T(8,128)(2,1)S(1)}, bf16[16,16,256]{2,1,0:T(8,128)(2,1)S(1)}, u32[]{:S(2)}, u32[]{:S(2)}) collective-permute-start(bf16[16,16,256]{2,1,0:T(8,128)(2,1)S(1)} %get-tuple-element.35), channel_id=1, source_target_pairs={{0,3},{1,2},{2,1},{3,0},{4,7},{5,6},{6,5},{7,4},{8,11},{9,10},{10,... | collective-permute-start | bytes 393224 | tf_op jit(solution)/shard_map/ppermute | solution.py:186
  69.1 8.2 %collective-permute-start.13 = (bf16[16,16,256]{2,1,0:T(8,128)(2,1)S(1)}, bf16[16,16,256]{2,1,0:T(8,128)(2,1)S(1)}, u32[]{:S(2)}, u32[]{:S(2)}) collective-permute-start(bf16[16,16,256]{2,1,0:T(8,128)(2,1)S(1)} %get-tuple-element.36), channel_id=1, source_target_pairs={{0,5},{1,4},{2,7},{3,6},{4,1},{5,0},{6,3},{7,2},{8,13},{9,12},{10,... | collective-permute-start | bytes 393224 | tf_op jit(solution)/shard_map/ppermute | solution.py:186

commit v5 on v4

--- a/solution.py
+++ b/solution.py
@@ -53,42 +53,49 @@
 ):
     copies, blocks, group, rows, tokens = out_hbm.shape
     hidden = blocks * group
+    chunks = tokens // 128
     loads = [
-        pltpu.make_async_copy(source, target, in_sems.at[i])
+        pltpu.make_async_copy(
+            pair_hbm.at[:, pl.ds(t * 128, 128)], pair_ref.at[:, pl.ds(t * 128, 128)], in_sems.at[t]
+        )
+        for t in range(chunks)
+    ]
+    small_loads = [
+        pltpu.make_async_copy(source, target, in_sems.at[chunks + i])
         for i, (source, target) in enumerate((
-            (pair_hbm, pair_ref),
             (proj_hbm.at[:, 2 * hidden : 4 * hidden], weights_ref),
             (mask_hbm, mask_ref),
             (gain_hbm, gain_ref),
         ))
     ]
-    for load in loads:
+    for load in loads[:1] + small_loads + loads[1:]:
         load.start()
-    for load in loads:
+    for load in small_loads:
         load.wait()
     weights = weights_ref[...].T
     gain = gain_ref[...]
-    step = 4 if rows % 4 == 0 else 1
-    for first in range(0, rows, step):
-        x = pair_ref[first : first + step].reshape(step * tokens, -1)
-        proj = lax.dot_general(
-            weights, normed_rows(x, gain), OVER_LAST, preferred_element_type=jnp.float32
-        )
-        for r in range(first, first + step):
-            of_row = proj[:, (r - first) * tokens : (r - first + 1) * tokens]
-            keep = mask_ref[r : r + 1, :].astype(jnp.float32)
-            value = keep * sigmoid(of_row[hidden:]) * of_row[:hidden]
-            for t in range(tokens // 128):
-                total[t, pl.ds(r, hidden, stride=rows), :] = value[:, t * 128 : (t + 1) * 128]
     stores = []
-    for b in range(blocks):
-        for t in range(tokens // 128):
+    for t in range(chunks):
+        lanes = slice(t * 128, (t + 1) * 128)
+        loads[t].wait()
+        normed = normed_rows(pair_ref[:, lanes].reshape(rows * 128, -1), gain)
+        proj = lax.dot_general(weights, normed, OVER_LAST, preferred_element_type=jnp.float32)
+        for r in range(rows):
+            of_row = proj[:, r * 128 : (r + 1) * 128]
+            keep = mask_ref[r : r + 1, lanes].astype(jnp.float32)
+            total[t, pl.ds(r, hidden, stride=rows), :] = (
+                keep * sigmoid(of_row[hidden:]) * of_row[:hidden]
+            )
+        for b in range(blocks):
             block = total[t, b * group * rows : (b + 1) * group * rows, :].astype(jnp.bfloat16)
-            staged[b, :, :, t * 128 : (t + 1) * 128] = block.reshape(group, rows, 128)
-        for c in range(copies):
-            store = pltpu.make_async_copy(staged.at[b], out_hbm.at[c, b], out_sems.at[c, b])
-            store.start()
-            stores.append(store)
+            staged[b, :, :, lanes] = block.reshape(group, rows, 128)
+            part = pl.ds(t * 128, 128)
+            for c in range(copies):
+                store = pltpu.make_async_copy(
+                    staged.at[b, :, :, part], out_hbm.at[c, b, :, :, part], out_sems.at[c, b, t]
+                )
+                store.start()
+                stores.append(store)
     for store in stores:
         store.wait()
 
@@ -210,8 +217,8 @@
             pltpu.VMEM((width, 2 * hidden), bf16),
             total,
             pltpu.VMEM((blocks, group, rows, tokens), bf16),
-            pltpu.SemaphoreType.DMA((4,)),
-            pltpu.SemaphoreType.DMA((2, blocks)),
+            pltpu.SemaphoreType.DMA((tokens // 128 + 3,)),
+            pltpu.SemaphoreType.DMA((2, blocks, tokens // 128)),
         ),
         in_hbm=range(4),
         out_hbm=True,

time: 79.9 us -> 79.7 us (level)
  no operation moved by 1% of the time
where the time goes in v5:
time: 79.7 us; the launch traced here: 79.5 us
  waiting for transfers between devices  41.3 us (52%)
  starting transfers between devices  23.7 us (30%)
  Pallas kernels  14.3 us (18%)
    ppermute x14, waiting for transfers between devices, exchange(): lax.ppermute(part, 'row', [(i, i ^ step) for i in range(devices)])  41.3 us
    ppermute x14, starting transfers between devices, exchange(): lax.ppermute(part, 'row', [(i, i ^ step) for i in range(devices)])  16.1 us
    pallas_call x5, Pallas kernels, call(): pl.pallas_call(kernel, out_shape=out_shape, in_specs=specs, out_specs=jax...  14.3 us
    all_to_all x1, starting transfers between devices, on_device(): lax.all_to_all(right, 'row', split_axis=0, concat_axis=0, tiled=True)  7.52 us
  transfers between devices with their start and end apart: 15, of which 8 were waited for; matrix products, arithmetic and copies ran while one was open for 0% of the time, Pallas kernels for 8%

profile of v5, /device:TPU:0, one launch (start us, length us, event | category | flops | bytes accessed | tf_op | source)
XLA Modules:
  0.0 79.5 jit_solution(303421184414066424)
XLA Ops:
  0.0 4.8 %shard_map.65 = bf16[2,8,16,16,256]{4,3,2,1,0:T(8,128)(2,1)} custom-call(bf16[16,256,128]{2,1,0:T(8,128)(2,1)} %pair_ref.1, s32[16,256]{1,0:T(8,128)} %mask_ref.1, f32[1,128]{1,0:T(1,128)} %bitcast.3, bf16[128,512]{1,0:T(8,128)(2,1)} %proj_ref.4), custom_call_target="tpu_custom_call" | custom-call | flops 1000000000 | bytes 4000000 | tf_op jit(solution)/shard_map/pallas_call | solution.py:178
  4.8 0.0 copy-start.1
  4.8 0.0 copy-start.2
  4.8 0.0 copy-start.4
  4.8 0.0 copy-start.5
  4.8 7.5 %all-to-all-start = ((bf16[16,16,16,256]{3,2,1,0:T(8,128)(2,1)}), bf16[16,16,16,256]{3,2,1,0:T(8,128)(2,1)S(1)}, u32[]{:S(2)}, u32[]{:S(2)}) async-start(bf16[16,16,16,256]{3,2,1,0:T(8,128)(2,1)} %bitcast.6), calls=%async_computation | async-start | bytes 4194304 | tf_op jit(solution)/shard_map/all_to_all | solution.py:227
  12.4 0.0 copy-done.1
  12.4 0.0 copy-done.2
  12.4 0.0 copy-done.4
  12.4 0.0 copy-done.5
  12.4 3.2 %shard_map.66 = (bf16[16,16,256]{2,1,0:T(8,128)(2,1)S(1)}, bf16[16,16,256]{2,1,0:T(8,128)(2,1)S(1)}, bf16[16,16,256]{2,1,0:T(8,128)(2,1)S(1)}, bf16[16,16,256]{2...) custom-call(s32[1]{0:T(128)} %bitcast.me_ref, ...), custom_call_target="tpu_custom_call" | custom-call | flops 1000000000 | bytes 4000000 | tf_op jit(solution)/shard_map/pallas_call | solution.py:178
  15.6 0.0 copy-start.3
  15.6 0.5 collective-permute-start
  16.1 2.6 %collective-permute-start.1 = (bf16[16,16,256]{2,1,0:T(8,128)(2,1)S(1)}, bf16[16,16,256]{2,1,0:T(8,128)(2,1)S(1)}, u32[]{:S(2)}, u32[]{:S(2)}) collective-permute-start(bf16[16,16,256]{2,1,0:T(8,128)(2,1)S(1)} %get-tuple-element.23), channel_id=1, source_target_pairs={{0,6},{1,7},{2,4},{3,5},{4,2},{5,3},{6,0},{7,1},{8,14},{9,15},{10,... | collective-permute-start | bytes 393224 | tf_op jit(solution)/shard_map/ppermute | solution.py:193
  18.6 0.6 collective-permute-start.2
  19.2 0.3 collective-permute-start.3
  19.6 1.7 %collective-permute-start.4 = (bf16[16,16,256]{2,1,0:T(8,128)(2,1)S(1)}, bf16[16,16,256]{2,1,0:T(8,128)(2,1)S(1)}, u32[]{:S(2)}, u32[]{:S(2)}) collective-permute-start(bf16[16,16,256]{2,1,0:T(8,128)(2,1)S(1)} %get-tuple-element.26), channel_id=1, source_target_pairs={{0,7},{1,6},{2,5},{3,4},{4,3},{5,2},{6,1},{7,0},{8,15},{9,14},{10,... | collective-permute-start | bytes 393224 | tf_op jit(solution)/shard_map/ppermute | solution.py:193
  21.2 0.0 collective-permute-done.rest_1_
  21.2 1.2 %collective-permute-start.5 = (bf16[16,16,256]{2,1,0:T(8,128)(2,1)S(1)}, bf16[16,16,256]{2,1,0:T(8,128)(2,1)S(1)}, u32[]{:S(2)}, u32[]{:S(2)}) collective-permute-start(bf16[16,16,256]{2,1,0:T(8,128)(2,1)S(1)} %get-tuple-element.27), channel_id=1, source_target_pairs={{0,3},{1,2},{2,1},{3,0},{4,7},{5,6},{6,5},{7,4},{8,11},{9,10},{10,... | collective-permute-start | bytes 393224 | tf_op jit(solution)/shard_map/ppermute | solution.py:193
  22.4 28.8 %collective-permute-done.1.rest_2_ = bf16[16,16,256]{2,1,0:T(8,128)(2,1)S(1)} collective-permute-done((bf16[16,16,256]{2,1,0:T(8,128)(2,1)S(1)}, bf16[16,16,256]{2,1,0:T(8,128)(2,1)S(1)}, u32[]{:S(2)}, u32[]{:S(2)}) %collective-permute-start.1) | collective-permute-done | bytes 131104 | tf_op jit(solution)/shard_map/ppermute | solution.py:193
  51.2 2.1 %collective-permute-start.6 = (bf16[16,16,256]{2,1,0:T(8,128)(2,1)S(1)}, bf16[16,16,256]{2,1,0:T(8,128)(2,1)S(1)}, u32[]{:S(2)}, u32[]{:S(2)}) collective-permute-start(bf16[16,16,256]{2,1,0:T(8,128)(2,1)S(1)} %get-tuple-element.28), channel_id=1, source_target_pairs={{0,5},{1,4},{2,7},{3,6},{4,1},{5,0},{6,3},{7,2},{8,13},{9,12},{10,... | collective-permute-start | bytes 393224 | tf_op jit(solution)/shard_map/ppermute | solution.py:193
  53.3 0.0 collective-permute-done.2.rest_3_
  53.3 0.8 collective-permute-done.3.rest_4_
  54.0 4.2 %collective-permute-done.4.rest_5_ = bf16[16,16,256]{2,1,0:T(8,128)(2,1)S(1)} collective-permute-done((bf16[16,16,256]{2,1,0:T(8,128)(2,1)S(1)}, bf16[16,16,256]{2,1,0:T(8,128)(2,1)S(1)}, u32[]{:S(2)}, u32[]{:S(2)}) %collective-permute-start.4) | collective-permute-done | bytes 131104 | tf_op jit(solution)/shard_map/ppermute | solution.py:193
  58.2 0.0 collective-permute-done.5.rest_6_
  58.2 1.8 %collective-permute-done.6.rest_7_ = bf16[16,16,256]{2,1,0:T(8,128)(2,1)S(1)} collective-permute-done((bf16[16,16,256]{2,1,0:T(8,128)(2,1)S(1)}, bf16[16,16,256]{2,1,0:T(8,128)(2,1)S(1)}, u32[]{:S(2)}, u32[]{:S(2)}) %collective-permute-start.6) | collective-permute-done | bytes 131104 | tf_op jit(solution)/shard_map/ppermute | solution.py:193
  60.0 0.0 all-to-all-done.right_ref
  60.0 0.8 shard_map.67
  60.8 0.0 copy-start
  60.8 0.4 collective-permute-start.7
  61.2 3.7 %collective-permute-start.8 = (bf16[16,16,256]{2,1,0:T(8,128)(2,1)S(1)}, bf16[16,16,256]{2,1,0:T(8,128)(2,1)S(1)}, u32[]{:S(2)}, u32[]{:S(2)}) collective-permute-start(bf16[16,16,256]{2,1,0:T(8,128)(2,1)S(1)} %get-tuple-element.31), channel_id=1, source_target_pairs={{0,6},{1,7},{2,4},{3,5},{4,2},{5,3},{6,0},{7,1},{8,14},{9,15},{10,... | collective-permute-start | bytes 393224 | tf_op jit(solution)/shard_map/ppermute | solution.py:193
  64.9 0.0 collective-permute-start.9
  64.9 0.6 collective-permute-start.10
  65.4 1.9 %collective-permute-start.11 = (bf16[16,16,256]{2,1,0:T(8,128)(2,1)S(1)}, bf16[16,16,256]{2,1,0:T(8,128)(2,1)S(1)}, u32[]{:S(2)}, u32[]{:S(2)}) collective-permute-start(bf16[16,16,256]{2,1,0:T(8,128)(2,1)S(1)} %get-tuple-element.34), channel_id=1, source_target_pairs={{0,7},{1,6},{2,5},{3,4},{4,3},{5,2},{6,1},{7,0},{8,15},{9,14},{10,... | collective-permute-start | bytes 393224 | tf_op jit(solution)/shard_map/ppermute | solution.py:193
  67.3 0.0 collective-permute-done.7.rest_1_
  67.3 0.8 collective-permute-start.12
  68.1 0.8 collective-permute-done.8.rest_2_
  68.9 0.0 collective-permute-start.13
  68.9 0.0 copy-done.3
  68.9 3.2 %shard_map.64.gate_ref = f32[16,256,128]{2,1,0:T(8,128)S(1)} custom-call(bf16[16,256,128]{2,1,0:T(8,128)(2,1)} %pair_ref.1, f32[1,128]{1,0:T(1,128)S(1)} %bitcast.5, bf16[128,128]{1,0:T(8,128)(2,1)S(1)} %copy-done.3), custom_call_target="tpu_custom_call" | custom-call | flops 1000000000 | bytes 4000000 | tf_op jit(solution)/shard_map/pallas_call | solution.py:178
  72.0 0.8 %collective-permute-done.9.rest_3_ = bf16[16,16,256]{2,1,0:T(8,128)(2,1)S(1)} collective-permute-done((bf16[16,16,256]{2,1,0:T(8,128)(2,1)S(1)}, bf16[16,16,256]{2,1,0:T(8,128)(2,1)S(1)}, u32[]{:S(2)}, u32[]{:S(2)}) %collective-permute-start.9) | collective-permute-done | bytes 131104 | tf_op jit(solution)/shard_map/ppermute | solution.py:193
  72.9 0.0 collective-permute-done.10.rest_4_
  72.9 1.6 %collective-permute-done.11.rest_5_ = bf16[16,16,256]{2,1,0:T(8,128)(2,1)S(1)} collective-permute-done((bf16[16,16,256]{2,1,0:T(8,128)(2,1)S(1)}, bf16[16,16,256]{2,1,0:T(8,128)(2,1)S(1)}, u32[]{:S(2)}, u32[]{:S(2)}) %collective-permute-start.11) | collective-permute-done | bytes 131104 | tf_op jit(solution)/shard_map/ppermute | solution.py:193
  74.4 2.6 %collective-permute-done.12.rest_6_ = bf16[16,16,256]{2,1,0:T(8,128)(2,1)S(1)} collective-permute-done((bf16[16,16,256]{2,1,0:T(8,128)(2,1)S(1)}, bf16[16,16,256]{2,1,0:T(8,128)(2,1)S(1)}, u32[]{:S(2)}, u32[]{:S(2)}) %collective-permute-start.12) | collective-permute-done | bytes 131104 | tf_op jit(solution)/shard_map/ppermute | solution.py:193
  77.1 0.0 collective-permute-done.13.rest_7_
  77.1 0.0 copy-done
  77.1 2.4 %shard_map.68 = bf16[16,256,128]{2,1,0:T(8,128)(2,1)} custom-call(s32[1]{0:T(128)} %bitcast.me_ref, f32[16,256,128]{2,1,0:T(8,128)S(1)} %shard_map.64.gate_ref, bf16[128,128]{1,0:T(8,128)(2,1)S(1)} %copy-done, bf16[16,16,256]{2,1,0:T(8,128)(2,1)S(1)} %get-tuple-element.29.rest_0_, bf16[16,16,256]{2,1,0:T(8,128)(2,1)S(1)} %collective-permute-done.7.rest_1_, ...), custom_call_target="tpu_custom_call" | custom-call | flops 1000000000 | bytes 4000000 | tf_op jit(solution)/shard_map/pallas_call | solution.py:178
Async XLA Ops:
  4.8 7.6 %copy-start.1 = (bf16[16,256,128]{2,1,0:T(8,128)(2,1)S(1)}, bf16[16,256,128]{2,1,0:T(8,128)(2,1)}, u32[]{:S(2)}) copy-start(bf16[16,256,128]{2,1,0:T(8,128)(2,1)} %pair_ref.1) | copy-start | bytes 3145732
  4.8 7.6 %copy-start.2 = (bf16[128,512]{1,0:T(8,128)(2,1)S(1)}, bf16[128,512]{1,0:T(8,128)(2,1)}, u32[]{:S(2)}) copy-start(bf16[128,512]{1,0:T(8,128)(2,1)} %proj_ref.4) | copy-start | bytes 393220
  4.8 7.6 %copy-start.4 = (s32[16,256]{1,0:T(8,128)S(1)}, s32[16,256]{1,0:T(8,128)}, u32[]{:S(2)}) copy-start(s32[16,256]{1,0:T(8,128)} %mask_ref.1) | copy-start | bytes 49156
  4.8 7.6 %copy-start.5 = (f32[128]{0:T(128)S(1)}, f32[128]{0:T(128)}, u32[]{:S(2)}) copy-start(f32[128]{0:T(128)} %param.8) | copy-start | bytes 1540
  4.8 55.2 %all-to-all-start = ((bf16[16,16,16,256]{3,2,1,0:T(8,128)(2,1)}), bf16[16,16,16,256]{3,2,1,0:T(8,128)(2,1)S(1)}, u32[]{:S(2)}, u32[]{:S(2)}) async-start(bf16[16,16,16,256]{3,2,1,0:T(8,128)(2,1)} %bitcast.6), calls=%async_computation | async-start | bytes 4194304 | tf_op jit(solution)/shard_map/all_to_all | solution.py:227
  15.6 53.3 %copy-start.3 = (bf16[128,128]{1,0:T(8,128)(2,1)S(1)}, bf16[128,128]{1,0:T(8,128)(2,1)}, u32[]{:S(2)}) copy-start(bf16[128,128]{1,0:T(8,128)(2,1)} %proj_ref.3) | copy-start | bytes 98308
  15.6 5.7 %collective-permute-start = (bf16[16,16,256]{2,1,0:T(8,128)(2,1)S(1)}, bf16[16,16,256]{2,1,0:T(8,128)(2,1)S(1)}, u32[]{:S(2)}, u32[]{:S(2)}) collective-permute-start(bf16[16,16,256]{2,1,0:T(8,128)(2,1)S(1)} %get-tuple-element.22), channel_id=1, source_target_pairs={{0,1},{1,0},{2,3},{3,2},{4,5},{5,4},{6,7},{7,6},{8,9},{9,8},{10,11... | collective-permute-start | bytes 393224 | tf_op jit(solution)/shard_map/ppermute | solution.py:193
  16.1 35.2 %collective-permute-start.1 = (bf16[16,16,256]{2,1,0:T(8,128)(2,1)S(1)}, bf16[16,16,256]{2,1,0:T(8,128)(2,1)S(1)}, u32[]{:S(2)}, u32[]{:S(2)}) collective-permute-start(bf16[16,16,256]{2,1,0:T(8,128)(2,1)S(1)} %get-tuple-element.23), channel_id=1, source_target_pairs={{0,6},{1,7},{2,4},{3,5},{4,2},{5,3},{6,0},{7,1},{8,14},{9,15},{10,... | collective-permute-start | bytes 393224 | tf_op jit(solution)/shard_map/ppermute | solution.py:193
  18.6 34.6 %collective-permute-start.2 = (bf16[16,16,256]{2,1,0:T(8,128)(2,1)S(1)}, bf16[16,16,256]{2,1,0:T(8,128)(2,1)S(1)}, u32[]{:S(2)}, u32[]{:S(2)}) collective-permute-start(bf16[16,16,256]{2,1,0:T(8,128)(2,1)S(1)} %get-tuple-element.24), channel_id=1, source_target_pairs={{0,2},{1,3},{2,0},{3,1},{4,6},{5,7},{6,4},{7,5},{8,10},{9,11},{10,... | collective-permute-start | bytes 393224 | tf_op jit(solution)/shard_map/ppermute | solution.py:193
  19.2 34.8 %collective-permute-start.3 = (bf16[16,16,256]{2,1,0:T(8,128)(2,1)S(1)}, bf16[16,16,256]{2,1,0:T(8,128)(2,1)S(1)}, u32[]{:S(2)}, u32[]{:S(2)}) collective-permute-start(bf16[16,16,256]{2,1,0:T(8,128)(2,1)S(1)} %get-tuple-element.25), channel_id=1, source_target_pairs={{0,4},{1,5},{2,6},{3,7},{4,0},{5,1},{6,2},{7,3},{8,12},{9,13},{10,... | collective-permute-start | bytes 393224 | tf_op jit(solution)/shard_map/ppermute | solution.py:193
  19.6 38.6 %collective-permute-start.4 = (bf16[16,16,256]{2,1,0:T(8,128)(2,1)S(1)}, bf16[16,16,256]{2,1,0:T(8,128)(2,1)S(1)}, u32[]{:S(2)}, u32[]{:S(2)}) collective-permute-start(bf16[16,16,256]{2,1,0:T(8,128)(2,1)S(1)} %get-tuple-element.26), channel_id=1, source_target_pairs={{0,7},{1,6},{2,5},{3,4},{4,3},{5,2},{6,1},{7,0},{8,15},{9,14},{10,... | collective-permute-start | bytes 393224 | tf_op jit(solution)/shard_map/ppermute | solution.py:193
  21.2 37.0 %collective-permute-start.5 = (bf16[16,16,256]{2,1,0:T(8,128)(2,1)S(1)}, bf16[16,16,256]{2,1,0:T(8,128)(2,1)S(1)}, u32[]{:S(2)}, u32[]{:S(2)}) collective-permute-start(bf16[16,16,256]{2,1,0:T(8,128)(2,1)S(1)} %get-tuple-element.27), channel_id=1, source_target_pairs={{0,3},{1,2},{2,1},{3,0},{4,7},{5,6},{6,5},{7,4},{8,11},{9,10},{10,... | collective-permute-start | bytes 393224 | tf_op jit(solution)/shard_map/ppermute | solution.py:193
  51.2 8.8 %collective-permute-start.6 = (bf16[16,16,256]{2,1,0:T(8,128)(2,1)S(1)}, bf16[16,16,256]{2,1,0:T(8,128)(2,1)S(1)}, u32[]{:S(2)}, u32[]{:S(2)}) collective-permute-start(bf16[16,16,256]{2,1,0:T(8,128)(2,1)S(1)} %get-tuple-element.28), channel_id=1, source_target_pairs={{0,5},{1,4},{2,7},{3,6},{4,1},{5,0},{6,3},{7,2},{8,13},{9,12},{10,... | collective-permute-start | bytes 393224 | tf_op jit(solution)/shard_map/ppermute | solution.py:193
  60.8 16.3 %copy-start = (bf16[128,128]{1,0:T(8,128)(2,1)S(1)}, bf16[128,128]{1,0:T(8,128)(2,1)}, u32[]{:S(2)}) copy-start(bf16[128,128]{1,0:T(8,128)(2,1)} %proj_ref.5) | copy-start | bytes 98308
  60.8 6.5 %collective-permute-start.7 = (bf16[16,16,256]{2,1,0:T(8,128)(2,1)S(1)}, bf16[16,16,256]{2,1,0:T(8,128)(2,1)S(1)}, u32[]{:S(2)}, u32[]{:S(2)}) collective-permute-start(bf16[16,16,256]{2,1,0:T(8,128)(2,1)S(1)} %get-tuple-element.30), channel_id=1, source_target_pairs={{0,1},{1,0},{2,3},{3,2},{4,5},{5,4},{6,7},{7,6},{8,9},{9,8},{10,11... | collective-permute-start | bytes 393224 | tf_op jit(solution)/shard_map/ppermute | solution.py:193
  61.2 7.7 %collective-permute-start.8 = (bf16[16,16,256]{2,1,0:T(8,128)(2,1)S(1)}, bf16[16,16,256]{2,1,0:T(8,128)(2,1)S(1)}, u32[]{:S(2)}, u32[]{:S(2)}) collective-permute-start(bf16[16,16,256]{2,1,0:T(8,128)(2,1)S(1)} %get-tuple-element.31), channel_id=1, source_target_pairs={{0,6},{1,7},{2,4},{3,5},{4,2},{5,3},{6,0},{7,1},{8,14},{9,15},{10,... | collective-permute-start | bytes 393224 | tf_op jit(solution)/shard_map/ppermute | solution.py:193
  64.9 8.0 %collective-permute-start.9 = (bf16[16,16,256]{2,1,0:T(8,128)(2,1)S(1)}, bf16[16,16,256]{2,1,0:T(8,128)(2,1)S(1)}, u32[]{:S(2)}, u32[]{:S(2)}) collective-permute-start(bf16[16,16,256]{2,1,0:T(8,128)(2,1)S(1)} %get-tuple-element.32), channel_id=1, source_target_pairs={{0,2},{1,3},{2,0},{3,1},{4,6},{5,7},{6,4},{7,5},{8,10},{9,11},{10,... | collective-permute-start | bytes 393224 | tf_op jit(solution)/shard_map/ppermute | solution.py:193
  64.9 8.0 %collective-permute-start.10 = (bf16[16,16,256]{2,1,0:T(8,128)(2,1)S(1)}, bf16[16,16,256]{2,1,0:T(8,128)(2,1)S(1)}, u32[]{:S(2)}, u32[]{:S(2)}) collective-permute-start(bf16[16,16,256]{2,1,0:T(8,128)(2,1)S(1)} %get-tuple-element.33), channel_id=1, source_target_pairs={{0,4},{1,5},{2,6},{3,7},{4,0},{5,1},{6,2},{7,3},{8,12},{9,13},{10,... | collective-permute-start | bytes 393224 | tf_op jit(solution)/shard_map/ppermute | solution.py:193
  65.4 9.0 %collective-permute-start.11 = (bf16[16,16,256]{2,1,0:T(8,128)(2,1)S(1)}, bf16[16,16,256]{2,1,0:T(8,128)(2,1)S(1)}, u32[]{:S(2)}, u32[]{:S(2)}) collective-permute-start(bf16[16,16,256]{2,1,0:T(8,128)(2,1)S(1)} %get-tuple-element.34), channel_id=1, source_target_pairs={{0,7},{1,6},{2,5},{3,4},{4,3},{5,2},{6,1},{7,0},{8,15},{9,14},{10,... | collective-permute-start | bytes 393224 | tf_op jit(solution)/shard_map/ppermute | solution.py:193
  67.3 9.7 %collective-permute-start.12 = (bf16[16,16,256]{2,1,0:T(8,128)(2,1)S(1)}, bf16[16,16,256]{2,1,0:T(8,128)(2,1)S(1)}, u32[]{:S(2)}, u32[]{:S(2)}) collective-permute-start(bf16[16,16,256]{2,1,0:T(8,128)(2,1)S(1)} %get-tuple-element.35), channel_id=1, source_target_pairs={{0,3},{1,2},{2,1},{3,0},{4,7},{5,6},{6,5},{7,4},{8,11},{9,10},{10,... | collective-permute-start | bytes 393224 | tf_op jit(solution)/shard_map/ppermute | solution.py:193
  68.9 8.2 %collective-permute-start.13 = (bf16[16,16,256]{2,1,0:T(8,128)(2,1)S(1)}, bf16[16,16,256]{2,1,0:T(8,128)(2,1)S(1)}, u32[]{:S(2)}, u32[]{:S(2)}) collective-permute-start(bf16[16,16,256]{2,1,0:T(8,128)(2,1)S(1)} %get-tuple-element.36), channel_id=1, source_target_pairs={{0,5},{1,4},{2,7},{3,6},{4,1},{5,0},{6,3},{7,2},{8,13},{9,12},{10,... | collective-permute-start | bytes 393224 | tf_op jit(solution)/shard_map/ppermute | solution.py:193

commit v6 on v5

--- a/solution.py
+++ b/solution.py
@@ -29,22 +29,18 @@
     return (centered * lax.rsqrt(variance + EPS) * gain).astype(jnp.bfloat16)
 
 
-def operand(pair_ref, mask_ref, gain_ref, proj_ref, total, first):
-    rows, tokens, _ = pair_ref.shape
-    hidden = proj_ref.shape[1] // 4
-    weights = proj_ref[:, first * hidden : (first + 2) * hidden].T
-    gain = gain_ref[...]
-
-    def step(r, carry):
-        normed = normed_rows(pair_ref[r], gain)
-        proj = lax.dot_general(weights, normed, OVER_LAST, preferred_element_type=jnp.float32)
-        keep = mask_ref[pl.ds(r, 1), :].astype(jnp.float32)
-        value = keep * sigmoid(proj[hidden:]) * proj[:hidden]
-        for t in range(tokens // 128):
-            total[t, pl.ds(r, hidden, stride=rows), :] = value[:, t * 128 : (t + 1) * 128]
-        return carry
-
-    lax.fori_loop(0, rows, step, 0, unroll=4)
+def gated(pair_ref, mask_ref, weights, gain, total, t):
+    rows = pair_ref.shape[0]
+    hidden = weights.shape[0] // 2
+    lanes = slice(t * 128, (t + 1) * 128)
+    normed = normed_rows(pair_ref[:, lanes].reshape(rows * 128, -1), gain)
+    proj = lax.dot_general(weights, normed, OVER_LAST, preferred_element_type=jnp.float32)
+    for r in range(rows):
+        of_row = proj[:, r * 128 : (r + 1) * 128]
+        keep = mask_ref[r : r + 1, lanes].astype(jnp.float32)
+        total[t, pl.ds(r, hidden, stride=rows), :] = (
+            keep * sigmoid(of_row[hidden:]) * of_row[:hidden]
+        )
 
 
 def right_kernel(
@@ -78,14 +74,7 @@
     for t in range(chunks):
         lanes = slice(t * 128, (t + 1) * 128)
         loads[t].wait()
-        normed = normed_rows(pair_ref[:, lanes].reshape(rows * 128, -1), gain)
-        proj = lax.dot_general(weights, normed, OVER_LAST, preferred_element_type=jnp.float32)
-        for r in range(rows):
-            of_row = proj[:, r * 128 : (r + 1) * 128]
-            keep = mask_ref[r : r + 1, lanes].astype(jnp.float32)
-            total[t, pl.ds(r, hidden, stride=rows), :] = (
-                keep * sigmoid(of_row[hidden:]) * of_row[:hidden]
-            )
+        gated(pair_ref, mask_ref, weights, gain, total, t)
         for b in range(blocks):
             block = total[t, b * group * rows : (b + 1) * group * rows, :].astype(jnp.bfloat16)
             staged[b, :, :, lanes] = block.reshape(group, rows, 128)
@@ -104,12 +93,14 @@
     *out_refs, total = rest
     blocks = len(out_refs)
     group, rows, tokens = out_refs[0].shape
-    operand(pair_ref, mask_ref, gain_ref, proj_ref, total, 0)
-    for step, out_ref in zip(steps_of(blocks), out_refs):
-        b = me_ref[0] ^ step
-        for t in range(tokens // 128):
-            block = total[t, pl.ds(pl.multiple_of(b * group * rows, group * rows), group * rows), :]
-            out_ref[:, :, t * 128 : (t + 1) * 128] = block.astype(jnp.bfloat16).reshape(group, rows, 128)
+    weights = proj_ref[:, : 2 * blocks * group].T
+    gain = gain_ref[...]
+    for t in range(tokens // 128):
+        gated(pair_ref, mask_ref, weights, gain, total, t)
+        for step, out_ref in zip(steps_of(blocks), out_refs):
+            first = pl.multiple_of((me_ref[0] ^ step) * (group * rows), group * rows)
+            block = total[t, pl.ds(first, group * rows), :].astype(jnp.bfloat16)
+            out_ref[:, :, t * 128 : (t + 1) * 128] = block.reshape(group, rows, 128)
 
 
 def cross_kernel(right_ref, *rest):
@@ -204,7 +195,7 @@
     bf16 = jnp.bfloat16
     me = lax.rem(lax.axis_index("row"), blocks).astype(jnp.int32).reshape(1)
     gain = in_gain.reshape(1, width)
-    total = pltpu.VMEM((tokens // 128, hidden * rows, 128), jnp.float32)
+    total = pltpu.VMEM((tokens // 128, (hidden + 1) * rows, 128), jnp.float32)
 
     right = call(
         right_kernel,

time: 79.7 us -> 79.7 us (level)
  waiting for transfers between devices: 41.3 us -> 42.3 us
  Pallas kernels: 14.3 us -> 13.4 us
    ppermute x14, waiting for transfers between devices: 41.3 us -> 42.3 us  [exchange(): lax.ppermute(part, 'row', [(i, i ^ step) for i in range(devices)])]
    pallas_call x5, Pallas kernels: 14.3 us -> 13.4 us  [call(): pl.pallas_call(kernel, out_shape=out_shape, in_specs=specs, out_specs=jax...]
  transfers between devices with their start and end apart: 15 -> 15, of which waited for: 8 -> 8; matrix products, arithmetic and copies ran while one was open for 0% -> 0% of each run, Pallas kernels for 8% -> 7%
where the time goes in v6:
time: 79.7 us; the launch traced here: 79.5 us
  waiting for transfers between devices  42.3 us (53%)
  starting transfers between devices  23.6 us (30%)
  Pallas kernels  13.4 us (17%)
    ppermute x14, waiting for transfers between devices, exchange(): lax.ppermute(part, 'row', [(i, i ^ step) for i in range(devices)])  42.3 us
    ppermute x14, starting transfers between devices, exchange(): lax.ppermute(part, 'row', [(i, i ^ step) for i in range(devices)])  16.1 us
    pallas_call x5, Pallas kernels, call(): pl.pallas_call(kernel, out_shape=out_shape, in_specs=specs, out_specs=jax...  13.4 us
    all_to_all x1, starting transfers between devices, on_device(): lax.all_to_all(right, 'row', split_axis=0, concat_axis=0, tiled=True)  7.52 us
  transfers between devices with their start and end apart: 15, of which 8 were waited for; matrix products, arithmetic and copies ran while one was open for 0% of the time, Pallas kernels for 7%

profile of v6, /device:TPU:0, one launch (start us, length us, event | category | flops | bytes accessed | tf_op | source)
XLA Modules:
  0.0 79.5 jit_solution(13351850787424176457)
XLA Ops:
  0.0 4.8 %shard_map.65 = bf16[2,8,16,16,256]{4,3,2,1,0:T(8,128)(2,1)} custom-call(bf16[16,256,128]{2,1,0:T(8,128)(2,1)} %pair_ref.1, s32[16,256]{1,0:T(8,128)} %mask_ref.1, f32[1,128]{1,0:T(1,128)} %bitcast.3, bf16[128,512]{1,0:T(8,128)(2,1)} %proj_ref.4), custom_call_target="tpu_custom_call" | custom-call | flops 1000000000 | bytes 4000000 | tf_op jit(solution)/shard_map/pallas_call | solution.py:169
  4.8 0.0 copy-start.1
  4.8 0.0 copy-start.2
  4.8 0.0 copy-start.4
  4.8 0.0 copy-start.5
  4.8 7.5 %all-to-all-start = ((bf16[16,16,16,256]{3,2,1,0:T(8,128)(2,1)}), bf16[16,16,16,256]{3,2,1,0:T(8,128)(2,1)S(1)}, u32[]{:S(2)}, u32[]{:S(2)}) async-start(bf16[16,16,16,256]{3,2,1,0:T(8,128)(2,1)} %bitcast.6), calls=%async_computation | async-start | bytes 4194304 | tf_op jit(solution)/shard_map/all_to_all | solution.py:218
  12.4 0.0 copy-done.1
  12.4 0.0 copy-done.2
  12.4 0.0 copy-done.4
  12.4 0.0 copy-done.5
  12.4 2.2 %shard_map.66 = (bf16[16,16,256]{2,1,0:T(8,128)(2,1)S(1)}, bf16[16,16,256]{2,1,0:T(8,128)(2,1)S(1)}, bf16[16,16,256]{2,1,0:T(8,128)(2,1)S(1)}, bf16[16,16,256]{2...) custom-call(s32[1]{0:T(128)} %bitcast.me_ref, ...), custom_call_target="tpu_custom_call" | custom-call | flops 1000000000 | bytes 4000000 | tf_op jit(solution)/shard_map/pallas_call | solution.py:169
  14.7 0.0 copy-start.3
  14.7 0.5 collective-permute-start
  15.2 2.6 %collective-permute-start.1 = (bf16[16,16,256]{2,1,0:T(8,128)(2,1)S(1)}, bf16[16,16,256]{2,1,0:T(8,128)(2,1)S(1)}, u32[]{:S(2)}, u32[]{:S(2)}) collective-permute-start(bf16[16,16,256]{2,1,0:T(8,128)(2,1)S(1)} %get-tuple-element.23), channel_id=1, source_target_pairs={{0,6},{1,7},{2,4},{3,5},{4,2},{5,3},{6,0},{7,1},{8,14},{9,15},{10,... | collective-permute-start | bytes 393224 | tf_op jit(solution)/shard_map/ppermute | solution.py:184
  17.7 0.6 collective-permute-start.2
  18.3 0.4 collective-permute-start.3
  18.6 1.7 %collective-permute-start.4 = (bf16[16,16,256]{2,1,0:T(8,128)(2,1)S(1)}, bf16[16,16,256]{2,1,0:T(8,128)(2,1)S(1)}, u32[]{:S(2)}, u32[]{:S(2)}) collective-permute-start(bf16[16,16,256]{2,1,0:T(8,128)(2,1)S(1)} %get-tuple-element.26), channel_id=1, source_target_pairs={{0,7},{1,6},{2,5},{3,4},{4,3},{5,2},{6,1},{7,0},{8,15},{9,14},{10,... | collective-permute-start | bytes 393224 | tf_op jit(solution)/shard_map/ppermute | solution.py:184
  20.3 0.0 collective-permute-done.rest_1_
  20.3 1.2 %collective-permute-start.5 = (bf16[16,16,256]{2,1,0:T(8,128)(2,1)S(1)}, bf16[16,16,256]{2,1,0:T(8,128)(2,1)S(1)}, u32[]{:S(2)}, u32[]{:S(2)}) collective-permute-start(bf16[16,16,256]{2,1,0:T(8,128)(2,1)S(1)} %get-tuple-element.27), channel_id=1, source_target_pairs={{0,3},{1,2},{2,1},{3,0},{4,7},{5,6},{6,5},{7,4},{8,11},{9,10},{10,... | collective-permute-start | bytes 393224 | tf_op jit(solution)/shard_map/ppermute | solution.py:184
  21.5 29.7 %collective-permute-done.1.rest_2_ = bf16[16,16,256]{2,1,0:T(8,128)(2,1)S(1)} collective-permute-done((bf16[16,16,256]{2,1,0:T(8,128)(2,1)S(1)}, bf16[16,16,256]{2,1,0:T(8,128)(2,1)S(1)}, u32[]{:S(2)}, u32[]{:S(2)}) %collective-permute-start.1) | collective-permute-done | bytes 131104 | tf_op jit(solution)/shard_map/ppermute | solution.py:184
  51.2 2.1 %collective-permute-start.6 = (bf16[16,16,256]{2,1,0:T(8,128)(2,1)S(1)}, bf16[16,16,256]{2,1,0:T(8,128)(2,1)S(1)}, u32[]{:S(2)}, u32[]{:S(2)}) collective-permute-start(bf16[16,16,256]{2,1,0:T(8,128)(2,1)S(1)} %get-tuple-element.28), channel_id=1, source_target_pairs={{0,5},{1,4},{2,7},{3,6},{4,1},{5,0},{6,3},{7,2},{8,13},{9,12},{10,... | collective-permute-start | bytes 393224 | tf_op jit(solution)/shard_map/ppermute | solution.py:184
  53.3 0.0 collective-permute-done.2.rest_3_
  53.3 0.8 collective-permute-done.3.rest_4_
  54.0 4.2 %collective-permute-done.4.rest_5_ = bf16[16,16,256]{2,1,0:T(8,128)(2,1)S(1)} collective-permute-done((bf16[16,16,256]{2,1,0:T(8,128)(2,1)S(1)}, bf16[16,16,256]{2,1,0:T(8,128)(2,1)S(1)}, u32[]{:S(2)}, u32[]{:S(2)}) %collective-permute-start.4) | collective-permute-done | bytes 131104 | tf_op jit(solution)/shard_map/ppermute | solution.py:184
  58.2 0.0 collective-permute-done.5.rest_6_
  58.2 1.8 %collective-permute-done.6.rest_7_ = bf16[16,16,256]{2,1,0:T(8,128)(2,1)S(1)} collective-permute-done((bf16[16,16,256]{2,1,0:T(8,128)(2,1)S(1)}, bf16[16,16,256]{2,1,0:T(8,128)(2,1)S(1)}, u32[]{:S(2)}, u32[]{:S(2)}) %collective-permute-start.6) | collective-permute-done | bytes 131104 | tf_op jit(solution)/shard_map/ppermute | solution.py:184
  60.0 0.0 all-to-all-done.right_ref
  60.0 0.8 shard_map.67
  60.8 0.0 copy-start
  60.8 0.4 collective-permute-start.7
  61.2 3.7 %collective-permute-start.8 = (bf16[16,16,256]{2,1,0:T(8,128)(2,1)S(1)}, bf16[16,16,256]{2,1,0:T(8,128)(2,1)S(1)}, u32[]{:S(2)}, u32[]{:S(2)}) collective-permute-start(bf16[16,16,256]{2,1,0:T(8,128)(2,1)S(1)} %get-tuple-element.31), channel_id=1, source_target_pairs={{0,6},{1,7},{2,4},{3,5},{4,2},{5,3},{6,0},{7,1},{8,14},{9,15},{10,... | collective-permute-start | bytes 393224 | tf_op jit(solution)/shard_map/ppermute | solution.py:184
  64.9 0.0 collective-permute-start.9
  64.9 0.6 collective-permute-start.10
  65.4 1.9 %collective-permute-start.11 = (bf16[16,16,256]{2,1,0:T(8,128)(2,1)S(1)}, bf16[16,16,256]{2,1,0:T(8,128)(2,1)S(1)}, u32[]{:S(2)}, u32[]{:S(2)}) collective-permute-start(bf16[16,16,256]{2,1,0:T(8,128)(2,1)S(1)} %get-tuple-element.34), channel_id=1, source_target_pairs={{0,7},{1,6},{2,5},{3,4},{4,3},{5,2},{6,1},{7,0},{8,15},{9,14},{10,... | collective-permute-start | bytes 393224 | tf_op jit(solution)/shard_map/ppermute | solution.py:184
  67.3 0.0 collective-permute-done.7.rest_1_
  67.3 0.7 collective-permute-start.12
  68.1 0.8 collective-permute-done.8.rest_2_
  68.9 0.0 collective-permute-start.13
  68.9 0.0 copy-done.3
  68.9 3.2 %shard_map.64.gate_ref = f32[16,256,128]{2,1,0:T(8,128)S(1)} custom-call(bf16[16,256,128]{2,1,0:T(8,128)(2,1)} %pair_ref.1, f32[1,128]{1,0:T(1,128)S(1)} %bitcast.5, bf16[128,128]{1,0:T(8,128)(2,1)S(1)} %copy-done.3), custom_call_target="tpu_custom_call" | custom-call | flops 1000000000 | bytes 4000000 | tf_op jit(solution)/shard_map/pallas_call | solution.py:169
  72.0 0.8 %collective-permute-done.9.rest_3_ = bf16[16,16,256]{2,1,0:T(8,128)(2,1)S(1)} collective-permute-done((bf16[16,16,256]{2,1,0:T(8,128)(2,1)S(1)}, bf16[16,16,256]{2,1,0:T(8,128)(2,1)S(1)}, u32[]{:S(2)}, u32[]{:S(2)}) %collective-permute-start.9) | collective-permute-done | bytes 131104 | tf_op jit(solution)/shard_map/ppermute | solution.py:184
  72.8 0.0 collective-permute-done.10.rest_4_
  72.9 1.6 %collective-permute-done.11.rest_5_ = bf16[16,16,256]{2,1,0:T(8,128)(2,1)S(1)} collective-permute-done((bf16[16,16,256]{2,1,0:T(8,128)(2,1)S(1)}, bf16[16,16,256]{2,1,0:T(8,128)(2,1)S(1)}, u32[]{:S(2)}, u32[]{:S(2)}) %collective-permute-start.11) | collective-permute-done | bytes 131104 | tf_op jit(solution)/shard_map/ppermute | solution.py:184
  74.4 2.6 %collective-permute-done.12.rest_6_ = bf16[16,16,256]{2,1,0:T(8,128)(2,1)S(1)} collective-permute-done((bf16[16,16,256]{2,1,0:T(8,128)(2,1)S(1)}, bf16[16,16,256]{2,1,0:T(8,128)(2,1)S(1)}, u32[]{:S(2)}, u32[]{:S(2)}) %collective-permute-start.12) | collective-permute-done | bytes 131104 | tf_op jit(solution)/shard_map/ppermute | solution.py:184
  77.1 0.0 collective-permute-done.13.rest_7_
  77.1 0.0 copy-done
  77.1 2.4 %shard_map.68 = bf16[16,256,128]{2,1,0:T(8,128)(2,1)} custom-call(s32[1]{0:T(128)} %bitcast.me_ref, f32[16,256,128]{2,1,0:T(8,128)S(1)} %shard_map.64.gate_ref, bf16[128,128]{1,0:T(8,128)(2,1)S(1)} %copy-done, bf16[16,16,256]{2,1,0:T(8,128)(2,1)S(1)} %get-tuple-element.29.rest_0_, bf16[16,16,256]{2,1,0:T(8,128)(2,1)S(1)} %collective-permute-done.7.rest_1_, ...), custom_call_target="tpu_custom_call" | custom-call | flops 1000000000 | bytes 4000000 | tf_op jit(solution)/shard_map/pallas_call | solution.py:169
Async XLA Ops:
  4.8 7.6 %copy-start.1 = (bf16[16,256,128]{2,1,0:T(8,128)(2,1)S(1)}, bf16[16,256,128]{2,1,0:T(8,128)(2,1)}, u32[]{:S(2)}) copy-start(bf16[16,256,128]{2,1,0:T(8,128)(2,1)} %pair_ref.1) | copy-start | bytes 3145732
  4.8 7.6 %copy-start.2 = (bf16[128,512]{1,0:T(8,128)(2,1)S(1)}, bf16[128,512]{1,0:T(8,128)(2,1)}, u32[]{:S(2)}) copy-start(bf16[128,512]{1,0:T(8,128)(2,1)} %proj_ref.4) | copy-start | bytes 393220
  4.8 7.6 %copy-start.4 = (s32[16,256]{1,0:T(8,128)S(1)}, s32[16,256]{1,0:T(8,128)}, u32[]{:S(2)}) copy-start(s32[16,256]{1,0:T(8,128)} %mask_ref.1) | copy-start | bytes 49156
  4.8 7.6 %copy-start.5 = (f32[128]{0:T(128)S(1)}, f32[128]{0:T(128)}, u32[]{:S(2)}) copy-start(f32[128]{0:T(128)} %param.8) | copy-start | bytes 1540
  4.8 55.2 %all-to-all-start = ((bf16[16,16,16,256]{3,2,1,0:T(8,128)(2,1)}), bf16[16,16,16,256]{3,2,1,0:T(8,128)(2,1)S(1)}, u32[]{:S(2)}, u32[]{:S(2)}) async-start(bf16[16,16,16,256]{3,2,1,0:T(8,128)(2,1)} %bitcast.6), calls=%async_computation | async-start | bytes 4194304 | tf_op jit(solution)/shard_map/all_to_all | solution.py:218
  14.7 54.2 %copy-start.3 = (bf16[128,128]{1,0:T(8,128)(2,1)S(1)}, bf16[128,128]{1,0:T(8,128)(2,1)}, u32[]{:S(2)}) copy-start(bf16[128,128]{1,0:T(8,128)(2,1)} %proj_ref.3) | copy-start | bytes 98308
  14.7 5.7 %collective-permute-start = (bf16[16,16,256]{2,1,0:T(8,128)(2,1)S(1)}, bf16[16,16,256]{2,1,0:T(8,128)(2,1)S(1)}, u32[]{:S(2)}, u32[]{:S(2)}) collective-permute-start(bf16[16,16,256]{2,1,0:T(8,128)(2,1)S(1)} %get-tuple-element.22), channel_id=1, source_target_pairs={{0,1},{1,0},{2,3},{3,2},{4,5},{5,4},{6,7},{7,6},{8,9},{9,8},{10,11... | collective-permute-start | bytes 393224 | tf_op jit(solution)/shard_map/ppermute | solution.py:184
  15.2 36.1 %collective-permute-start.1 = (bf16[16,16,256]{2,1,0:T(8,128)(2,1)S(1)}, bf16[16,16,256]{2,1,0:T(8,128)(2,1)S(1)}, u32[]{:S(2)}, u32[]{:S(2)}) collective-permute-start(bf16[16,16,256]{2,1,0:T(8,128)(2,1)S(1)} %get-tuple-element.23), channel_id=1, source_target_pairs={{0,6},{1,7},{2,4},{3,5},{4,2},{5,3},{6,0},{7,1},{8,14},{9,15},{10,... | collective-permute-start | bytes 393224 | tf_op jit(solution)/shard_map/ppermute | solution.py:184
  17.7 35.5 %collective-permute-start.2 = (bf16[16,16,256]{2,1,0:T(8,128)(2,1)S(1)}, bf16[16,16,256]{2,1,0:T(8,128)(2,1)S(1)}, u32[]{:S(2)}, u32[]{:S(2)}) collective-permute-start(bf16[16,16,256]{2,1,0:T(8,128)(2,1)S(1)} %get-tuple-element.24), channel_id=1, source_target_pairs={{0,2},{1,3},{2,0},{3,1},{4,6},{5,7},{6,4},{7,5},{8,10},{9,11},{10,... | collective-permute-start | bytes 393224 | tf_op jit(solution)/shard_map/ppermute | solution.py:184
  18.3 35.7 %collective-permute-start.3 = (bf16[16,16,256]{2,1,0:T(8,128)(2,1)S(1)}, bf16[16,16,256]{2,1,0:T(8,128)(2,1)S(1)}, u32[]{:S(2)}, u32[]{:S(2)}) collective-permute-start(bf16[16,16,256]{2,1,0:T(8,128)(2,1)S(1)} %get-tuple-element.25), channel_id=1, source_target_pairs={{0,4},{1,5},{2,6},{3,7},{4,0},{5,1},{6,2},{7,3},{8,12},{9,13},{10,... | collective-permute-start | bytes 393224 | tf_op jit(solution)/shard_map/ppermute | solution.py:184
  18.6 39.6 %collective-permute-start.4 = (bf16[16,16,256]{2,1,0:T(8,128)(2,1)S(1)}, bf16[16,16,256]{2,1,0:T(8,128)(2,1)S(1)}, u32[]{:S(2)}, u32[]{:S(2)}) collective-permute-start(bf16[16,16,256]{2,1,0:T(8,128)(2,1)S(1)} %get-tuple-element.26), channel_id=1, source_target_pairs={{0,7},{1,6},{2,5},{3,4},{4,3},{5,2},{6,1},{7,0},{8,15},{9,14},{10,... | collective-permute-start | bytes 393224 | tf_op jit(solution)/shard_map/ppermute | solution.py:184
  20.3 37.9 %collective-permute-start.5 = (bf16[16,16,256]{2,1,0:T(8,128)(2,1)S(1)}, bf16[16,16,256]{2,1,0:T(8,128)(2,1)S(1)}, u32[]{:S(2)}, u32[]{:S(2)}) collective-permute-start(bf16[16,16,256]{2,1,0:T(8,128)(2,1)S(1)} %get-tuple-element.27), channel_id=1, source_target_pairs={{0,3},{1,2},{2,1},{3,0},{4,7},{5,6},{6,5},{7,4},{8,11},{9,10},{10,... | collective-permute-start | bytes 393224 | tf_op jit(solution)/shard_map/ppermute | solution.py:184
  51.2 8.8 %collective-permute-start.6 = (bf16[16,16,256]{2,1,0:T(8,128)(2,1)S(1)}, bf16[16,16,256]{2,1,0:T(8,128)(2,1)S(1)}, u32[]{:S(2)}, u32[]{:S(2)}) collective-permute-start(bf16[16,16,256]{2,1,0:T(8,128)(2,1)S(1)} %get-tuple-element.28), channel_id=1, source_target_pairs={{0,5},{1,4},{2,7},{3,6},{4,1},{5,0},{6,3},{7,2},{8,13},{9,12},{10,... | collective-permute-start | bytes 393224 | tf_op jit(solution)/shard_map/ppermute | solution.py:184
  60.8 16.3 %copy-start = (bf16[128,128]{1,0:T(8,128)(2,1)S(1)}, bf16[128,128]{1,0:T(8,128)(2,1)}, u32[]{:S(2)}) copy-start(bf16[128,128]{1,0:T(8,128)(2,1)} %proj_ref.5) | copy-start | bytes 98308
  60.8 6.5 %collective-permute-start.7 = (bf16[16,16,256]{2,1,0:T(8,128)(2,1)S(1)}, bf16[16,16,256]{2,1,0:T(8,128)(2,1)S(1)}, u32[]{:S(2)}, u32[]{:S(2)}) collective-permute-start(bf16[16,16,256]{2,1,0:T(8,128)(2,1)S(1)} %get-tuple-element.30), channel_id=1, source_target_pairs={{0,1},{1,0},{2,3},{3,2},{4,5},{5,4},{6,7},{7,6},{8,9},{9,8},{10,11... | collective-permute-start | bytes 393224 | tf_op jit(solution)/shard_map/ppermute | solution.py:184
  61.2 7.7 %collective-permute-start.8 = (bf16[16,16,256]{2,1,0:T(8,128)(2,1)S(1)}, bf16[16,16,256]{2,1,0:T(8,128)(2,1)S(1)}, u32[]{:S(2)}, u32[]{:S(2)}) collective-permute-start(bf16[16,16,256]{2,1,0:T(8,128)(2,1)S(1)} %get-tuple-element.31), channel_id=1, source_target_pairs={{0,6},{1,7},{2,4},{3,5},{4,2},{5,3},{6,0},{7,1},{8,14},{9,15},{10,... | collective-permute-start | bytes 393224 | tf_op jit(solution)/shard_map/ppermute | solution.py:184
  64.9 8.0 %collective-permute-start.9 = (bf16[16,16,256]{2,1,0:T(8,128)(2,1)S(1)}, bf16[16,16,256]{2,1,0:T(8,128)(2,1)S(1)}, u32[]{:S(2)}, u32[]{:S(2)}) collective-permute-start(bf16[16,16,256]{2,1,0:T(8,128)(2,1)S(1)} %get-tuple-element.32), channel_id=1, source_target_pairs={{0,2},{1,3},{2,0},{3,1},{4,6},{5,7},{6,4},{7,5},{8,10},{9,11},{10,... | collective-permute-start | bytes 393224 | tf_op jit(solution)/shard_map/ppermute | solution.py:184
  64.9 8.0 %collective-permute-start.10 = (bf16[16,16,256]{2,1,0:T(8,128)(2,1)S(1)}, bf16[16,16,256]{2,1,0:T(8,128)(2,1)S(1)}, u32[]{:S(2)}, u32[]{:S(2)}) collective-permute-start(bf16[16,16,256]{2,1,0:T(8,128)(2,1)S(1)} %get-tuple-element.33), channel_id=1, source_target_pairs={{0,4},{1,5},{2,6},{3,7},{4,0},{5,1},{6,2},{7,3},{8,12},{9,13},{10,... | collective-permute-start | bytes 393224 | tf_op jit(solution)/shard_map/ppermute | solution.py:184
  65.4 9.0 %collective-permute-start.11 = (bf16[16,16,256]{2,1,0:T(8,128)(2,1)S(1)}, bf16[16,16,256]{2,1,0:T(8,128)(2,1)S(1)}, u32[]{:S(2)}, u32[]{:S(2)}) collective-permute-start(bf16[16,16,256]{2,1,0:T(8,128)(2,1)S(1)} %get-tuple-element.34), channel_id=1, source_target_pairs={{0,7},{1,6},{2,5},{3,4},{4,3},{5,2},{6,1},{7,0},{8,15},{9,14},{10,... | collective-permute-start | bytes 393224 | tf_op jit(solution)/shard_map/ppermute | solution.py:184
  67.3 9.7 %collective-permute-start.12 = (bf16[16,16,256]{2,1,0:T(8,128)(2,1)S(1)}, bf16[16,16,256]{2,1,0:T(8,128)(2,1)S(1)}, u32[]{:S(2)}, u32[]{:S(2)}) collective-permute-start(bf16[16,16,256]{2,1,0:T(8,128)(2,1)S(1)} %get-tuple-element.35), channel_id=1, source_target_pairs={{0,3},{1,2},{2,1},{3,0},{4,7},{5,6},{6,5},{7,4},{8,11},{9,10},{10,... | collective-permute-start | bytes 393224 | tf_op jit(solution)/shard_map/ppermute | solution.py:184
  68.9 8.2 %collective-permute-start.13 = (bf16[16,16,256]{2,1,0:T(8,128)(2,1)S(1)}, bf16[16,16,256]{2,1,0:T(8,128)(2,1)S(1)}, u32[]{:S(2)}, u32[]{:S(2)}) collective-permute-start(bf16[16,16,256]{2,1,0:T(8,128)(2,1)S(1)} %get-tuple-element.36), channel_id=1, source_target_pairs={{0,5},{1,4},{2,7},{3,6},{4,1},{5,0},{6,3},{7,2},{8,13},{9,12},{10,... | collective-permute-start | bytes 393224 | tf_op jit(solution)/shard_map/ppermute | solution.py:184

commit v7 on v6

--- a/solution.py
+++ b/solution.py
@@ -22,9 +22,15 @@
     return 0.5 * jnp.tanh(0.5 * x) + 0.5
 
 
-def normed_rows(pair, gain):
+def normed_rows(pair, gain, mean_by_dot=False):
     x = pair.astype(jnp.float32)
-    centered = x - jnp.mean(x, axis=-1, keepdims=True)
+    if mean_by_dot:
+        width = pair.shape[1]
+        ones = jnp.full((width, width), 1 / width, jnp.bfloat16)
+        mean = jnp.dot(pair, ones, preferred_element_type=jnp.float32)
+    else:
+        mean = jnp.mean(x, axis=-1, keepdims=True)
+    centered = x - mean
     variance = jnp.mean(centered * centered, axis=-1, keepdims=True)
     return (centered * lax.rsqrt(variance + EPS) * gain).astype(jnp.bfloat16)
 
@@ -33,7 +39,7 @@
     rows = pair_ref.shape[0]
     hidden = weights.shape[0] // 2
     lanes = slice(t * 128, (t + 1) * 128)
-    normed = normed_rows(pair_ref[:, lanes].reshape(rows * 128, -1), gain)
+    normed = normed_rows(pair_ref[:, lanes].reshape(rows * 128, -1), gain, mean_by_dot=True)
     proj = lax.dot_general(weights, normed, OVER_LAST, preferred_element_type=jnp.float32)
     for r in range(rows):
         of_row = proj[:, r * 128 : (r + 1) * 128]

time: 79.7 us -> 79.3 us (level)
  no operation moved by 1% of the time
where the time goes in v7:
time: 79.3 us; the launch traced here: 79.1 us
  waiting for transfers between devices  42.5 us (54%)
  starting transfers between devices  23.7 us (30%)
  Pallas kernels  12.7 us (16%)
    ppermute x14, waiting for transfers between devices, exchange(): lax.ppermute(part, 'row', [(i, i ^ step) for i in range(devices)])  42.5 us
    ppermute x14, starting transfers between devices, exchange(): lax.ppermute(part, 'row', [(i, i ^ step) for i in range(devices)])  16.1 us
    pallas_call x5, Pallas kernels, call(): pl.pallas_call(kernel, out_shape=out_shape, in_specs=specs, out_specs=jax...  12.7 us
    all_to_all x1, starting transfers between devices, on_device(): lax.all_to_all(right, 'row', split_axis=0, concat_axis=0, tiled=True)  7.53 us
  transfers between devices with their start and end apart: 15, of which 8 were waited for; matrix products, arithmetic and copies ran while one was open for 0% of the time, Pallas kernels for 7%

profile of v7, /device:TPU:0, one launch (start us, length us, event | category | flops | bytes accessed | tf_op | source)
XLA Modules:
  0.0 79.1 jit_solution(6144438217478031708)
XLA Ops:
  0.0 4.4 %shard_map.65 = bf16[2,8,16,16,256]{4,3,2,1,0:T(8,128)(2,1)} custom-call(bf16[16,256,128]{2,1,0:T(8,128)(2,1)} %pair_ref.1, s32[16,256]{1,0:T(8,128)} %mask_ref.1, f32[1,128]{1,0:T(1,128)} %bitcast.3, bf16[128,512]{1,0:T(8,128)(2,1)} %proj_ref.4), custom_call_target="tpu_custom_call" | custom-call | flops 1000000000 | bytes 4000000 | tf_op jit(solution)/shard_map/pallas_call | solution.py:175
  4.4 0.0 copy-start.1
  4.4 0.0 copy-start.2
  4.4 0.0 copy-start.4
  4.4 0.0 copy-start.5
  4.5 7.5 %all-to-all-start = ((bf16[16,16,16,256]{3,2,1,0:T(8,128)(2,1)}), bf16[16,16,16,256]{3,2,1,0:T(8,128)(2,1)S(1)}, u32[]{:S(2)}, u32[]{:S(2)}) async-start(bf16[16,16,16,256]{3,2,1,0:T(8,128)(2,1)} %bitcast.6), calls=%async_computation | async-start | bytes 4194304 | tf_op jit(solution)/shard_map/all_to_all | solution.py:224
  12.0 0.0 copy-done.1
  12.0 0.0 copy-done.2
  12.0 0.0 copy-done.4
  12.0 0.0 copy-done.5
  12.0 2.0 %shard_map.66 = (bf16[16,16,256]{2,1,0:T(8,128)(2,1)S(1)}, bf16[16,16,256]{2,1,0:T(8,128)(2,1)S(1)}, bf16[16,16,256]{2,1,0:T(8,128)(2,1)S(1)}, bf16[16,16,256]{2...) custom-call(s32[1]{0:T(128)} %bitcast.me_ref, ...), custom_call_target="tpu_custom_call" | custom-call | flops 1000000000 | bytes 4000000 | tf_op jit(solution)/shard_map/pallas_call | solution.py:175
  14.0 0.0 copy-start.3
  14.0 0.5 collective-permute-start
  14.5 2.6 %collective-permute-start.1 = (bf16[16,16,256]{2,1,0:T(8,128)(2,1)S(1)}, bf16[16,16,256]{2,1,0:T(8,128)(2,1)S(1)}, u32[]{:S(2)}, u32[]{:S(2)}) collective-permute-start(bf16[16,16,256]{2,1,0:T(8,128)(2,1)S(1)} %get-tuple-element.23), channel_id=1, source_target_pairs={{0,6},{1,7},{2,4},{3,5},{4,2},{5,3},{6,0},{7,1},{8,14},{9,15},{10,... | collective-permute-start | bytes 393224 | tf_op jit(solution)/shard_map/ppermute | solution.py:190
  17.1 0.6 collective-permute-start.2
  17.6 0.3 collective-permute-start.3
  18.0 1.7 %collective-permute-start.4 = (bf16[16,16,256]{2,1,0:T(8,128)(2,1)S(1)}, bf16[16,16,256]{2,1,0:T(8,128)(2,1)S(1)}, u32[]{:S(2)}, u32[]{:S(2)}) collective-permute-start(bf16[16,16,256]{2,1,0:T(8,128)(2,1)S(1)} %get-tuple-element.26), channel_id=1, source_target_pairs={{0,7},{1,6},{2,5},{3,4},{4,3},{5,2},{6,1},{7,0},{8,15},{9,14},{10,... | collective-permute-start | bytes 393224 | tf_op jit(solution)/shard_map/ppermute | solution.py:190
  19.7 0.0 collective-permute-done.rest_1_
  19.7 1.2 %collective-permute-start.5 = (bf16[16,16,256]{2,1,0:T(8,128)(2,1)S(1)}, bf16[16,16,256]{2,1,0:T(8,128)(2,1)S(1)}, u32[]{:S(2)}, u32[]{:S(2)}) collective-permute-start(bf16[16,16,256]{2,1,0:T(8,128)(2,1)S(1)} %get-tuple-element.27), channel_id=1, source_target_pairs={{0,3},{1,2},{2,1},{3,0},{4,7},{5,6},{6,5},{7,4},{8,11},{9,10},{10,... | collective-permute-start | bytes 393224 | tf_op jit(solution)/shard_map/ppermute | solution.py:190
  20.9 30.0 %collective-permute-done.1.rest_2_ = bf16[16,16,256]{2,1,0:T(8,128)(2,1)S(1)} collective-permute-done((bf16[16,16,256]{2,1,0:T(8,128)(2,1)S(1)}, bf16[16,16,256]{2,1,0:T(8,128)(2,1)S(1)}, u32[]{:S(2)}, u32[]{:S(2)}) %collective-permute-start.1) | collective-permute-done | bytes 131104 | tf_op jit(solution)/shard_map/ppermute | solution.py:190
  50.8 2.1 %collective-permute-start.6 = (bf16[16,16,256]{2,1,0:T(8,128)(2,1)S(1)}, bf16[16,16,256]{2,1,0:T(8,128)(2,1)S(1)}, u32[]{:S(2)}, u32[]{:S(2)}) collective-permute-start(bf16[16,16,256]{2,1,0:T(8,128)(2,1)S(1)} %get-tuple-element.28), channel_id=1, source_target_pairs={{0,5},{1,4},{2,7},{3,6},{4,1},{5,0},{6,3},{7,2},{8,13},{9,12},{10,... | collective-permute-start | bytes 393224 | tf_op jit(solution)/shard_map/ppermute | solution.py:190
  52.9 0.0 collective-permute-done.2.rest_3_
  52.9 0.8 collective-permute-done.3.rest_4_
  53.6 4.2 %collective-permute-done.4.rest_5_ = bf16[16,16,256]{2,1,0:T(8,128)(2,1)S(1)} collective-permute-done((bf16[16,16,256]{2,1,0:T(8,128)(2,1)S(1)}, bf16[16,16,256]{2,1,0:T(8,128)(2,1)S(1)}, u32[]{:S(2)}, u32[]{:S(2)}) %collective-permute-start.4) | collective-permute-done | bytes 131104 | tf_op jit(solution)/shard_map/ppermute | solution.py:190
  57.8 0.0 collective-permute-done.5.rest_6_
  57.8 1.8 %collective-permute-done.6.rest_7_ = bf16[16,16,256]{2,1,0:T(8,128)(2,1)S(1)} collective-permute-done((bf16[16,16,256]{2,1,0:T(8,128)(2,1)S(1)}, bf16[16,16,256]{2,1,0:T(8,128)(2,1)S(1)}, u32[]{:S(2)}, u32[]{:S(2)}) %collective-permute-start.6) | collective-permute-done | bytes 131104 | tf_op jit(solution)/shard_map/ppermute | solution.py:190
  59.6 0.0 all-to-all-done.right_ref
  59.6 0.8 shard_map.67
  60.4 0.0 copy-start
  60.4 0.4 collective-permute-start.7
  60.8 3.7 %collective-permute-start.8 = (bf16[16,16,256]{2,1,0:T(8,128)(2,1)S(1)}, bf16[16,16,256]{2,1,0:T(8,128)(2,1)S(1)}, u32[]{:S(2)}, u32[]{:S(2)}) collective-permute-start(bf16[16,16,256]{2,1,0:T(8,128)(2,1)S(1)} %get-tuple-element.31), channel_id=1, source_target_pairs={{0,6},{1,7},{2,4},{3,5},{4,2},{5,3},{6,0},{7,1},{8,14},{9,15},{10,... | collective-permute-start | bytes 393224 | tf_op jit(solution)/shard_map/ppermute | solution.py:190
  64.5 0.0 collective-permute-start.9
  64.5 0.6 collective-permute-start.10
  65.0 1.9 %collective-permute-start.11 = (bf16[16,16,256]{2,1,0:T(8,128)(2,1)S(1)}, bf16[16,16,256]{2,1,0:T(8,128)(2,1)S(1)}, u32[]{:S(2)}, u32[]{:S(2)}) collective-permute-start(bf16[16,16,256]{2,1,0:T(8,128)(2,1)S(1)} %get-tuple-element.34), channel_id=1, source_target_pairs={{0,7},{1,6},{2,5},{3,4},{4,3},{5,2},{6,1},{7,0},{8,15},{9,14},{10,... | collective-permute-start | bytes 393224 | tf_op jit(solution)/shard_map/ppermute | solution.py:190
  66.9 0.0 collective-permute-done.7.rest_1_
  66.9 0.7 collective-permute-start.12
  67.7 0.8 collective-permute-done.8.rest_2_
  68.5 0.0 collective-permute-start.13
  68.5 0.0 copy-done.3
  68.5 3.2 %shard_map.64.gate_ref = f32[16,256,128]{2,1,0:T(8,128)S(1)} custom-call(bf16[16,256,128]{2,1,0:T(8,128)(2,1)} %pair_ref.1, f32[1,128]{1,0:T(1,128)S(1)} %bitcast.5, bf16[128,128]{1,0:T(8,128)(2,1)S(1)} %copy-done.3), custom_call_target="tpu_custom_call" | custom-call | flops 1000000000 | bytes 4000000 | tf_op jit(solution)/shard_map/pallas_call | solution.py:175
  71.7 0.8 %collective-permute-done.9.rest_3_ = bf16[16,16,256]{2,1,0:T(8,128)(2,1)S(1)} collective-permute-done((bf16[16,16,256]{2,1,0:T(8,128)(2,1)S(1)}, bf16[16,16,256]{2,1,0:T(8,128)(2,1)S(1)}, u32[]{:S(2)}, u32[]{:S(2)}) %collective-permute-start.9) | collective-permute-done | bytes 131104 | tf_op jit(solution)/shard_map/ppermute | solution.py:190
  72.5 0.0 collective-permute-done.10.rest_4_
  72.5 1.6 %collective-permute-done.11.rest_5_ = bf16[16,16,256]{2,1,0:T(8,128)(2,1)S(1)} collective-permute-done((bf16[16,16,256]{2,1,0:T(8,128)(2,1)S(1)}, bf16[16,16,256]{2,1,0:T(8,128)(2,1)S(1)}, u32[]{:S(2)}, u32[]{:S(2)}) %collective-permute-start.11) | collective-permute-done | bytes 131104 | tf_op jit(solution)/shard_map/ppermute | solution.py:190
  74.0 2.6 %collective-permute-done.12.rest_6_ = bf16[16,16,256]{2,1,0:T(8,128)(2,1)S(1)} collective-permute-done((bf16[16,16,256]{2,1,0:T(8,128)(2,1)S(1)}, bf16[16,16,256]{2,1,0:T(8,128)(2,1)S(1)}, u32[]{:S(2)}, u32[]{:S(2)}) %collective-permute-start.12) | collective-permute-done | bytes 131104 | tf_op jit(solution)/shard_map/ppermute | solution.py:190
  76.7 0.0 collective-permute-done.13.rest_7_
  76.7 0.0 copy-done
  76.7 2.4 %shard_map.68 = bf16[16,256,128]{2,1,0:T(8,128)(2,1)} custom-call(s32[1]{0:T(128)} %bitcast.me_ref, f32[16,256,128]{2,1,0:T(8,128)S(1)} %shard_map.64.gate_ref, bf16[128,128]{1,0:T(8,128)(2,1)S(1)} %copy-done, bf16[16,16,256]{2,1,0:T(8,128)(2,1)S(1)} %get-tuple-element.29.rest_0_, bf16[16,16,256]{2,1,0:T(8,128)(2,1)S(1)} %collective-permute-done.7.rest_1_, ...), custom_call_target="tpu_custom_call" | custom-call | flops 1000000000 | bytes 4000000 | tf_op jit(solution)/shard_map/pallas_call | solution.py:175
Async XLA Ops:
  4.4 7.6 %copy-start.1 = (bf16[16,256,128]{2,1,0:T(8,128)(2,1)S(1)}, bf16[16,256,128]{2,1,0:T(8,128)(2,1)}, u32[]{:S(2)}) copy-start(bf16[16,256,128]{2,1,0:T(8,128)(2,1)} %pair_ref.1) | copy-start | bytes 3145732
  4.4 7.6 %copy-start.2 = (bf16[128,512]{1,0:T(8,128)(2,1)S(1)}, bf16[128,512]{1,0:T(8,128)(2,1)}, u32[]{:S(2)}) copy-start(bf16[128,512]{1,0:T(8,128)(2,1)} %proj_ref.4) | copy-start | bytes 393220
  4.4 7.6 %copy-start.4 = (s32[16,256]{1,0:T(8,128)S(1)}, s32[16,256]{1,0:T(8,128)}, u32[]{:S(2)}) copy-start(s32[16,256]{1,0:T(8,128)} %mask_ref.1) | copy-start | bytes 49156
  4.4 7.6 %copy-start.5 = (f32[128]{0:T(128)S(1)}, f32[128]{0:T(128)}, u32[]{:S(2)}) copy-start(f32[128]{0:T(128)} %param.8) | copy-start | bytes 1540
  4.5 55.2 %all-to-all-start = ((bf16[16,16,16,256]{3,2,1,0:T(8,128)(2,1)}), bf16[16,16,16,256]{3,2,1,0:T(8,128)(2,1)S(1)}, u32[]{:S(2)}, u32[]{:S(2)}) async-start(bf16[16,16,16,256]{3,2,1,0:T(8,128)(2,1)} %bitcast.6), calls=%async_computation | async-start | bytes 4194304 | tf_op jit(solution)/shard_map/all_to_all | solution.py:224
  14.0 54.4 %copy-start.3 = (bf16[128,128]{1,0:T(8,128)(2,1)S(1)}, bf16[128,128]{1,0:T(8,128)(2,1)}, u32[]{:S(2)}) copy-start(bf16[128,128]{1,0:T(8,128)(2,1)} %proj_ref.3) | copy-start | bytes 98308
  14.0 5.7 %collective-permute-start = (bf16[16,16,256]{2,1,0:T(8,128)(2,1)S(1)}, bf16[16,16,256]{2,1,0:T(8,128)(2,1)S(1)}, u32[]{:S(2)}, u32[]{:S(2)}) collective-permute-start(bf16[16,16,256]{2,1,0:T(8,128)(2,1)S(1)} %get-tuple-element.22), channel_id=1, source_target_pairs={{0,1},{1,0},{2,3},{3,2},{4,5},{5,4},{6,7},{7,6},{8,9},{9,8},{10,11... | collective-permute-start | bytes 393224 | tf_op jit(solution)/shard_map/ppermute | solution.py:190
  14.5 36.3 %collective-permute-start.1 = (bf16[16,16,256]{2,1,0:T(8,128)(2,1)S(1)}, bf16[16,16,256]{2,1,0:T(8,128)(2,1)S(1)}, u32[]{:S(2)}, u32[]{:S(2)}) collective-permute-start(bf16[16,16,256]{2,1,0:T(8,128)(2,1)S(1)} %get-tuple-element.23), channel_id=1, source_target_pairs={{0,6},{1,7},{2,4},{3,5},{4,2},{5,3},{6,0},{7,1},{8,14},{9,15},{10,... | collective-permute-start | bytes 393224 | tf_op jit(solution)/shard_map/ppermute | solution.py:190
  17.1 35.8 %collective-permute-start.2 = (bf16[16,16,256]{2,1,0:T(8,128)(2,1)S(1)}, bf16[16,16,256]{2,1,0:T(8,128)(2,1)S(1)}, u32[]{:S(2)}, u32[]{:S(2)}) collective-permute-start(bf16[16,16,256]{2,1,0:T(8,128)(2,1)S(1)} %get-tuple-element.24), channel_id=1, source_target_pairs={{0,2},{1,3},{2,0},{3,1},{4,6},{5,7},{6,4},{7,5},{8,10},{9,11},{10,... | collective-permute-start | bytes 393224 | tf_op jit(solution)/shard_map/ppermute | solution.py:190
  17.6 36.0 %collective-permute-start.3 = (bf16[16,16,256]{2,1,0:T(8,128)(2,1)S(1)}, bf16[16,16,256]{2,1,0:T(8,128)(2,1)S(1)}, u32[]{:S(2)}, u32[]{:S(2)}) collective-permute-start(bf16[16,16,256]{2,1,0:T(8,128)(2,1)S(1)} %get-tuple-element.25), channel_id=1, source_target_pairs={{0,4},{1,5},{2,6},{3,7},{4,0},{5,1},{6,2},{7,3},{8,12},{9,13},{10,... | collective-permute-start | bytes 393224 | tf_op jit(solution)/shard_map/ppermute | solution.py:190
  18.0 39.8 %collective-permute-start.4 = (bf16[16,16,256]{2,1,0:T(8,128)(2,1)S(1)}, bf16[16,16,256]{2,1,0:T(8,128)(2,1)S(1)}, u32[]{:S(2)}, u32[]{:S(2)}) collective-permute-start(bf16[16,16,256]{2,1,0:T(8,128)(2,1)S(1)} %get-tuple-element.26), channel_id=1, source_target_pairs={{0,7},{1,6},{2,5},{3,4},{4,3},{5,2},{6,1},{7,0},{8,15},{9,14},{10,... | collective-permute-start | bytes 393224 | tf_op jit(solution)/shard_map/ppermute | solution.py:190
  19.7 38.1 %collective-permute-start.5 = (bf16[16,16,256]{2,1,0:T(8,128)(2,1)S(1)}, bf16[16,16,256]{2,1,0:T(8,128)(2,1)S(1)}, u32[]{:S(2)}, u32[]{:S(2)}) collective-permute-start(bf16[16,16,256]{2,1,0:T(8,128)(2,1)S(1)} %get-tuple-element.27), channel_id=1, source_target_pairs={{0,3},{1,2},{2,1},{3,0},{4,7},{5,6},{6,5},{7,4},{8,11},{9,10},{10,... | collective-permute-start | bytes 393224 | tf_op jit(solution)/shard_map/ppermute | solution.py:190
  50.8 8.8 %collective-permute-start.6 = (bf16[16,16,256]{2,1,0:T(8,128)(2,1)S(1)}, bf16[16,16,256]{2,1,0:T(8,128)(2,1)S(1)}, u32[]{:S(2)}, u32[]{:S(2)}) collective-permute-start(bf16[16,16,256]{2,1,0:T(8,128)(2,1)S(1)} %get-tuple-element.28), channel_id=1, source_target_pairs={{0,5},{1,4},{2,7},{3,6},{4,1},{5,0},{6,3},{7,2},{8,13},{9,12},{10,... | collective-permute-start | bytes 393224 | tf_op jit(solution)/shard_map/ppermute | solution.py:190
  60.4 16.3 %copy-start = (bf16[128,128]{1,0:T(8,128)(2,1)S(1)}, bf16[128,128]{1,0:T(8,128)(2,1)}, u32[]{:S(2)}) copy-start(bf16[128,128]{1,0:T(8,128)(2,1)} %proj_ref.5) | copy-start | bytes 98308
  60.4 6.5 %collective-permute-start.7 = (bf16[16,16,256]{2,1,0:T(8,128)(2,1)S(1)}, bf16[16,16,256]{2,1,0:T(8,128)(2,1)S(1)}, u32[]{:S(2)}, u32[]{:S(2)}) collective-permute-start(bf16[16,16,256]{2,1,0:T(8,128)(2,1)S(1)} %get-tuple-element.30), channel_id=1, source_target_pairs={{0,1},{1,0},{2,3},{3,2},{4,5},{5,4},{6,7},{7,6},{8,9},{9,8},{10,11... | collective-permute-start | bytes 393224 | tf_op jit(solution)/shard_map/ppermute | solution.py:190
  60.8 7.7 %collective-permute-start.8 = (bf16[16,16,256]{2,1,0:T(8,128)(2,1)S(1)}, bf16[16,16,256]{2,1,0:T(8,128)(2,1)S(1)}, u32[]{:S(2)}, u32[]{:S(2)}) collective-permute-start(bf16[16,16,256]{2,1,0:T(8,128)(2,1)S(1)} %get-tuple-element.31), channel_id=1, source_target_pairs={{0,6},{1,7},{2,4},{3,5},{4,2},{5,3},{6,0},{7,1},{8,14},{9,15},{10,... | collective-permute-start | bytes 393224 | tf_op jit(solution)/shard_map/ppermute | solution.py:190
  64.5 8.0 %collective-permute-start.9 = (bf16[16,16,256]{2,1,0:T(8,128)(2,1)S(1)}, bf16[16,16,256]{2,1,0:T(8,128)(2,1)S(1)}, u32[]{:S(2)}, u32[]{:S(2)}) collective-permute-start(bf16[16,16,256]{2,1,0:T(8,128)(2,1)S(1)} %get-tuple-element.32), channel_id=1, source_target_pairs={{0,2},{1,3},{2,0},{3,1},{4,6},{5,7},{6,4},{7,5},{8,10},{9,11},{10,... | collective-permute-start | bytes 393224 | tf_op jit(solution)/shard_map/ppermute | solution.py:190
  64.5 8.0 %collective-permute-start.10 = (bf16[16,16,256]{2,1,0:T(8,128)(2,1)S(1)}, bf16[16,16,256]{2,1,0:T(8,128)(2,1)S(1)}, u32[]{:S(2)}, u32[]{:S(2)}) collective-permute-start(bf16[16,16,256]{2,1,0:T(8,128)(2,1)S(1)} %get-tuple-element.33), channel_id=1, source_target_pairs={{0,4},{1,5},{2,6},{3,7},{4,0},{5,1},{6,2},{7,3},{8,12},{9,13},{10,... | collective-permute-start | bytes 393224 | tf_op jit(solution)/shard_map/ppermute | solution.py:190
  65.0 9.0 %collective-permute-start.11 = (bf16[16,16,256]{2,1,0:T(8,128)(2,1)S(1)}, bf16[16,16,256]{2,1,0:T(8,128)(2,1)S(1)}, u32[]{:S(2)}, u32[]{:S(2)}) collective-permute-start(bf16[16,16,256]{2,1,0:T(8,128)(2,1)S(1)} %get-tuple-element.34), channel_id=1, source_target_pairs={{0,7},{1,6},{2,5},{3,4},{4,3},{5,2},{6,1},{7,0},{8,15},{9,14},{10,... | collective-permute-start | bytes 393224 | tf_op jit(solution)/shard_map/ppermute | solution.py:190
  66.9 9.7 %collective-permute-start.12 = (bf16[16,16,256]{2,1,0:T(8,128)(2,1)S(1)}, bf16[16,16,256]{2,1,0:T(8,128)(2,1)S(1)}, u32[]{:S(2)}, u32[]{:S(2)}) collective-permute-start(bf16[16,16,256]{2,1,0:T(8,128)(2,1)S(1)} %get-tuple-element.35), channel_id=1, source_target_pairs={{0,3},{1,2},{2,1},{3,0},{4,7},{5,6},{6,5},{7,4},{8,11},{9,10},{10,... | collective-permute-start | bytes 393224 | tf_op jit(solution)/shard_map/ppermute | solution.py:190
  68.5 8.2 %collective-permute-start.13 = (bf16[16,16,256]{2,1,0:T(8,128)(2,1)S(1)}, bf16[16,16,256]{2,1,0:T(8,128)(2,1)S(1)}, u32[]{:S(2)}, u32[]{:S(2)}) collective-permute-start(bf16[16,16,256]{2,1,0:T(8,128)(2,1)S(1)} %get-tuple-element.36), channel_id=1, source_target_pairs={{0,5},{1,4},{2,7},{3,6},{4,1},{5,0},{6,3},{7,2},{8,13},{9,12},{10,... | collective-permute-start | bytes 393224 | tf_op jit(solution)/shard_map/ppermute | solution.py:190

commit v8 on v7

--- a/solution.py
+++ b/solution.py
@@ -15,7 +15,7 @@
 
 
 def steps_of(blocks):
-    return (0, 1, 6, 2, 4, 7, 3, 5) if blocks == 8 else tuple(range(blocks))
+    return (0, 6, 7, 2, 4, 3, 5, 1) if blocks == 8 else tuple(range(blocks))
 
 
 def sigmoid(x):
@@ -35,6 +35,11 @@
     return (centered * lax.rsqrt(variance + EPS) * gain).astype(jnp.bfloat16)
 
 
+def halved_gates(weights):
+    hidden = weights.shape[1] // 2
+    return jnp.concatenate([weights[:, :hidden], weights[:, hidden:] * 0.5], axis=1).T
+
+
 def gated(pair_ref, mask_ref, weights, gain, total, t):
     rows = pair_ref.shape[0]
     hidden = weights.shape[0] // 2
@@ -43,9 +48,9 @@
     proj = lax.dot_general(weights, normed, OVER_LAST, preferred_element_type=jnp.float32)
     for r in range(rows):
         of_row = proj[:, r * 128 : (r + 1) * 128]
-        keep = mask_ref[r : r + 1, lanes].astype(jnp.float32)
+        half_keep = 0.5 * mask_ref[r : r + 1, lanes].astype(jnp.float32)
         total[t, pl.ds(r, hidden, stride=rows), :] = (
-            keep * sigmoid(of_row[hidden:]) * of_row[:hidden]
+            (jnp.tanh(of_row[hidden:]) + 1.0) * (of_row[:hidden] * half_keep)
         )
 
 
@@ -74,7 +79,7 @@
         load.start()
     for load in small_loads:
         load.wait()
-    weights = weights_ref[...].T
+    weights = halved_gates(weights_ref[...])
     gain = gain_ref[...]
     stores = []
     for t in range(chunks):
@@ -99,7 +104,7 @@
     *out_refs, total = rest
     blocks = len(out_refs)
     group, rows, tokens = out_refs[0].shape
-    weights = proj_ref[:, : 2 * blocks * group].T
+    weights = halved_gates(proj_ref[:, : 2 * blocks * group])
     gain = gain_ref[...]
     for t in range(tokens // 128):
         gated(pair_ref, mask_ref, weights, gain, total, t)

time: 79.3 us -> 79 us (level); the launches traced: 79.1 us -> 77.8 us
  starting transfers between devices: 23.7 us -> 22.5 us
    ppermute x14, starting transfers between devices: 16.1 us -> 15 us  [exchange(): lax.ppermute(part, 'row', [(i, i ^ step) for i in range(devices)])]
where the time goes in v8:
time: 79 us; the launch traced here: 77.8 us
  waiting for transfers between devices  42.6 us (54%)
  starting transfers between devices  22.5 us (28%)
  Pallas kernels  12.5 us (16%)
    ppermute x14, waiting for transfers between devices, exchange(): lax.ppermute(part, 'row', [(i, i ^ step) for i in range(devices)])  42.6 us
    ppermute x14, starting transfers between devices, exchange(): lax.ppermute(part, 'row', [(i, i ^ step) for i in range(devices)])  15 us
    pallas_call x5, Pallas kernels, call(): pl.pallas_call(kernel, out_shape=out_shape, in_specs=specs, out_specs=jax...  12.5 us
    all_to_all x1, starting transfers between devices, on_device(): lax.all_to_all(right, 'row', split_axis=0, concat_axis=0, tiled=True)  7.53 us
  transfers between devices with their start and end apart: 15, of which 8 were waited for; matrix products, arithmetic and copies ran while one was open for 0% of the time, Pallas kernels for 7%

profile of v8, /device:TPU:0, one launch (start us, length us, event | category | flops | bytes accessed | tf_op | source)
XLA Modules:
  0.0 77.8 jit_solution(7457522715961299619)
XLA Ops:
  0.0 4.3 %shard_map.65 = bf16[2,8,16,16,256]{4,3,2,1,0:T(8,128)(2,1)} custom-call(bf16[16,256,128]{2,1,0:T(8,128)(2,1)} %pair_ref.1, s32[16,256]{1,0:T(8,128)} %mask_ref.1, f32[1,128]{1,0:T(1,128)} %bitcast.3, bf16[128,512]{1,0:T(8,128)(2,1)} %proj_ref.4), custom_call_target="tpu_custom_call" | custom-call | flops 1000000000 | bytes 4000000 | tf_op jit(solution)/shard_map/pallas_call | solution.py:180
  4.3 0.0 copy-start.1
  4.3 0.0 copy-start.2
  4.3 0.0 copy-start.4
  4.3 0.0 copy-start.5
  4.4 7.5 %all-to-all-start = ((bf16[16,16,16,256]{3,2,1,0:T(8,128)(2,1)}), bf16[16,16,16,256]{3,2,1,0:T(8,128)(2,1)S(1)}, u32[]{:S(2)}, u32[]{:S(2)}) async-start(bf16[16,16,16,256]{3,2,1,0:T(8,128)(2,1)} %bitcast.6), calls=%async_computation | async-start | bytes 4194304 | tf_op jit(solution)/shard_map/all_to_all | solution.py:229
  11.9 0.0 copy-done.1
  11.9 0.0 copy-done.2
  11.9 0.0 copy-done.4
  11.9 0.0 copy-done.5
  11.9 1.9 %shard_map.66 = (bf16[16,16,256]{2,1,0:T(8,128)(2,1)S(1)}, bf16[16,16,256]{2,1,0:T(8,128)(2,1)S(1)}, bf16[16,16,256]{2,1,0:T(8,128)(2,1)S(1)}, bf16[16,16,256]{2...) custom-call(s32[1]{0:T(128)} %bitcast.me_ref, ...), custom_call_target="tpu_custom_call" | custom-call | flops 1000000000 | bytes 4000000 | tf_op jit(solution)/shard_map/pallas_call | solution.py:180
  13.8 0.0 copy-start.3
  13.8 2.9 %collective-permute-start = (bf16[16,16,256]{2,1,0:T(8,128)(2,1)S(1)}, bf16[16,16,256]{2,1,0:T(8,128)(2,1)S(1)}, u32[]{:S(2)}, u32[]{:S(2)}) collective-permute-start(bf16[16,16,256]{2,1,0:T(8,128)(2,1)S(1)} %get-tuple-element.22), channel_id=1, source_target_pairs={{0,6},{1,7},{2,4},{3,5},{4,2},{5,3},{6,0},{7,1},{8,14},{9,15},{10,... | collective-permute-start | bytes 393224 | tf_op jit(solution)/shard_map/ppermute | solution.py:195
  16.7 0.0 collective-permute-start.1
  16.7 1.5 %collective-permute-start.2 = (bf16[16,16,256]{2,1,0:T(8,128)(2,1)S(1)}, bf16[16,16,256]{2,1,0:T(8,128)(2,1)S(1)}, u32[]{:S(2)}, u32[]{:S(2)}) collective-permute-start(bf16[16,16,256]{2,1,0:T(8,128)(2,1)S(1)} %get-tuple-element.24), channel_id=1, source_target_pairs={{0,2},{1,3},{2,0},{3,1},{4,6},{5,7},{6,4},{7,5},{8,10},{9,11},{10,... | collective-permute-start | bytes 393224 | tf_op jit(solution)/shard_map/ppermute | solution.py:195
  18.2 1.5 %collective-permute-start.3 = (bf16[16,16,256]{2,1,0:T(8,128)(2,1)S(1)}, bf16[16,16,256]{2,1,0:T(8,128)(2,1)S(1)}, u32[]{:S(2)}, u32[]{:S(2)}) collective-permute-start(bf16[16,16,256]{2,1,0:T(8,128)(2,1)S(1)} %get-tuple-element.25), channel_id=1, source_target_pairs={{0,4},{1,5},{2,6},{3,7},{4,0},{5,1},{6,2},{7,3},{8,12},{9,13},{10,... | collective-permute-start | bytes 393224 | tf_op jit(solution)/shard_map/ppermute | solution.py:195
  19.7 0.2 collective-permute-start.4
  19.9 30.8 %collective-permute-done.rest_1_ = bf16[16,16,256]{2,1,0:T(8,128)(2,1)S(1)} collective-permute-done((bf16[16,16,256]{2,1,0:T(8,128)(2,1)S(1)}, bf16[16,16,256]{2,1,0:T(8,128)(2,1)S(1)}, u32[]{:S(2)}, u32[]{:S(2)}) %collective-permute-start) | collective-permute-done | bytes 131104 | tf_op jit(solution)/shard_map/ppermute | solution.py:195
  50.7 2.1 %collective-permute-start.5 = (bf16[16,16,256]{2,1,0:T(8,128)(2,1)S(1)}, bf16[16,16,256]{2,1,0:T(8,128)(2,1)S(1)}, u32[]{:S(2)}, u32[]{:S(2)}) collective-permute-start(bf16[16,16,256]{2,1,0:T(8,128)(2,1)S(1)} %get-tuple-element.27), channel_id=1, source_target_pairs={{0,5},{1,4},{2,7},{3,6},{4,1},{5,0},{6,3},{7,2},{8,13},{9,12},{10,... | collective-permute-start | bytes 393224 | tf_op jit(solution)/shard_map/ppermute | solution.py:195
  52.8 0.8 collective-permute-done.1.rest_2_
  53.5 0.6 collective-permute-start.6
  54.1 0.0 collective-permute-done.2.rest_3_
  54.1 3.5 %collective-permute-done.3.rest_4_ = bf16[16,16,256]{2,1,0:T(8,128)(2,1)S(1)} collective-permute-done((bf16[16,16,256]{2,1,0:T(8,128)(2,1)S(1)}, bf16[16,16,256]{2,1,0:T(8,128)(2,1)S(1)}, u32[]{:S(2)}, u32[]{:S(2)}) %collective-permute-start.3) | collective-permute-done | bytes 131104 | tf_op jit(solution)/shard_map/ppermute | solution.py:195
  57.7 0.0 collective-permute-done.4.rest_5_
  57.7 1.9 %collective-permute-done.5.rest_6_ = bf16[16,16,256]{2,1,0:T(8,128)(2,1)S(1)} collective-permute-done((bf16[16,16,256]{2,1,0:T(8,128)(2,1)S(1)}, bf16[16,16,256]{2,1,0:T(8,128)(2,1)S(1)}, u32[]{:S(2)}, u32[]{:S(2)}) %collective-permute-start.5) | collective-permute-done | bytes 131104 | tf_op jit(solution)/shard_map/ppermute | solution.py:195
  59.5 0.0 collective-permute-done.6.rest_7_
  59.5 0.0 all-to-all-done.right_ref
  59.5 0.8 %shard_map.67 = (bf16[16,16,256]{2,1,0:T(8,128)(2,1)S(1)}, bf16[16,16,256]{2,1,0:T(8,128)(2,1)S(1)}, bf16[16,16,256]{2,1,0:T(8,128)(2,1)S(1)}, bf16[16,16,256]{2...) custom-call(bf16[16,16,16,256]{3,2,1,0:T(8,128)(2,1)S(1)} %all-to-al, ...), custom_call_target="tpu_custom_call" | custom-call | flops 1000000000 | bytes 4000000 | tf_op jit(solution)/shard_map/pallas_call | solution.py:180
  60.3 0.0 copy-start
  60.3 2.6 %collective-permute-start.7 = (bf16[16,16,256]{2,1,0:T(8,128)(2,1)S(1)}, bf16[16,16,256]{2,1,0:T(8,128)(2,1)S(1)}, u32[]{:S(2)}, u32[]{:S(2)}) collective-permute-start(bf16[16,16,256]{2,1,0:T(8,128)(2,1)S(1)} %get-tuple-element.30), channel_id=1, source_target_pairs={{0,6},{1,7},{2,4},{3,5},{4,2},{5,3},{6,0},{7,1},{8,14},{9,15},{10,... | collective-permute-start | bytes 393224 | tf_op jit(solution)/shard_map/ppermute | solution.py:195
  62.9 0.0 collective-permute-start.8
  63.0 1.5 %collective-permute-start.9 = (bf16[16,16,256]{2,1,0:T(8,128)(2,1)S(1)}, bf16[16,16,256]{2,1,0:T(8,128)(2,1)S(1)}, u32[]{:S(2)}, u32[]{:S(2)}) collective-permute-start(bf16[16,16,256]{2,1,0:T(8,128)(2,1)S(1)} %get-tuple-element.32), channel_id=1, source_target_pairs={{0,2},{1,3},{2,0},{3,1},{4,6},{5,7},{6,4},{7,5},{8,10},{9,11},{10,... | collective-permute-start | bytes 393224 | tf_op jit(solution)/shard_map/ppermute | solution.py:195
  64.5 1.5 %collective-permute-start.10 = (bf16[16,16,256]{2,1,0:T(8,128)(2,1)S(1)}, bf16[16,16,256]{2,1,0:T(8,128)(2,1)S(1)}, u32[]{:S(2)}, u32[]{:S(2)}) collective-permute-start(bf16[16,16,256]{2,1,0:T(8,128)(2,1)S(1)} %get-tuple-element.33), channel_id=1, source_target_pairs={{0,4},{1,5},{2,6},{3,7},{4,0},{5,1},{6,2},{7,3},{8,12},{9,13},{10,... | collective-permute-start | bytes 393224 | tf_op jit(solution)/shard_map/ppermute | solution.py:195
  66.1 0.2 collective-permute-start.11
  66.3 1.0 %collective-permute-done.7.rest_1_ = bf16[16,16,256]{2,1,0:T(8,128)(2,1)S(1)} collective-permute-done((bf16[16,16,256]{2,1,0:T(8,128)(2,1)S(1)}, bf16[16,16,256]{2,1,0:T(8,128)(2,1)S(1)}, u32[]{:S(2)}, u32[]{:S(2)}) %collective-permute-start.7) | collective-permute-done | bytes 131104 | tf_op jit(solution)/shard_map/ppermute | solution.py:195
  67.2 0.2 collective-permute-start.12
  67.5 2.3 %collective-permute-done.8.rest_2_ = bf16[16,16,256]{2,1,0:T(8,128)(2,1)S(1)} collective-permute-done((bf16[16,16,256]{2,1,0:T(8,128)(2,1)S(1)}, bf16[16,16,256]{2,1,0:T(8,128)(2,1)S(1)}, u32[]{:S(2)}, u32[]{:S(2)}) %collective-permute-start.8) | collective-permute-done | bytes 131104 | tf_op jit(solution)/shard_map/ppermute | solution.py:195
  69.8 0.1 collective-permute-start.13
  69.9 0.0 copy-done.3
  69.9 3.2 %shard_map.64.gate_ref = f32[16,256,128]{2,1,0:T(8,128)S(1)} custom-call(bf16[16,256,128]{2,1,0:T(8,128)(2,1)} %pair_ref.1, f32[1,128]{1,0:T(1,128)S(1)} %bitcast.5, bf16[128,128]{1,0:T(8,128)(2,1)S(1)} %copy-done.3), custom_call_target="tpu_custom_call" | custom-call | flops 1000000000 | bytes 4000000 | tf_op jit(solution)/shard_map/pallas_call | solution.py:180
  73.1 0.0 collective-permute-done.9.rest_3_
  73.1 0.3 collective-permute-done.10.rest_4_
  73.4 2.0 %collective-permute-done.11.rest_5_ = bf16[16,16,256]{2,1,0:T(8,128)(2,1)S(1)} collective-permute-done((bf16[16,16,256]{2,1,0:T(8,128)(2,1)S(1)}, bf16[16,16,256]{2,1,0:T(8,128)(2,1)S(1)}, u32[]{:S(2)}, u32[]{:S(2)}) %collective-permute-start.11) | collective-permute-done | bytes 131104 | tf_op jit(solution)/shard_map/ppermute | solution.py:195
  75.4 0.0 collective-permute-done.12.rest_6_
  75.4 0.0 collective-permute-done.13.rest_7_
  75.4 0.0 copy-done
  75.4 2.4 %shard_map.68 = bf16[16,256,128]{2,1,0:T(8,128)(2,1)} custom-call(s32[1]{0:T(128)} %bitcast.me_ref, f32[16,256,128]{2,1,0:T(8,128)S(1)} %shard_map.64.gate_ref, bf16[128,128]{1,0:T(8,128)(2,1)S(1)} %copy-done, bf16[16,16,256]{2,1,0:T(8,128)(2,1)S(1)} %get-tuple-element.29.rest_0_, bf16[16,16,256]{2,1,0:T(8,128)(2,1)S(1)} %collective-permute-done.7.rest_1_, ...), custom_call_target="tpu_custom_call" | custom-call | flops 1000000000 | bytes 4000000 | tf_op jit(solution)/shard_map/pallas_call | solution.py:180
Async XLA Ops:
  4.3 7.6 %copy-start.1 = (bf16[16,256,128]{2,1,0:T(8,128)(2,1)S(1)}, bf16[16,256,128]{2,1,0:T(8,128)(2,1)}, u32[]{:S(2)}) copy-start(bf16[16,256,128]{2,1,0:T(8,128)(2,1)} %pair_ref.1) | copy-start | bytes 3145732
  4.3 7.6 %copy-start.2 = (bf16[128,512]{1,0:T(8,128)(2,1)S(1)}, bf16[128,512]{1,0:T(8,128)(2,1)}, u32[]{:S(2)}) copy-start(bf16[128,512]{1,0:T(8,128)(2,1)} %proj_ref.4) | copy-start | bytes 393220
  4.3 7.6 %copy-start.4 = (s32[16,256]{1,0:T(8,128)S(1)}, s32[16,256]{1,0:T(8,128)}, u32[]{:S(2)}) copy-start(s32[16,256]{1,0:T(8,128)} %mask_ref.1) | copy-start | bytes 49156
  4.3 7.6 %copy-start.5 = (f32[128]{0:T(128)S(1)}, f32[128]{0:T(128)}, u32[]{:S(2)}) copy-start(f32[128]{0:T(128)} %param.8) | copy-start | bytes 1540
  4.4 55.2 %all-to-all-start = ((bf16[16,16,16,256]{3,2,1,0:T(8,128)(2,1)}), bf16[16,16,16,256]{3,2,1,0:T(8,128)(2,1)S(1)}, u32[]{:S(2)}, u32[]{:S(2)}) async-start(bf16[16,16,16,256]{3,2,1,0:T(8,128)(2,1)} %bitcast.6), calls=%async_computation | async-start | bytes 4194304 | tf_op jit(solution)/shard_map/all_to_all | solution.py:229
  13.8 56.0 %copy-start.3 = (bf16[128,128]{1,0:T(8,128)(2,1)S(1)}, bf16[128,128]{1,0:T(8,128)(2,1)}, u32[]{:S(2)}) copy-start(bf16[128,128]{1,0:T(8,128)(2,1)} %proj_ref.3) | copy-start | bytes 98308
  13.8 36.9 %collective-permute-start = (bf16[16,16,256]{2,1,0:T(8,128)(2,1)S(1)}, bf16[16,16,256]{2,1,0:T(8,128)(2,1)S(1)}, u32[]{:S(2)}, u32[]{:S(2)}) collective-permute-start(bf16[16,16,256]{2,1,0:T(8,128)(2,1)S(1)} %get-tuple-element.22), channel_id=1, source_target_pairs={{0,6},{1,7},{2,4},{3,5},{4,2},{5,3},{6,0},{7,1},{8,14},{9,15},{10,... | collective-permute-start | bytes 393224 | tf_op jit(solution)/shard_map/ppermute | solution.py:195
  16.7 36.8 %collective-permute-start.1 = (bf16[16,16,256]{2,1,0:T(8,128)(2,1)S(1)}, bf16[16,16,256]{2,1,0:T(8,128)(2,1)S(1)}, u32[]{:S(2)}, u32[]{:S(2)}) collective-permute-start(bf16[16,16,256]{2,1,0:T(8,128)(2,1)S(1)} %get-tuple-element.23), channel_id=1, source_target_pairs={{0,7},{1,6},{2,5},{3,4},{4,3},{5,2},{6,1},{7,0},{8,15},{9,14},{10,... | collective-permute-start | bytes 393224 | tf_op jit(solution)/shard_map/ppermute | solution.py:195
  16.7 37.4 %collective-permute-start.2 = (bf16[16,16,256]{2,1,0:T(8,128)(2,1)S(1)}, bf16[16,16,256]{2,1,0:T(8,128)(2,1)S(1)}, u32[]{:S(2)}, u32[]{:S(2)}) collective-permute-start(bf16[16,16,256]{2,1,0:T(8,128)(2,1)S(1)} %get-tuple-element.24), channel_id=1, source_target_pairs={{0,2},{1,3},{2,0},{3,1},{4,6},{5,7},{6,4},{7,5},{8,10},{9,11},{10,... | collective-permute-start | bytes 393224 | tf_op jit(solution)/shard_map/ppermute | solution.py:195
  18.2 39.4 %collective-permute-start.3 = (bf16[16,16,256]{2,1,0:T(8,128)(2,1)S(1)}, bf16[16,16,256]{2,1,0:T(8,128)(2,1)S(1)}, u32[]{:S(2)}, u32[]{:S(2)}) collective-permute-start(bf16[16,16,256]{2,1,0:T(8,128)(2,1)S(1)} %get-tuple-element.25), channel_id=1, source_target_pairs={{0,4},{1,5},{2,6},{3,7},{4,0},{5,1},{6,2},{7,3},{8,12},{9,13},{10,... | collective-permute-start | bytes 393224 | tf_op jit(solution)/shard_map/ppermute | solution.py:195
  19.7 38.0 %collective-permute-start.4 = (bf16[16,16,256]{2,1,0:T(8,128)(2,1)S(1)}, bf16[16,16,256]{2,1,0:T(8,128)(2,1)S(1)}, u32[]{:S(2)}, u32[]{:S(2)}) collective-permute-start(bf16[16,16,256]{2,1,0:T(8,128)(2,1)S(1)} %get-tuple-element.26), channel_id=1, source_target_pairs={{0,3},{1,2},{2,1},{3,0},{4,7},{5,6},{6,5},{7,4},{8,11},{9,10},{10,... | collective-permute-start | bytes 393224 | tf_op jit(solution)/shard_map/ppermute | solution.py:195
  50.7 8.8 %collective-permute-start.5 = (bf16[16,16,256]{2,1,0:T(8,128)(2,1)S(1)}, bf16[16,16,256]{2,1,0:T(8,128)(2,1)S(1)}, u32[]{:S(2)}, u32[]{:S(2)}) collective-permute-start(bf16[16,16,256]{2,1,0:T(8,128)(2,1)S(1)} %get-tuple-element.27), channel_id=1, source_target_pairs={{0,5},{1,4},{2,7},{3,6},{4,1},{5,0},{6,3},{7,2},{8,13},{9,12},{10,... | collective-permute-start | bytes 393224 | tf_op jit(solution)/shard_map/ppermute | solution.py:195
  53.5 6.0 %collective-permute-start.6 = (bf16[16,16,256]{2,1,0:T(8,128)(2,1)S(1)}, bf16[16,16,256]{2,1,0:T(8,128)(2,1)S(1)}, u32[]{:S(2)}, u32[]{:S(2)}) collective-permute-start(bf16[16,16,256]{2,1,0:T(8,128)(2,1)S(1)} %get-tuple-element.28), channel_id=1, source_target_pairs={{0,1},{1,0},{2,3},{3,2},{4,5},{5,4},{6,7},{7,6},{8,9},{9,8},{10,11... | collective-permute-start | bytes 393224 | tf_op jit(solution)/shard_map/ppermute | solution.py:195
  60.3 15.1 %copy-start = (bf16[128,128]{1,0:T(8,128)(2,1)S(1)}, bf16[128,128]{1,0:T(8,128)(2,1)}, u32[]{:S(2)}) copy-start(bf16[128,128]{1,0:T(8,128)(2,1)} %proj_ref.5) | copy-start | bytes 98308
  60.3 6.9 %collective-permute-start.7 = (bf16[16,16,256]{2,1,0:T(8,128)(2,1)S(1)}, bf16[16,16,256]{2,1,0:T(8,128)(2,1)S(1)}, u32[]{:S(2)}, u32[]{:S(2)}) collective-permute-start(bf16[16,16,256]{2,1,0:T(8,128)(2,1)S(1)} %get-tuple-element.30), channel_id=1, source_target_pairs={{0,6},{1,7},{2,4},{3,5},{4,2},{5,3},{6,0},{7,1},{8,14},{9,15},{10,... | collective-permute-start | bytes 393224 | tf_op jit(solution)/shard_map/ppermute | solution.py:195
  62.9 6.9 %collective-permute-start.8 = (bf16[16,16,256]{2,1,0:T(8,128)(2,1)S(1)}, bf16[16,16,256]{2,1,0:T(8,128)(2,1)S(1)}, u32[]{:S(2)}, u32[]{:S(2)}) collective-permute-start(bf16[16,16,256]{2,1,0:T(8,128)(2,1)S(1)} %get-tuple-element.31), channel_id=1, source_target_pairs={{0,7},{1,6},{2,5},{3,4},{4,3},{5,2},{6,1},{7,0},{8,15},{9,14},{10,... | collective-permute-start | bytes 393224 | tf_op jit(solution)/shard_map/ppermute | solution.py:195
  63.0 10.1 %collective-permute-start.9 = (bf16[16,16,256]{2,1,0:T(8,128)(2,1)S(1)}, bf16[16,16,256]{2,1,0:T(8,128)(2,1)S(1)}, u32[]{:S(2)}, u32[]{:S(2)}) collective-permute-start(bf16[16,16,256]{2,1,0:T(8,128)(2,1)S(1)} %get-tuple-element.32), channel_id=1, source_target_pairs={{0,2},{1,3},{2,0},{3,1},{4,6},{5,7},{6,4},{7,5},{8,10},{9,11},{10,... | collective-permute-start | bytes 393224 | tf_op jit(solution)/shard_map/ppermute | solution.py:195
  64.5 8.9 %collective-permute-start.10 = (bf16[16,16,256]{2,1,0:T(8,128)(2,1)S(1)}, bf16[16,16,256]{2,1,0:T(8,128)(2,1)S(1)}, u32[]{:S(2)}, u32[]{:S(2)}) collective-permute-start(bf16[16,16,256]{2,1,0:T(8,128)(2,1)S(1)} %get-tuple-element.33), channel_id=1, source_target_pairs={{0,4},{1,5},{2,6},{3,7},{4,0},{5,1},{6,2},{7,3},{8,12},{9,13},{10,... | collective-permute-start | bytes 393224 | tf_op jit(solution)/shard_map/ppermute | solution.py:195
  66.1 9.3 %collective-permute-start.11 = (bf16[16,16,256]{2,1,0:T(8,128)(2,1)S(1)}, bf16[16,16,256]{2,1,0:T(8,128)(2,1)S(1)}, u32[]{:S(2)}, u32[]{:S(2)}) collective-permute-start(bf16[16,16,256]{2,1,0:T(8,128)(2,1)S(1)} %get-tuple-element.34), channel_id=1, source_target_pairs={{0,3},{1,2},{2,1},{3,0},{4,7},{5,6},{6,5},{7,4},{8,11},{9,10},{10,... | collective-permute-start | bytes 393224 | tf_op jit(solution)/shard_map/ppermute | solution.py:195
  67.2 8.2 %collective-permute-start.12 = (bf16[16,16,256]{2,1,0:T(8,128)(2,1)S(1)}, bf16[16,16,256]{2,1,0:T(8,128)(2,1)S(1)}, u32[]{:S(2)}, u32[]{:S(2)}) collective-permute-start(bf16[16,16,256]{2,1,0:T(8,128)(2,1)S(1)} %get-tuple-element.35), channel_id=1, source_target_pairs={{0,5},{1,4},{2,7},{3,6},{4,1},{5,0},{6,3},{7,2},{8,13},{9,12},{10,... | collective-permute-start | bytes 393224 | tf_op jit(solution)/shard_map/ppermute | solution.py:195
  69.8 5.6 %collective-permute-start.13 = (bf16[16,16,256]{2,1,0:T(8,128)(2,1)S(1)}, bf16[16,16,256]{2,1,0:T(8,128)(2,1)S(1)}, u32[]{:S(2)}, u32[]{:S(2)}) collective-permute-start(bf16[16,16,256]{2,1,0:T(8,128)(2,1)S(1)} %get-tuple-element.36), channel_id=1, source_target_pairs={{0,1},{1,0},{2,3},{3,2},{4,5},{5,4},{6,7},{7,6},{8,9},{9,8},{10,11... | collective-permute-start | bytes 393224 | tf_op jit(solution)/shard_map/ppermute | solution.py:195

commit v9 on v8

--- a/solution.py
+++ b/solution.py
@@ -15,7 +15,11 @@
 
 
 def steps_of(blocks):
-    return (0, 6, 7, 2, 4, 3, 5, 1) if blocks == 8 else tuple(range(blocks))
+    return (0, 1, 6, 2, 4, 7, 3, 5) if blocks == 8 else tuple(range(blocks))
+
+
+def back_of(blocks):
+    return (0, 6, 2, 4, 3, 5, 7, 1) if blocks == 8 else tuple(range(blocks))
 
 
 def sigmoid(x):
@@ -123,8 +127,8 @@
         left = jnp.concatenate([ref[c] for ref in left_refs], axis=0)
         crossed = lax.dot_general(left, right, OVER_LAST, preferred_element_type=jnp.float32)
         crossed = crossed.astype(jnp.bfloat16).reshape(blocks, rows, sources * rows)
-        for s, out_ref in enumerate(out_refs):
-            out_ref[c] = crossed[s]
+        for step, out_ref in zip(back_of(blocks), out_refs):
+            out_ref[c] = crossed[steps_of(blocks).index(step)]
 
 
 def gate_kernel(pair_hbm, gain_ref, proj_ref, out_ref, pair_ref, sem):
@@ -156,7 +160,7 @@
         centered = x - jnp.mean(x, axis=0, keepdims=True)
         variance = jnp.mean(centered * centered, axis=0, keepdims=True)
         x = (centered * lax.rsqrt(variance + EPS)).reshape(len(crossed_refs), group * rows, 128)
-        for s, step in enumerate(steps_of(len(crossed_refs))):
+        for s, step in enumerate(back_of(len(crossed_refs))):
             owner = me_ref[0] ^ step
             first = pl.multiple_of(owner * (group * rows), group * rows)
             total[t, pl.ds(first, group * rows), :] = x[s]
@@ -190,7 +194,7 @@
     )(*operands)
 
 
-def exchange(parts, devices):
+def exchange(parts, devices, steps_of=steps_of):
     return [
         lax.ppermute(part, "row", [(i, i ^ step) for i in range(devices)]) if step else part
         for part, step in zip(parts, steps_of(len(parts)))
@@ -246,7 +250,7 @@
         tuple(sds((group, rows, devices * rows), bf16) for _ in range(blocks)),
         (right, *lefts),
     )
-    crossed = exchange(crossed, devices)
+    crossed = exchange(crossed, devices, back_of)
     return call(
         final_kernel,
         sds((rows, tokens, width), bf16),

time: 79 us -> 78.5 us (level); the launches traced: 77.8 us -> 78.2 us
  starting transfers between devices: 22.5 us -> 26.1 us
  waiting for transfers between devices: 42.6 us -> 39.3 us
    ppermute x14, starting transfers between devices: 15 us -> 18.6 us  [exchange(): lax.ppermute(part, 'row', [(i, i ^ step) for i in range(devices)])]
    ppermute x14, waiting for transfers between devices: 42.6 us -> 39.3 us  [exchange(): lax.ppermute(part, 'row', [(i, i ^ step) for i in range(devices)])]
  transfers between devices with their start and end apart: 15 -> 15, of which waited for: 8 -> 7; matrix products, arithmetic and copies ran while one was open for 0% -> 0% of each run, Pallas kernels for 7% -> 6%
where the time goes in v9:
time: 78.5 us; the launch traced here: 78.2 us
  waiting for transfers between devices  39.3 us (50%)
  starting transfers between devices  26.1 us (33%)
  Pallas kernels  12.5 us (16%)
    ppermute x14, waiting for transfers between devices, exchange(): lax.ppermute(part, 'row', [(i, i ^ step) for i in range(devices)])  39.3 us
    ppermute x14, starting transfers between devices, exchange(): lax.ppermute(part, 'row', [(i, i ^ step) for i in range(devices)])  18.6 us
    pallas_call x5, Pallas kernels, call(): pl.pallas_call(kernel, out_shape=out_shape, in_specs=specs, out_specs=jax...  12.5 us
    all_to_all x1, starting transfers between devices, on_device(): lax.all_to_all(right, 'row', split_axis=0, concat_axis=0, tiled=True)  7.53 us
  transfers between devices with their start and end apart: 15, of which 7 were waited for; matrix products, arithmetic and copies ran while one was open for 0% of the time, Pallas kernels for 6%

profile of v9, /device:TPU:0, one launch (start us, length us, event | category | flops | bytes accessed | tf_op | source)
XLA Modules:
  0.0 78.2 jit_solution(10538259914501014973)
XLA Ops:
  0.0 4.3 %shard_map.65 = bf16[2,8,16,16,256]{4,3,2,1,0:T(8,128)(2,1)} custom-call(bf16[16,256,128]{2,1,0:T(8,128)(2,1)} %pair_ref.1, s32[16,256]{1,0:T(8,128)} %mask_ref.1, f32[1,128]{1,0:T(1,128)} %bitcast.3, bf16[128,512]{1,0:T(8,128)(2,1)} %proj_ref.4), custom_call_target="tpu_custom_call" | custom-call | flops 1000000000 | bytes 4000000 | tf_op jit(solution)/shard_map/pallas_call | solution.py:184
  4.3 0.0 copy-start.1
  4.3 0.0 copy-start.2
  4.3 0.0 copy-start.4
  4.3 0.0 copy-start.5
  4.4 7.5 %all-to-all-start = ((bf16[16,16,16,256]{3,2,1,0:T(8,128)(2,1)}), bf16[16,16,16,256]{3,2,1,0:T(8,128)(2,1)S(1)}, u32[]{:S(2)}, u32[]{:S(2)}) async-start(bf16[16,16,16,256]{3,2,1,0:T(8,128)(2,1)} %bitcast.6), calls=%async_computation | async-start | bytes 4194304 | tf_op jit(solution)/shard_map/all_to_all | solution.py:233
  11.9 0.0 copy-done.1
  11.9 0.0 copy-done.2
  11.9 0.0 copy-done.4
  11.9 0.0 copy-done.5
  11.9 1.9 %shard_map.66 = (bf16[16,16,256]{2,1,0:T(8,128)(2,1)S(1)}, bf16[16,16,256]{2,1,0:T(8,128)(2,1)S(1)}, bf16[16,16,256]{2,1,0:T(8,128)(2,1)S(1)}, bf16[16,16,256]{2...) custom-call(s32[1]{0:T(128)} %bitcast.me_ref, ...), custom_call_target="tpu_custom_call" | custom-call | flops 1000000000 | bytes 4000000 | tf_op jit(solution)/shard_map/pallas_call | solution.py:184
  13.8 0.0 copy-start.3
  13.8 0.5 collective-permute-start
  14.3 2.6 %collective-permute-start.1 = (bf16[16,16,256]{2,1,0:T(8,128)(2,1)S(1)}, bf16[16,16,256]{2,1,0:T(8,128)(2,1)S(1)}, u32[]{:S(2)}, u32[]{:S(2)}) collective-permute-start(bf16[16,16,256]{2,1,0:T(8,128)(2,1)S(1)} %get-tuple-element.23), channel_id=1, source_target_pairs={{0,6},{1,7},{2,4},{3,5},{4,2},{5,3},{6,0},{7,1},{8,14},{9,15},{10,... | collective-permute-start | bytes 393224 | tf_op jit(solution)/shard_map/ppermute | solution.py:199
  16.9 0.6 collective-permute-start.2
  17.5 0.3 collective-permute-start.3
  17.8 1.7 %collective-permute-start.4 = (bf16[16,16,256]{2,1,0:T(8,128)(2,1)S(1)}, bf16[16,16,256]{2,1,0:T(8,128)(2,1)S(1)}, u32[]{:S(2)}, u32[]{:S(2)}) collective-permute-start(bf16[16,16,256]{2,1,0:T(8,128)(2,1)S(1)} %get-tuple-element.26), channel_id=1, source_target_pairs={{0,7},{1,6},{2,5},{3,4},{4,3},{5,2},{6,1},{7,0},{8,15},{9,14},{10,... | collective-permute-start | bytes 393224 | tf_op jit(solution)/shard_map/ppermute | solution.py:199
  19.5 0.0 collective-permute-done.rest_1_
  19.5 1.2 %collective-permute-start.5 = (bf16[16,16,256]{2,1,0:T(8,128)(2,1)S(1)}, bf16[16,16,256]{2,1,0:T(8,128)(2,1)S(1)}, u32[]{:S(2)}, u32[]{:S(2)}) collective-permute-start(bf16[16,16,256]{2,1,0:T(8,128)(2,1)S(1)} %get-tuple-element.27), channel_id=1, source_target_pairs={{0,3},{1,2},{2,1},{3,0},{4,7},{5,6},{6,5},{7,4},{8,11},{9,10},{10,... | collective-permute-start | bytes 393224 | tf_op jit(solution)/shard_map/ppermute | solution.py:199
  20.7 30.1 %collective-permute-done.1.rest_2_ = bf16[16,16,256]{2,1,0:T(8,128)(2,1)S(1)} collective-permute-done((bf16[16,16,256]{2,1,0:T(8,128)(2,1)S(1)}, bf16[16,16,256]{2,1,0:T(8,128)(2,1)S(1)}, u32[]{:S(2)}, u32[]{:S(2)}) %collective-permute-start.1) | collective-permute-done | bytes 131104 | tf_op jit(solution)/shard_map/ppermute | solution.py:199
  50.7 2.1 %collective-permute-start.6 = (bf16[16,16,256]{2,1,0:T(8,128)(2,1)S(1)}, bf16[16,16,256]{2,1,0:T(8,128)(2,1)S(1)}, u32[]{:S(2)}, u32[]{:S(2)}) collective-permute-start(bf16[16,16,256]{2,1,0:T(8,128)(2,1)S(1)} %get-tuple-element.28), channel_id=1, source_target_pairs={{0,5},{1,4},{2,7},{3,6},{4,1},{5,0},{6,3},{7,2},{8,13},{9,12},{10,... | collective-permute-start | bytes 393224 | tf_op jit(solution)/shard_map/ppermute | solution.py:199
  52.8 0.0 collective-permute-done.2.rest_3_
  52.8 0.8 collective-permute-done.3.rest_4_
  53.5 4.2 %collective-permute-done.4.rest_5_ = bf16[16,16,256]{2,1,0:T(8,128)(2,1)S(1)} collective-permute-done((bf16[16,16,256]{2,1,0:T(8,128)(2,1)S(1)}, bf16[16,16,256]{2,1,0:T(8,128)(2,1)S(1)}, u32[]{:S(2)}, u32[]{:S(2)}) %collective-permute-start.4) | collective-permute-done | bytes 131104 | tf_op jit(solution)/shard_map/ppermute | solution.py:199
  57.7 0.0 collective-permute-done.5.rest_6_
  57.7 1.8 %collective-permute-done.6.rest_7_ = bf16[16,16,256]{2,1,0:T(8,128)(2,1)S(1)} collective-permute-done((bf16[16,16,256]{2,1,0:T(8,128)(2,1)S(1)}, bf16[16,16,256]{2,1,0:T(8,128)(2,1)S(1)}, u32[]{:S(2)}, u32[]{:S(2)}) %collective-permute-start.6) | collective-permute-done | bytes 131104 | tf_op jit(solution)/shard_map/ppermute | solution.py:199
  59.5 0.0 all-to-all-done.right_ref
  59.5 0.8 %shard_map.67 = (bf16[16,16,256]{2,1,0:T(8,128)(2,1)S(1)}, bf16[16,16,256]{2,1,0:T(8,128)(2,1)S(1)}, bf16[16,16,256]{2,1,0:T(8,128)(2,1)S(1)}, bf16[16,16,256]{2...) custom-call(bf16[16,16,16,256]{3,2,1,0:T(8,128)(2,1)S(1)} %all-to-al, ...), custom_call_target="tpu_custom_call" | custom-call | flops 1000000000 | bytes 4000000 | tf_op jit(solution)/shard_map/pallas_call | solution.py:184
  60.3 0.0 copy-start
  60.3 3.8 %collective-permute-start.7 = (bf16[16,16,256]{2,1,0:T(8,128)(2,1)S(1)}, bf16[16,16,256]{2,1,0:T(8,128)(2,1)S(1)}, u32[]{:S(2)}, u32[]{:S(2)}) collective-permute-start(bf16[16,16,256]{2,1,0:T(8,128)(2,1)S(1)} %get-tuple-element.30), channel_id=1, source_target_pairs={{0,6},{1,7},{2,4},{3,5},{4,2},{5,3},{6,0},{7,1},{8,14},{9,15},{10,... | collective-permute-start | bytes 393224 | tf_op jit(solution)/shard_map/ppermute | solution.py:199
  64.1 0.0 collective-permute-start.8
  64.1 0.6 collective-permute-start.9
  64.7 0.7 collective-permute-start.10
  65.5 2.4 %collective-permute-start.11 = (bf16[16,16,256]{2,1,0:T(8,128)(2,1)S(1)}, bf16[16,16,256]{2,1,0:T(8,128)(2,1)S(1)}, u32[]{:S(2)}, u32[]{:S(2)}) collective-permute-start(bf16[16,16,256]{2,1,0:T(8,128)(2,1)S(1)} %get-tuple-element.34), channel_id=1, source_target_pairs={{0,5},{1,4},{2,7},{3,6},{4,1},{5,0},{6,3},{7,2},{8,13},{9,12},{10,... | collective-permute-start | bytes 393224 | tf_op jit(solution)/shard_map/ppermute | solution.py:199
  67.9 0.3 collective-permute-done.7.rest_1_
  68.2 1.7 %collective-permute-start.12 = (bf16[16,16,256]{2,1,0:T(8,128)(2,1)S(1)}, bf16[16,16,256]{2,1,0:T(8,128)(2,1)S(1)}, u32[]{:S(2)}, u32[]{:S(2)}) collective-permute-start(bf16[16,16,256]{2,1,0:T(8,128)(2,1)S(1)} %get-tuple-element.35), channel_id=1, source_target_pairs={{0,7},{1,6},{2,5},{3,4},{4,3},{5,2},{6,1},{7,0},{8,15},{9,14},{10,... | collective-permute-start | bytes 393224 | tf_op jit(solution)/shard_map/ppermute | solution.py:199
  69.8 1.1 %collective-permute-done.8.rest_2_ = bf16[16,16,256]{2,1,0:T(8,128)(2,1)S(1)} collective-permute-done((bf16[16,16,256]{2,1,0:T(8,128)(2,1)S(1)}, bf16[16,16,256]{2,1,0:T(8,128)(2,1)S(1)}, u32[]{:S(2)}, u32[]{:S(2)}) %collective-permute-start.8) | collective-permute-done | bytes 131104 | tf_op jit(solution)/shard_map/ppermute | solution.py:199
  70.9 0.5 collective-permute-start.13
  71.5 0.0 copy-done.3
  71.5 3.2 %shard_map.64.gate_ref = f32[16,256,128]{2,1,0:T(8,128)S(1)} custom-call(bf16[16,256,128]{2,1,0:T(8,128)(2,1)} %pair_ref.1, f32[1,128]{1,0:T(1,128)S(1)} %bitcast.5, bf16[128,128]{1,0:T(8,128)(2,1)S(1)} %copy-done.3), custom_call_target="tpu_custom_call" | custom-call | flops 1000000000 | bytes 4000000 | tf_op jit(solution)/shard_map/pallas_call | solution.py:184
  74.7 0.0 collective-permute-done.9.rest_3_
  74.7 0.0 collective-permute-done.10.rest_4_
  74.7 0.0 collective-permute-done.11.rest_5_
  74.7 1.1 %collective-permute-done.12.rest_6_ = bf16[16,16,256]{2,1,0:T(8,128)(2,1)S(1)} collective-permute-done((bf16[16,16,256]{2,1,0:T(8,128)(2,1)S(1)}, bf16[16,16,256]{2,1,0:T(8,128)(2,1)S(1)}, u32[]{:S(2)}, u32[]{:S(2)}) %collective-permute-start.12) | collective-permute-done | bytes 131104 | tf_op jit(solution)/shard_map/ppermute | solution.py:199
  75.8 0.0 collective-permute-done.13.rest_7_
  75.8 0.0 copy-done
  75.8 2.4 %shard_map.68 = bf16[16,256,128]{2,1,0:T(8,128)(2,1)} custom-call(s32[1]{0:T(128)} %bitcast.me_ref, f32[16,256,128]{2,1,0:T(8,128)S(1)} %shard_map.64.gate_ref, bf16[128,128]{1,0:T(8,128)(2,1)S(1)} %copy-done, bf16[16,16,256]{2,1,0:T(8,128)(2,1)S(1)} %get-tuple-element.29.rest_0_, bf16[16,16,256]{2,1,0:T(8,128)(2,1)S(1)} %collective-permute-done.7.rest_1_, ...), custom_call_target="tpu_custom_call" | custom-call | flops 1000000000 | bytes 4000000 | tf_op jit(solution)/shard_map/pallas_call | solution.py:184
Async XLA Ops:
  4.3 7.6 %copy-start.1 = (bf16[16,256,128]{2,1,0:T(8,128)(2,1)S(1)}, bf16[16,256,128]{2,1,0:T(8,128)(2,1)}, u32[]{:S(2)}) copy-start(bf16[16,256,128]{2,1,0:T(8,128)(2,1)} %pair_ref.1) | copy-start | bytes 3145732
  4.3 7.6 %copy-start.2 = (bf16[128,512]{1,0:T(8,128)(2,1)S(1)}, bf16[128,512]{1,0:T(8,128)(2,1)}, u32[]{:S(2)}) copy-start(bf16[128,512]{1,0:T(8,128)(2,1)} %proj_ref.4) | copy-start | bytes 393220
  4.3 7.6 %copy-start.4 = (s32[16,256]{1,0:T(8,128)S(1)}, s32[16,256]{1,0:T(8,128)}, u32[]{:S(2)}) copy-start(s32[16,256]{1,0:T(8,128)} %mask_ref.1) | copy-start | bytes 49156
  4.3 7.6 %copy-start.5 = (f32[128]{0:T(128)S(1)}, f32[128]{0:T(128)}, u32[]{:S(2)}) copy-start(f32[128]{0:T(128)} %param.8) | copy-start | bytes 1540
  4.4 55.2 %all-to-all-start = ((bf16[16,16,16,256]{3,2,1,0:T(8,128)(2,1)}), bf16[16,16,16,256]{3,2,1,0:T(8,128)(2,1)S(1)}, u32[]{:S(2)}, u32[]{:S(2)}) async-start(bf16[16,16,16,256]{3,2,1,0:T(8,128)(2,1)} %bitcast.6), calls=%async_computation | async-start | bytes 4194304 | tf_op jit(solution)/shard_map/all_to_all | solution.py:233
  13.8 57.6 %copy-start.3 = (bf16[128,128]{1,0:T(8,128)(2,1)S(1)}, bf16[128,128]{1,0:T(8,128)(2,1)}, u32[]{:S(2)}) copy-start(bf16[128,128]{1,0:T(8,128)(2,1)} %proj_ref.3) | copy-start | bytes 98308
  13.8 5.7 %collective-permute-start = (bf16[16,16,256]{2,1,0:T(8,128)(2,1)S(1)}, bf16[16,16,256]{2,1,0:T(8,128)(2,1)S(1)}, u32[]{:S(2)}, u32[]{:S(2)}) collective-permute-start(bf16[16,16,256]{2,1,0:T(8,128)(2,1)S(1)} %get-tuple-element.22), channel_id=1, source_target_pairs={{0,1},{1,0},{2,3},{3,2},{4,5},{5,4},{6,7},{7,6},{8,9},{9,8},{10,11... | collective-permute-start | bytes 393224 | tf_op jit(solution)/shard_map/ppermute | solution.py:199
  14.3 36.4 %collective-permute-start.1 = (bf16[16,16,256]{2,1,0:T(8,128)(2,1)S(1)}, bf16[16,16,256]{2,1,0:T(8,128)(2,1)S(1)}, u32[]{:S(2)}, u32[]{:S(2)}) collective-permute-start(bf16[16,16,256]{2,1,0:T(8,128)(2,1)S(1)} %get-tuple-element.23), channel_id=1, source_target_pairs={{0,6},{1,7},{2,4},{3,5},{4,2},{5,3},{6,0},{7,1},{8,14},{9,15},{10,... | collective-permute-start | bytes 393224 | tf_op jit(solution)/shard_map/ppermute | solution.py:199
  16.9 35.9 %collective-permute-start.2 = (bf16[16,16,256]{2,1,0:T(8,128)(2,1)S(1)}, bf16[16,16,256]{2,1,0:T(8,128)(2,1)S(1)}, u32[]{:S(2)}, u32[]{:S(2)}) collective-permute-start(bf16[16,16,256]{2,1,0:T(8,128)(2,1)S(1)} %get-tuple-element.24), channel_id=1, source_target_pairs={{0,2},{1,3},{2,0},{3,1},{4,6},{5,7},{6,4},{7,5},{8,10},{9,11},{10,... | collective-permute-start | bytes 393224 | tf_op jit(solution)/shard_map/ppermute | solution.py:199
  17.5 36.1 %collective-permute-start.3 = (bf16[16,16,256]{2,1,0:T(8,128)(2,1)S(1)}, bf16[16,16,256]{2,1,0:T(8,128)(2,1)S(1)}, u32[]{:S(2)}, u32[]{:S(2)}) collective-permute-start(bf16[16,16,256]{2,1,0:T(8,128)(2,1)S(1)} %get-tuple-element.25), channel_id=1, source_target_pairs={{0,4},{1,5},{2,6},{3,7},{4,0},{5,1},{6,2},{7,3},{8,12},{9,13},{10,... | collective-permute-start | bytes 393224 | tf_op jit(solution)/shard_map/ppermute | solution.py:199
  17.8 39.9 %collective-permute-start.4 = (bf16[16,16,256]{2,1,0:T(8,128)(2,1)S(1)}, bf16[16,16,256]{2,1,0:T(8,128)(2,1)S(1)}, u32[]{:S(2)}, u32[]{:S(2)}) collective-permute-start(bf16[16,16,256]{2,1,0:T(8,128)(2,1)S(1)} %get-tuple-element.26), channel_id=1, source_target_pairs={{0,7},{1,6},{2,5},{3,4},{4,3},{5,2},{6,1},{7,0},{8,15},{9,14},{10,... | collective-permute-start | bytes 393224 | tf_op jit(solution)/shard_map/ppermute | solution.py:199
  19.5 38.2 %collective-permute-start.5 = (bf16[16,16,256]{2,1,0:T(8,128)(2,1)S(1)}, bf16[16,16,256]{2,1,0:T(8,128)(2,1)S(1)}, u32[]{:S(2)}, u32[]{:S(2)}) collective-permute-start(bf16[16,16,256]{2,1,0:T(8,128)(2,1)S(1)} %get-tuple-element.27), channel_id=1, source_target_pairs={{0,3},{1,2},{2,1},{3,0},{4,7},{5,6},{6,5},{7,4},{8,11},{9,10},{10,... | collective-permute-start | bytes 393224 | tf_op jit(solution)/shard_map/ppermute | solution.py:199
  50.7 8.8 %collective-permute-start.6 = (bf16[16,16,256]{2,1,0:T(8,128)(2,1)S(1)}, bf16[16,16,256]{2,1,0:T(8,128)(2,1)S(1)}, u32[]{:S(2)}, u32[]{:S(2)}) collective-permute-start(bf16[16,16,256]{2,1,0:T(8,128)(2,1)S(1)} %get-tuple-element.28), channel_id=1, source_target_pairs={{0,5},{1,4},{2,7},{3,6},{4,1},{5,0},{6,3},{7,2},{8,13},{9,12},{10,... | collective-permute-start | bytes 393224 | tf_op jit(solution)/shard_map/ppermute | solution.py:199
  60.3 15.5 %copy-start = (bf16[128,128]{1,0:T(8,128)(2,1)S(1)}, bf16[128,128]{1,0:T(8,128)(2,1)}, u32[]{:S(2)}) copy-start(bf16[128,128]{1,0:T(8,128)(2,1)} %proj_ref.5) | copy-start | bytes 98308
  60.3 7.8 %collective-permute-start.7 = (bf16[16,16,256]{2,1,0:T(8,128)(2,1)S(1)}, bf16[16,16,256]{2,1,0:T(8,128)(2,1)S(1)}, u32[]{:S(2)}, u32[]{:S(2)}) collective-permute-start(bf16[16,16,256]{2,1,0:T(8,128)(2,1)S(1)} %get-tuple-element.30), channel_id=1, source_target_pairs={{0,6},{1,7},{2,4},{3,5},{4,2},{5,3},{6,0},{7,1},{8,14},{9,15},{10,... | collective-permute-start | bytes 393224 | tf_op jit(solution)/shard_map/ppermute | solution.py:199
  64.1 6.9 %collective-permute-start.8 = (bf16[16,16,256]{2,1,0:T(8,128)(2,1)S(1)}, bf16[16,16,256]{2,1,0:T(8,128)(2,1)S(1)}, u32[]{:S(2)}, u32[]{:S(2)}) collective-permute-start(bf16[16,16,256]{2,1,0:T(8,128)(2,1)S(1)} %get-tuple-element.31), channel_id=1, source_target_pairs={{0,2},{1,3},{2,0},{3,1},{4,6},{5,7},{6,4},{7,5},{8,10},{9,11},{10,... | collective-permute-start | bytes 393224 | tf_op jit(solution)/shard_map/ppermute | solution.py:199
  64.1 10.6 %collective-permute-start.9 = (bf16[16,16,256]{2,1,0:T(8,128)(2,1)S(1)}, bf16[16,16,256]{2,1,0:T(8,128)(2,1)S(1)}, u32[]{:S(2)}, u32[]{:S(2)}) collective-permute-start(bf16[16,16,256]{2,1,0:T(8,128)(2,1)S(1)} %get-tuple-element.32), channel_id=1, source_target_pairs={{0,4},{1,5},{2,6},{3,7},{4,0},{5,1},{6,2},{7,3},{8,12},{9,13},{10,... | collective-permute-start | bytes 393224 | tf_op jit(solution)/shard_map/ppermute | solution.py:199
  64.7 9.9 %collective-permute-start.10 = (bf16[16,16,256]{2,1,0:T(8,128)(2,1)S(1)}, bf16[16,16,256]{2,1,0:T(8,128)(2,1)S(1)}, u32[]{:S(2)}, u32[]{:S(2)}) collective-permute-start(bf16[16,16,256]{2,1,0:T(8,128)(2,1)S(1)} %get-tuple-element.33), channel_id=1, source_target_pairs={{0,3},{1,2},{2,1},{3,0},{4,7},{5,6},{6,5},{7,4},{8,11},{9,10},{10,... | collective-permute-start | bytes 393224 | tf_op jit(solution)/shard_map/ppermute | solution.py:199
  65.5 9.2 %collective-permute-start.11 = (bf16[16,16,256]{2,1,0:T(8,128)(2,1)S(1)}, bf16[16,16,256]{2,1,0:T(8,128)(2,1)S(1)}, u32[]{:S(2)}, u32[]{:S(2)}) collective-permute-start(bf16[16,16,256]{2,1,0:T(8,128)(2,1)S(1)} %get-tuple-element.34), channel_id=1, source_target_pairs={{0,5},{1,4},{2,7},{3,6},{4,1},{5,0},{6,3},{7,2},{8,13},{9,12},{10,... | collective-permute-start | bytes 393224 | tf_op jit(solution)/shard_map/ppermute | solution.py:199
  68.2 7.6 %collective-permute-start.12 = (bf16[16,16,256]{2,1,0:T(8,128)(2,1)S(1)}, bf16[16,16,256]{2,1,0:T(8,128)(2,1)S(1)}, u32[]{:S(2)}, u32[]{:S(2)}) collective-permute-start(bf16[16,16,256]{2,1,0:T(8,128)(2,1)S(1)} %get-tuple-element.35), channel_id=1, source_target_pairs={{0,7},{1,6},{2,5},{3,4},{4,3},{5,2},{6,1},{7,0},{8,15},{9,14},{10,... | collective-permute-start | bytes 393224 | tf_op jit(solution)/shard_map/ppermute | solution.py:199
  70.9 4.8 %collective-permute-start.13 = (bf16[16,16,256]{2,1,0:T(8,128)(2,1)S(1)}, bf16[16,16,256]{2,1,0:T(8,128)(2,1)S(1)}, u32[]{:S(2)}, u32[]{:S(2)}) collective-permute-start(bf16[16,16,256]{2,1,0:T(8,128)(2,1)S(1)} %get-tuple-element.36), channel_id=1, source_target_pairs={{0,1},{1,0},{2,3},{3,2},{4,5},{5,4},{6,7},{7,6},{8,9},{9,8},{10,11... | collective-permute-start | bytes 393224 | tf_op jit(solution)/shard_map/ppermute | solution.py:199
